TPU v7x, 512 devices: a whole 4x8x8 slice. The times are simulated.
512 devices in a mesh: dp: 16 (over x, z_lo), ctx: 32 (over y, z_hi, core).
Axes of the slice: x: 4, y: 8, z: 8 (z_hi: 2, z_lo: 4; z = z_hi * 4 + z_lo), core: 2. Of those that a mesh axis runs over, the one named last changes fastest.
Arguments:
- series: bfloat16 [16, 4096, 1536], P('dp', 'ctx'), may hold values from -6 to 6
- cotangent: bfloat16 [16, 4096, 1536], P('dp', 'ctx'), may hold values from -6 to 6
- step_times: float32 [16, 4096], P('dp', 'ctx'), may hold values from 0 to 4096
- seg_starts: int32 [16, 4], P('dp'), may hold values from 0 to 4095, as said below
- star_of_row: int32 [16], P('dp'), may hold values from 0 to 15
- block_weight: bfloat16 [1536, 128], replicated, may hold values from -0.5 to 0.5
- star_table: float32 [16, 1536], replicated, may hold values from -6 to 6
- log_rate: float32 [1536], replicated, may hold values from -12 to -3
Outputs:
- grad_series: bfloat16 [16, 4096, 1536], P('dp', 'ctx')
- grad_weight: float32 [1536, 128], P('dp')
- grad_star: float32 [16, 1536], P(None, 'dp')
- grad_log_rate: float32 [1536], P('dp')
Inputs may be any that keep to these rules, and one draw needn't show every extreme that they name: `seg_starts`: in each row the offsets strictly rise and the first one is 0.
All inputs are finite; a program needn't handle non-finite values.
Results may differ from a plain program's by a relative error of at most 0.0039.
Values sent between devices are 32-bit elements; how exact they have to be, the bound alone decides.
No kernel may reach another device: no remote copies, remote signals or barrier semaphores. Data moves between devices by JAX's collectives and lax.ppermute only.
A program may use at most 64 MiB of HBM per device.

v0:
```python
import jax
import jax.numpy as jnp
from jax import lax
from jax.sharding import PartitionSpec as P


def entering(part, axis, combine, identity, reverse):
    count = lax.axis_size(axis)
    place = lax.axis_index(axis)
    ahead = count - 1 - place if reverse else place
    gathered = jax.tree.map(lambda a: lax.all_gather(a, axis), part)
    state = jax.tree.map(lambda a, e: jnp.zeros_like(a) + jnp.asarray(e, a.dtype), part, identity)

    def one(turn, state):
        source = count - 1 - turn if reverse else turn
        return combine(
            state, jax.tree.map(lambda a: lax.dynamic_index_in_dim(a, source, 0, False), gathered)
        )

    return lax.fori_loop(0, ahead, one, state)


def affine(earlier, later):
    return (earlier[0] * later[0], later[1] + later[0] * earlier[1])


def body(
    series, cotangent, step_times, seg_starts, star_of_row, block_weight, star_table, log_rate
):
    row_count, slab_len, width = series.shape
    block_size = block_weight.shape[1]
    head_count = width // block_size
    star_count = star_table.shape[0]
    total_tokens = row_count * lax.axis_size("dp") * slab_len * lax.axis_size("ctx")
    highest = lax.Precision.HIGHEST
    star_pick = (star_of_row[:, None] == jnp.arange(star_count)[None, :]).astype(jnp.float32)
    star_bias = jnp.dot(star_pick, star_table, precision=highest)
    series_blocks = series.reshape(row_count * slab_len, head_count, block_size)
    weight_blocks = block_weight.reshape(head_count, block_size, block_size)
    projected = jnp.einsum(
        "nhi,hij->nhj", series_blocks, weight_blocks, preferred_element_type=jnp.float32
    )
    projected = projected.reshape(row_count, slab_len, width) + star_bias[:, None, :]
    decay_rate = jnp.exp(log_rate)
    input_gain = jnp.sqrt(-jnp.expm1(-2.0 * decay_rate))
    drive_in = input_gain * projected
    positions = lax.axis_index("ctx") * slab_len + jnp.arange(slab_len)
    resets = jnp.any(seg_starts[:, :, None] == positions[None, None, :], axis=1)
    kept_mask = 1.0 - resets.astype(jnp.float32)
    decays = jnp.exp(-decay_rate * step_times[:, :, None]) * kept_mask[:, :, None]
    grad_out = cotangent.astype(jnp.float32)
    sources = jnp.stack([drive_in, grad_out])
    through_fwd, local_fwd = lax.associative_scan(affine, (decays[None], sources), axis=2)
    shifted = jnp.concatenate([decays[:, 1:], jnp.ones((row_count, 1, width), jnp.float32)], axis=1)
    flipped_cum, flipped_loc = lax.associative_scan(
        affine, (jnp.flip(shifted[None], 2), jnp.flip(sources, 2)), axis=2
    )
    through_rev = jnp.flip(flipped_cum, 2)
    local_rev = jnp.flip(flipped_loc, 2)
    slab_product = through_fwd[0, :, -1]
    fwd_end = local_fwd[:, :, -1]
    rev_head = decays[None, :, 0] * local_rev[:, :, 0]
    identity = (
        jnp.ones((row_count, width), jnp.float32),
        jnp.zeros((2, row_count, width), jnp.float32),
    )
    _, carry_early = entering((slab_product, fwd_end), "ctx", affine, identity, False)
    _, carry_late = entering((slab_product, rev_head), "ctx", affine, identity, True)
    states_fwd = local_fwd + through_fwd * carry_early[:, :, None, :]
    states_rev = local_rev + through_rev * carry_late[:, :, None, :]
    adj_bwd = states_fwd[1]
    bwd_state = states_rev[0]
    adj_fwd = states_rev[1]
    earlier = jnp.concatenate([carry_early[:, :, None, :], states_fwd[:, :, :-1]], axis=2)
    grad_drive = adj_fwd + adj_bwd
    grad_proj = input_gain * grad_drive
    rate_term = -jnp.sum(
        step_times[:, :, None] * decays * (adj_fwd * earlier[0] + earlier[1] * bwd_state),
        axis=(0, 1),
    )
    rate_term = rate_term + jnp.exp(-2.0 * decay_rate) / input_gain * jnp.sum(
        grad_drive * projected, axis=(0, 1)
    )
    log_term = decay_rate * rate_term
    grad_low = grad_proj.astype(jnp.bfloat16)
    low_blocks = grad_low.reshape(row_count * slab_len, head_count, block_size)
    weight_term = jnp.einsum(
        "nhi,nhj->hij", series_blocks, low_blocks, preferred_element_type=jnp.float32
    )
    weight_term = weight_term.reshape(width, block_size)
    star_term = jnp.dot(star_pick.T, jnp.sum(grad_proj, axis=1), precision=highest)
    back = jnp.einsum("nhj,hij->nhi", low_blocks, weight_blocks, preferred_element_type=jnp.float32)
    grad_series = (grad_out + back.reshape(row_count, slab_len, width)).astype(jnp.bfloat16)
    summed = lax.psum((weight_term, log_term, star_term), "ctx")
    grad_weight, grad_log_rate, grad_star = (
        lax.psum_scatter(summed[0], "dp", scatter_dimension=0, tiled=True),
        lax.psum_scatter(summed[1], "dp", scatter_dimension=0, tiled=True),
        lax.psum_scatter(summed[2], "dp", scatter_dimension=1, tiled=True),
    )
    norm_factor = 1.0 / jnp.sqrt(jnp.float32(total_tokens))
    return (
        grad_series,
        grad_weight * norm_factor,
        grad_star * norm_factor,
        grad_log_rate * norm_factor,
    )


def solution(mesh):
    in_specs = (
        P("dp", "ctx", None),
        P("dp", "ctx", None),
        P("dp", "ctx"),
        P("dp", None),
        P("dp"),
        P(),
        P(),
        P(),
    )
    out_specs = (P("dp", "ctx", None), P("dp", None), P(None, "dp"), P("dp"))
    return jax.shard_map(body, mesh=mesh, in_specs=in_specs, out_specs=out_specs, check_vma=False)
```

profile of v0, /device:TPU:32, one launch (start us, length us, event | category | flops | bytes accessed | tf_op | source)
XLA Modules:
  0.0 933.9 jit_solution(2024660226828096306)
XLA Ops:
  21.7 1.4 pad_maximum_fusion
  33.3 1.9 pad.189
  35.3 1.9 pad.190
  37.2 1.4 add_multiply_fusion.20
  38.6 1.4 add.439
  41.3 3.2 pad.191
  44.5 3.2 pad.192
  47.7 1.5 add_multiply_fusion.16
  49.2 1.5 add.440
  52.1 4.7 pad.193
  56.8 4.7 pad.194
  61.4 1.8 add_multiply_fusion.12
  63.2 1.7 add.441
  64.9 1.4 pad_maximum_fusion.13
  66.3 8.5 pad.195
  74.8 8.5 pad.196
  83.3 2.1 add_multiply_fusion.8
  85.4 1.9 add.442
  87.3 1.5 pad_maximum_fusion.9
  88.8 15.2 %pad.197 = f32[1,1,64,1536]{3,0,2,1:T(1,128)} pad(f32[1,1,32,1536]{3,0,2,1:T(1,128)} %pad_maximum_fusion.9, f32[]{:T(128)} %constant.68.clone.1), padding=0_0_0x0_0_0x0_1_1x0_0_0 | pad | bytes 589828 | tf_op jit(solution)/shard_map/pad | solution.py:55
  104.0 15.2 %pad.198 = f32[1,1,64,1536]{3,0,2,1:T(1,128)} pad(f32[1,1,32,1536]{3,0,2,1:T(1,128)} %add.442, f32[]{:T(128)} %constant.68.clone.1), padding=0_0_0x0_0_0x1_0_1x0_0_0 | pad | bytes 589828 | tf_op jit(solution)/shard_map/pad | solution.py:55
  119.3 2.8 add_multiply_fusion.4
  123.7 58.9 %all-gather = f32[32,1,1,1536]{3,2,1,0:T(1,128)} all-gather(f32[1,1,1,1536]{3,2,1,0:T(1,128)} %slice_add_fusion.4), channel_id=2, replica_groups=mesh['dp'=16,'ctx'=32] {'ctx'}, dimensions={0}, use_global_device_ids=true | all-gather | bytes 202752 | tf_op jit(solution)/shard_map/all_gather | solution.py:11
  182.6 1.7 copy.254
  185.1 1.6 copy.304
  186.7 1.5 copy.306
  188.3 1.4 copy.308
  195.8 22.8 %pad.200 = f32[1,1,128,1536]{3,0,2,1:T(1,128)S(1)} pad(f32[1,1,64,1536]{3,0,2,1:T(1,128)} %add.443, f32[]{:T(128)} %constant.68.clone.1), padding=0_0_0x0_0_0x1_0_1x0_0_0 | pad | bytes 1179652 | tf_op jit(solution)/shard_map/pad | solution.py:55
  218.6 1.8 add.444
  229.5 2.0 pad.175
  231.5 2.0 pad.176
  233.5 1.5 add.427
  236.4 3.3 pad.177
  239.7 3.3 pad.178
  243.0 1.6 add.429
  245.7 1.4 pad_maximum_fusion.12
  247.1 4.8 pad.179
  251.9 4.8 pad.180
  256.7 1.8 add.431
  260.6 8.7 pad.181
  269.3 8.7 pad.182
  278.0 2.1 add.433
  280.1 2.3 fusion.11
  287.9 1.5 pad.220
  291.9 3.0 pad.222
  297.2 5.9 pad.224
  306.1 11.7 %pad.226 = f32[2,1,64,1536]{3,0,2,1:T(2,128)S(1)} pad(f32[2,1,32,1536]{3,0,2,1:T(2,128)} %add.468, f32[]{:T(128)} %constant.68.clone.1), padding=0_0_0x0_0_0x1_0_1x0_0_0 | pad | bytes 1179652 | tf_op jit(solution)/shard_map/pad | solution.py:53
  319.1 2.1 fusion.38
  323.1 1.4 add.435
  325.6 1.7 pad_maximum_fusion.2
  328.5 23.3 %pad.186 = f32[2,1,128,1536]{3,0,2,1:T(2,128)S(1)} pad(f32[2,1,64,1536]{3,0,2,1:T(2,128)} %add.435, f32[]{:T(128)} %constant.68.clone.1), padding=0_0_0x0_0_0x1_0_1x0_0_0 | pad | bytes 2359300 | tf_op jit(solution)/shard_map/pad | solution.py:55
  351.9 2.0 add.437
  353.9 48.1 %all_gather.11 = f32[32,2,1,1536]{3,1,2,0:T(2,128)S(1)} all-gather(f32[1,2,1,1536]{3,1,2,0:T(2,128)S(1)} %fusion.28), channel_id=1, replica_groups=mesh['dp'=16,'ctx'=32] {'ctx'}, dimensions={0}, use_global_device_ids=true | all-gather | bytes 405504 | tf_op jit(solution)/shard_map/all_gather | solution.py:11
  402.0 11.8 %while.26 = (s32[]{:T(128)}, f32[2,1,1536]{2,1,0:T(1,128)S(1)}, s32[]{:T(128)}, f32[32,2,1,1536]{3,1,2,0:T(2,128)S(1)}, f32[32,1,1536]{2,1,0:T(1,128)}, /*index=5*/s32[]{:T(128)}, s32[]{:T(128)}, s32[]{:T(128)}, s32[]{:T(128)}) while((s32[]{:T(128)}, f32[2,1,1536]{2,1,0:T(1,128)S(1)}, s32[]{:T(128)}, f32[32,2,1,1536]{3,1,2,0:T(2,128)S(1)}, ...), condition=%wide.region_2.3_spmd, body=%wide.region_1.2_spmd.sunk | while | flops 6150 | bytes 80027 | solution.py:20
  414.4 23.3 %pad.228 = f32[2,1,128,1536]{3,0,2,1:T(2,128)S(1)} pad(f32[2,1,64,1536]{3,0,2,1:T(2,128)} %add.470, f32[]{:T(128)} %constant.68.clone.1), padding=0_0_0x0_0_0x1_0_1x0_0_0 | pad | bytes 2359300 | tf_op jit(solution)/shard_map/pad | solution.py:53
  437.8 23.3 %pad.227 = f32[2,1,128,1536]{3,0,2,1:T(2,128)S(1)} pad(f32[2,1,64,1536]{3,0,2,1:T(2,128)} %get-tuple-element.290, f32[]{:T(128)} %constant.68.clone.1), padding=0_0_0x0_0_0x0_1_1x0_0_0 | pad | bytes 2359300 | tf_op jit(solution)/shard_map/pad | solution.py:53
  461.1 62.8 %all-gather.1 = f32[64,1,1,1536]{3,2,1,0:T(1,128)} all-gather(f32[2,1,1,1536]{3,2,1,0:T(1,128)S(1)} %copy.249), channel_id=3, replica_groups=mesh['dp'=16,'ctx'=32] {'ctx'}, dimensions={0}, use_global_device_ids=true | all-gather | bytes 405504 | tf_op jit(solution)/shard_map/all_gather | solution.py:11
  524.0 23.6 %while.27 = (s32[]{:T(128)}, f32[2,1,1536]{2,1,0:T(1,128)S(1)}, s32[]{:T(128)}, f32[32,2,1,1536]{3,2,1,0:T(1,128)}, f32[32,1,1536]{2,1,0:T(1,128)}, /*index=5*/s32[]{:T(128)}, s32[]{:T(128)}, s32[]{:T(128)}) while((s32[]{:T(128)}, f32[2,1,1536]{2,1,0:T(1,128)S(1)}, s32[]{:T(128)}, f32[32,2,1,1536]{3,2,1,0:T(1,128)}, f32[32,1,1536]{2,1,0:T(1,128)}, ...), condition=%wide.region_4.5_spmd, body=%wide.region_3.4_spmd.sunk | while | flops 6149 | bytes 55431 | solution.py:20
  547.6 2.2 multiply_add_fusion
  552.6 6.0 fusion.6
  566.6 43.1 %all-reduce.57 = f32[1536]{0:T(1024)S(1)} all-reduce(f32[1536]{0:T(1024)S(1)} %get-tuple-element.285), channel_id=6, replica_groups=mesh['dp'=16,'ctx'=32] {'dp'}, use_global_device_ids=true, to_apply=%region_13.14.clone | all-reduce | flops 1536 | bytes 12288
  609.9 59.8 %reduce-scatter.7.cloned.1.call-done = f32[96,16]{1,0:T(8,128)} async-done(((f32[1536,16]{1,0:T(8,128)}), f32[96,16]{1,0:T(8,128)}) %reduce-scatter.7.cloned.1.call-update) | async-done | bytes 6160
  670.5 87.3 %reduce-scatter.5.cloned.1.call-done = f32[96,128]{1,0:T(8,128)} async-done(((f32[1536,128]{1,0:T(8,128)}), f32[96,128]{1,0:T(8,128)}) %reduce-scatter.5.cloned.1.call-update) | async-done | bytes 49168 | tf_op jit(solution)/shard_map/reduce_scatter | solution.py:96
  757.9 167.5 %all-reduce.58 = (f32[96,128]{1,0:T(8,128)S(1)}, f32[16,96]{1,0:T(8,128)S(1)}, f32[96]{0:T(128)S(1)}) all-reduce(f32[96,128]{1,0:T(8,128)} %reduce-scatter.5.cloned.1.call-done, f32[16,96]{1,0:T(8,128)S(1)} %copy.261, f32[96]{0:T(128)S(1)} %dynamic-slice.1), channel_id=1, replica_groups=mesh['dp'=16,'ctx'=32] {'ctx'}, use_global_device_ids=true, to_apply=%region_5.6 | all-reduce | flops 13920 | bytes 111360 | tf_op jit(solution)/shard_map/psum | solution.py:94
  (433 shorter events, 114.8 us)
Async XLA Ops:
  7.2 12.2 %copy-start = (bf16[1536,128]{1,0:T(8,128)(2,1)S(1)}, bf16[1536,128]{1,0:T(8,128)(2,1)}, u32[]{:S(2)}) copy-start(bf16[1536,128]{1,0:T(8,128)(2,1)} %param.17) | copy-start | bytes 1179652
  7.2 662.5 %reduce-scatter.7.cloned.1.call-start = ((), (), s32[]{:S(2)}) async-start(), calls=%async_computation.3 | async-start | bytes 835584
  8.0 7.9 copy-start.76
  8.8 7.1 copy-start.52
  8.8 11.7 %copy-start.58 = (f32[1536]{0:T(1024)}, f32[1536]{0:T(1024)S(1)}, u32[]{:S(2)}) copy-start(f32[1536]{0:T(1024)S(1)} %get-tuple-element.288) | copy-start | bytes 18436
  10.0 3.9 copy-start.4
  11.0 2.7 copy-start.19
  11.2 2.2 copy-start.20
  11.4 2.1 copy-start.33
  11.5 1.9 copy-start.34
  11.6 2.0 copy-start.40
  11.6 1.7 copy-start.41
  11.7 1.7 copy-start.47
  11.7 1.7 copy-start.48
  11.8 1.3 copy-start.54
  14.2 1.7 copy-start.74
  15.9 2.6 copy-start.43
  15.9 2.8 copy-start.26
  18.7 1.6 copy-start.8
  21.7 1.4 slice-start.2
  23.8 95.5 %copy-start.2 = (f32[1,1,128,1536]{3,0,2,1:T(1,128)}, f32[1,1,128,1536]{3,0,2,1:T(1,128)S(1)}, u32[]{:S(2)}) copy-start(f32[1,1,128,1536]{3,0,2,1:T(1,128)S(1)} %reverse_bitcast_fusion) | copy-start | bytes 2359300
  119.2 2.8 copy-start.10
  119.3 2.8 copy-start.11
  122.0 62.3 %copy-start.22 = (f32[1,1,64,1536]{3,0,2,1:T(1,128)S(1)}, f32[1,1,64,1536]{3,0,2,1:T(1,128)}, u32[]{:S(2)}) copy-start(f32[1,1,64,1536]{3,0,2,1:T(1,128)} %get-tuple-element.244) | copy-start | bytes 1179652
  182.6 11.7 %slice-start = ((f32[1,1,128,1536]{3,0,2,1:T(1,128)}), f32[1,1,1,1536]{3,0,2,1:T(1,128)S(1)}, s32[]{:S(2)}) async-start(f32[1,1,128,1536]{3,0,2,1:T(1,128)} %copy-done.2), calls=%async_computation.4 | async-start | bytes 12288 | tf_op jit(solution)/shard_map/slice | solution.py:55
  182.6 11.7 %copy-start.29 = (f32[1,1,63,1536]{3,0,2,1:T(1,128)S(1)}, f32[1,1,63,1536]{3,0,2,1:T(1,128)}, u32[]{:S(2)}) copy-start(f32[1,1,63,1536]{3,0,2,1:T(1,128)} %get-tuple-element.241) | copy-start | bytes 1161220
  184.3 7.3 copy-start.62
  184.3 7.9 copy-start.51
  184.3 8.6 copy-start.45
  184.3 9.2 copy-start.37
  220.4 2.2 copy-start.28
  220.4 3.0 copy-start.7
  224.2 1.4 copy-start.36
  224.4 2.3 copy-start.44
  224.9 55.2 %copy-start.3 = (f32[2,1,64,1536]{3,0,2,1:T(2,128)}, f32[2,1,64,1536]{3,0,2,1:T(2,128)S(1)}, u32[]{:S(2)}) copy-start(f32[2,1,64,1536]{3,0,2,1:T(2,128)S(1)} %multiply_add_fusion.3) | copy-start | bytes 2359300
  224.9 2.5 copy-start.50
  224.9 3.2 copy-start.57
  224.9 3.3 copy-start.66
  225.0 3.3 copy-start.73
  225.0 3.9 copy-start.72
  236.4 23.4 %slice-start.3 = ((f32[2,1,32,1536]{3,0,2,1:T(2,128)}), f32[2,1,1,1536]{3,0,2,1:T(2,128)S(1)}, s32[]{:S(2)}) async-start(f32[2,1,32,1536]{3,0,2,1:T(2,128)} %copy-done.18), calls=%async_computation.7 | async-start | bytes 24576 | tf_op jit(solution)/shard_map/slice | solution.py:55
  278.0 4.4 copy-start.21
  280.1 2.6 copy-start.35
  280.1 3.4 copy-start.42
  282.3 1.8 copy-start.49
  282.3 1.8 copy-start.55
  282.3 1.8 copy-start.71
  282.3 2.5 copy-start.70
  303.0 2.2 copy-start.67
  317.8 1.3 copy-start.5
  319.1 2.1 slice-start.1
  319.1 2.1 copy-start.30
  322.2 2.2 copy-start.16
  322.2 2.2 copy-start.24
  351.9 2.0 copy-start.69
  549.8 1.4 copy-start.1
  549.9 1.6 copy-start.14
  549.9 1.6 copy-start.65
  551.5 1.1 copy-start.53
  551.5 1.1 copy-start.59
  552.6 6.0 copy-start.78
  558.7 1.9 copy-start.68
  558.7 1.9 copy-start.9
  560.0 197.9 %reduce-scatter.5.cloned.1.call-start = ((), (), s32[]{:S(2)}) async-start(), calls=%async_computation.2 | async-start | bytes 835584 | tf_op jit(solution)/shard_map/reduce_scatter | solution.py:96
  (21 other events, 19.2 us)
Sparse Core Ops, SparseCore 0:
  560.1 109.5 reduce-scatter.6
  672.7 85.0 reduce-scatter.4
where the time goes:
time: 952 us; the launch traced here: 934 us
  blocking collectives  380 us (40%)
  local copies, waits for them, and re-layouts  282 us (30%)
  waiting for transfers between devices  147 us (15%)
  other arithmetic  104 us (11%)
  between operations  16.9 us (2%)
    all_gather x3, blocking collectives, entering(): gathered = jax.tree.map(lambda a: lax.all_gather(a, axis), part)  170 us
    psum x1, blocking collectives, body(): summed = lax.psum((weight_term, log_term, star_term), 'ctx')  168 us
    pad x24, local copies, waits for them, and re-layouts, body(): lax.associative_scan(affine, (jnp.flip(shifted[None], 2), jnp.flip(source...  155 us
    reduce_scatter x1, waiting for transfers between devices, body(): lax.psum_scatter(summed[0], 'dp', scatter_dimension=0, tiled=True)  87.3 us
    pad x24, local copies, waits for them, and re-layouts, body(): lax.associative_scan(affine, (decays[None], sources), axis=2)  71.2 us
    unnamed x3, waiting for transfers between devices  59.8 us
    unnamed x1, blocking collectives  43.1 us
    add x53, other arithmetic, affine(): return (earlier[0] * later[0], later[1] + later[0] * earlier[1])  24.1 us
  transfers between devices with their start and end apart: 2, of which 2 were waited for; matrix products, arithmetic and copies ran while one was open for 1% of the time, Pallas kernels for 0%

commit v1 on v0

v1 whole, which is shorter than its diff:
```python
import functools
import jax
import jax.numpy as jnp
from jax import lax
from jax.experimental import pallas as pl
from jax.experimental.pallas import tpu as pltpu
from jax.sharding import Mesh, PartitionSpec as P

SLAB = 128
LANES = 128
CHUNKS = 8
STEPS = SLAB // CHUNKS
FAR = 1e9
F32 = jnp.float32
BF16 = jnp.bfloat16


def slab_index():
    return (lax.axis_index("y") * 2 + lax.axis_index("zh")) * 2 + lax.axis_index("core")


def elapsed_row(starts_ref, times_ref, me):
    position = lax.broadcasted_iota(jnp.int32, (1, SLAB), 1) + me * SLAB
    reset = position == starts_ref[0, 0]
    for k in range(1, starts_ref.shape[1]):
        reset = jnp.logical_or(reset, position == starts_ref[0, k])
    return jnp.where(reset, FAR, times_ref[...])


def ends_kernel(
    blocks, slabs, starts_ref, star_ref, times_ref, series_ref, cot_ref, w_ref, table_ref, lograte_ref,
    out_ref, ends_ref,
):
    me = slab_index()
    elapsed = elapsed_row(starts_ref, times_ref, me)
    row = lax.broadcasted_iota(jnp.int32, (SLAB, SLAB), 0)
    lane = lax.broadcasted_iota(jnp.int32, (SLAB, SLAB), 1)
    spread = jnp.broadcast_to(elapsed, (SLAB, SLAB))
    to_end = jnp.sum(jnp.where(lane > row, spread, 0.0), axis=1, keepdims=True)
    from_start = jnp.sum(jnp.where(lane <= row, spread, 0.0), axis=1, keepdims=True)
    to_end = jnp.broadcast_to(to_end, (SLAB, LANES))
    from_start = jnp.broadcast_to(from_start, (SLAB, LANES))
    total = jnp.sum(elapsed, axis=1, keepdims=True)
    bias = table_ref[pl.ds(star_ref[0], 1), :]
    for h in range(blocks):
        cols = slice(h * LANES, (h + 1) * LANES)
        proj = jnp.dot(series_ref[0, :, cols], w_ref[cols, :], preferred_element_type=F32) + bias[:, cols]
        grad = cot_ref[0, :, cols].astype(F32)
        slope = -jnp.exp(lograte_ref[h : h + 1, :])
        late = jnp.exp(slope * to_end)
        early = jnp.exp(slope * from_start)
        ends_ref[0, h : h + 1, :] = jnp.sum(late * proj, axis=0, keepdims=True)
        ends_ref[0, blocks + h : blocks + h + 1, :] = jnp.sum(late * grad, axis=0, keepdims=True)
        ends_ref[1, h : h + 1, :] = jnp.sum(early * proj, axis=0, keepdims=True)
        ends_ref[1, blocks + h : blocks + h + 1, :] = jnp.sum(early * grad, axis=0, keepdims=True)
    tail = jnp.broadcast_to(total, (8, LANES))
    ends_ref[0, 2 * blocks : 2 * blocks + 8, :] = tail
    ends_ref[1, 2 * blocks : 2 * blocks + 8, :] = tail
    for d in range(slabs):
        out_ref[d] = ends_ref[jnp.where(d > me, 0, 1)]


def shift(x, k, fill, sublane):
    if k > 0:
        return jnp.where(sublane < k, fill, pltpu.roll(x, k, 0))
    return jnp.where(sublane >= CHUNKS + k, fill, pltpu.roll(x, CHUNKS + k, 0))


def chunk_entries(ends, through, carry, sublane, sign):
    for k in (1, 2, 4):
        ends = ends + through * shift(ends, sign * k, 0.0, sublane)
        through = through * shift(through, sign * k, 1.0, sublane)
    return shift(ends + through * carry, sign, jnp.broadcast_to(carry, ends.shape), sublane)


def main_kernel(
    blocks, slabs, rows_dp, starts_ref, star_ref, times_ref, series_ref, cot_ref, w_ref, table_ref, lograte_ref,
    gain_ref, got_ref, dx_ref, keep_ref, send_ref, carry_ref, sums_ref, part_ref,
):
    me = slab_index()
    width = blocks * LANES
    elapsed = elapsed_row(starts_ref, times_ref, me)
    row = lax.broadcasted_iota(jnp.int32, (SLAB, SLAB), 0)
    lane = lax.broadcasted_iota(jnp.int32, (SLAB, SLAB), 1)
    time_of_row = (row % CHUNKS) * STEPS + row // CHUNKS
    order = (lane == time_of_row).astype(F32).astype(BF16)
    time_of_lane = (lane % CHUNKS) * STEPS + lane // CHUNKS
    unorder = (row == time_of_lane).astype(F32).astype(BF16)
    gap = jnp.sum(jnp.where(lane == time_of_row, jnp.broadcast_to(elapsed, (SLAB, SLAB)), 0.0), axis=1, keepdims=True)
    gap = jnp.broadcast_to(gap, (SLAB, LANES))
    bias = table_ref[pl.ds(star_ref[0], 1), :]
    sublane = lax.broadcasted_iota(jnp.int32, (CHUNKS, LANES), 0)

    slope = -jnp.exp(lograte_ref[...])
    slope2 = jnp.concatenate([slope, slope], axis=0)
    between = [None] * slabs
    run = jnp.zeros((1, LANES), F32)
    for s in reversed(range(slabs)):
        between[s] = run
        run = jnp.where(s < me, run + got_ref[s, 2 * blocks : 2 * blocks + 1, :], 0.0)
    run = jnp.zeros((1, LANES), F32)
    carry_early = jnp.zeros((2 * blocks, LANES), F32)
    carry_late = jnp.zeros((2 * blocks, LANES), F32)
    for s in range(slabs):
        x = jnp.exp(slope2 * jnp.where(s < me, between[s], run)) * got_ref[s, 0 : 2 * blocks, :]
        carry_early = carry_early + jnp.where(s < me, x, 0.0)
        carry_late = carry_late + jnp.where(s > me, x, 0.0)
        run = jnp.where(s > me, run + got_ref[s, 2 * blocks : 2 * blocks + 1, :], 0.0)
    gains = jnp.concatenate([gain_ref[...], jnp.ones((blocks, LANES), F32)], axis=0)
    carry_ref[0] = carry_early * gains
    carry_ref[1] = carry_late * gains

    for h in range(blocks):
        cols = slice(h * LANES, (h + 1) * LANES)
        rate = jnp.exp(lograte_ref[h : h + 1, :])
        gain = gain_ref[h : h + 1, :]
        weight = w_ref[cols, :]
        xs = jnp.dot(order, series_ref[0, :, cols], preferred_element_type=F32).astype(BF16)
        grad = jnp.dot(order, cot_ref[0, :, cols], preferred_element_type=F32)
        proj = jnp.dot(xs, weight, preferred_element_type=F32) + bias[:, cols]
        drive = gain * proj
        decay = jnp.exp(-rate * gap)
        tiles = lambda v: [v[j * CHUNKS : (j + 1) * CHUNKS, :] for j in range(STEPS)]
        a, d, g, pr, dt = tiles(decay), tiles(drive), tiles(grad), tiles(proj), tiles(gap)
        before_d, before_g, through = [None], [None], [a[0]]
        state_d, state_g = d[0], g[0]
        for j in range(1, STEPS):
            before_d.append(a[j] * state_d)
            before_g.append(a[j] * state_g)
            state_d = before_d[j] + d[j]
            state_g = before_g[j] + g[j]
            through.append(a[j] * through[j - 1])
        enter_d = chunk_entries(state_d, through[-1], carry_ref[0, h : h + 1, :], sublane, 1)
        enter_g = chunk_entries(state_g, through[-1], carry_ref[0, blocks + h : blocks + h + 1, :], sublane, 1)
        after_d, after_g, back_through = [None] * STEPS, [None] * STEPS, [None] * STEPS
        after_d[-1], after_g[-1] = d[-1], g[-1]
        for j in reversed(range(STEPS - 1)):
            after_d[j] = a[j + 1] * after_d[j + 1] + d[j]
            after_g[j] = a[j + 1] * after_g[j + 1] + g[j]
            back_through[j] = a[j + 1] if j == STEPS - 2 else a[j + 1] * back_through[j + 1]
        leave_d = chunk_entries(a[0] * after_d[0], through[-1], carry_ref[1, h : h + 1, :], sublane, -1)
        leave_g = chunk_entries(a[0] * after_g[0], through[-1], carry_ref[1, blocks + h : blocks + h + 1, :], sublane, -1)
        rate_sum = jnp.zeros((CHUNKS, LANES), F32)
        grad_sum = jnp.zeros((CHUNKS, LANES), F32)
        cross_sum = jnp.zeros((CHUNKS, LANES), F32)
        low = []
        for j in range(STEPS):
            kept_d = through[j] * enter_d if j == 0 else before_d[j] + through[j] * enter_d
            kept_g = through[j] * enter_g if j == 0 else before_g[j] + through[j] * enter_g
            later_d = after_d[j] + (leave_d if j == STEPS - 1 else back_through[j] * leave_d)
            later_g = after_g[j] + (leave_g if j == STEPS - 1 else back_through[j] * leave_g)
            total = later_g + (kept_g + g[j])
            rate_sum = rate_sum + dt[j] * (later_g * kept_d + kept_g * later_d)
            grad_sum = grad_sum + total
            cross_sum = cross_sum + total * pr[j]
            low.append(gain * total)
        low = jnp.concatenate(low, axis=0).astype(BF16)
        product = lax.dot_general(xs, low, (((0,), (0,)), ((), ())), preferred_element_type=F32)
        back = lax.dot_general(low, weight, (((1,), (1,)), ((), ())), preferred_element_type=F32)
        out = (grad + back).astype(BF16)
        dx_ref[0, :, cols] = jnp.dot(unorder, out, preferred_element_type=F32).astype(BF16)
        for k in range(LANES // 8):
            piece, third = divmod(h * (LANES // 8) + k, 3)
            dp, quarter = divmod(piece, 4)
            core, zh = divmod(quarter, 2)
            part_ref[core, dp * 2 + zh, third * 8 : third * 8 + 8, :] = product[k * 8 : k * 8 + 8, :]
        total = lambda v: jnp.sum(v, axis=0, keepdims=True)
        sums_ref[0:1, cols] = gain * total(grad_sum)
        sums_ref[1:2, cols] = rate * (jnp.exp(-2.0 * rate) / gain * total(cross_sum) - total(rate_sum))
    share = width // rows_dp
    lane8 = lax.broadcasted_iota(jnp.int32, (8, LANES), 1)
    sub8 = lax.broadcasted_iota(jnp.int32, (8, LANES), 0)
    sums_ref[2:8, :] = jnp.zeros((6, sums_ref.shape[1]), F32)
    sums_ref[0:2, width:] = jnp.zeros((2, sums_ref.shape[1] - width), F32)
    star_half = jnp.broadcast_to(0.5 * star_ref[0].astype(F32), (8, LANES))
    for dp in range(rows_dp):
        window = sums_ref[:, dp * share : dp * share + LANES]
        tile = jnp.where(sub8 == 2, star_half, jnp.where(lane8 < share, window, 0.0))
        for core in range(2):
            for zh in range(2):
                part_ref[core, dp * 2 + zh, 24:32, :] = tile
    core = lax.axis_index("core")
    keep_ref[...] = part_ref[core]
    send_ref[...] = part_ref[1 - core]


def piece_kernel(norm, got_ref, out_ref):
    first = (lax.axis_index("core") * 2 + lax.axis_index("zh")) * 4
    total = got_ref[0, 0:24, :]
    logs = got_ref[0, 25:26, :]
    stars = [jnp.zeros((1, LANES), F32)] * 4
    for s in range(got_ref.shape[0]):
        if s:
            total = total + got_ref[s, 0:24, :]
            logs = logs + got_ref[s, 25:26, :]
        for k in range(4):
            hit = got_ref[s, 26:27, :] == (first + k).astype(F32)
            stars[k] = stars[k] + jnp.where(hit, got_ref[s, 24:25, :], 0.0)
    total = total * norm
    tail = jnp.concatenate(stars + [logs] + [jnp.zeros((3, LANES), F32)], axis=0) * norm
    for d in range(out_ref.shape[0]):
        out_ref[d, 0:24, :] = total
        out_ref[d, 24:32, :] = tail


def final_kernel(got_ref, weight_ref, star_ref, log_ref):
    share = star_ref.shape[1]
    for core in range(2):
        for zh in range(2):
            q = core * 2 + zh
            total = got_ref[core, zh]
            for y in range(1, got_ref.shape[1] // 2):
                total = total + got_ref[core, y * 2 + zh]
            weight_ref[q * 24 : q * 24 + 24, :] = total[0:24, :]
            star_ref[q * 4 : q * 4 + 4, :] = total[24:28, 0:share]
            if q == 0:
                log_ref[...] = total[28:29, 0:share]


def body(series, cotangent, step_times, seg_starts, star_of_row, block_weight, star_table, log_rate):
    _, slab_len, width = series.shape
    blocks = width // LANES
    slabs = lax.axis_size(("y", "zh", "core"))
    rows_dp = lax.axis_size(("x", "zl"))
    norm = float(1.0 / (rows_dp * slabs * slab_len) ** 0.5)
    log_blocks = log_rate.reshape(blocks, LANES)
    gain = jnp.sqrt(-jnp.expm1(-2.0 * jnp.exp(log_blocks)))
    smem = pl.BlockSpec(memory_space=pltpu.SMEM)
    vmem = pl.BlockSpec(memory_space=pltpu.VMEM)
    params = pltpu.CompilerParams(vmem_limit_bytes=40 * 1024 * 1024)
    common = (seg_starts, star_of_row, step_times, series, cotangent, block_weight, star_table, log_blocks)
    ends = pl.pallas_call(
        functools.partial(ends_kernel, blocks, slabs),
        out_shape=jax.ShapeDtypeStruct((slabs, 32, LANES), F32),
        in_specs=[smem, smem] + [vmem] * 6,
        out_specs=vmem,
        scratch_shapes=[pltpu.VMEM((2, 32, LANES), F32)],
        compiler_params=params,
        name="slab_ends",
    )(*common)
    got = lax.all_to_all(ends, ("y", "zh", "core"), 0, 0)
    grad_series, keep, send = pl.pallas_call(
        functools.partial(main_kernel, blocks, slabs, rows_dp),
        out_shape=[
            jax.ShapeDtypeStruct(series.shape, BF16),
            jax.ShapeDtypeStruct((rows_dp * 2, 32, LANES), F32),
            jax.ShapeDtypeStruct((rows_dp * 2, 32, LANES), F32),
        ],
        in_specs=[smem, smem] + [vmem] * 8,
        out_specs=[vmem] * 3,
        scratch_shapes=[
            pltpu.VMEM((2, 2 * blocks, LANES), F32),
            pltpu.VMEM((8, width + LANES), F32),
            pltpu.VMEM((2, rows_dp * 2, 32, LANES), F32),
        ],
        compiler_params=params,
        name="gradients",
    )(*common, gain, got)
    pair = keep + lax.ppermute(send, "core", [(0, 1), (1, 0)])
    pieces = lax.all_to_all(pair, ("x", "zl", "zh"), 0, 0)
    piece = pl.pallas_call(
        functools.partial(piece_kernel, norm),
        out_shape=jax.ShapeDtypeStruct((slabs // 2, 32, LANES), F32),
        in_specs=[vmem],
        out_specs=vmem,
        compiler_params=params,
        name="sum_pieces",
    )(pieces)
    spread = lax.all_to_all(piece, ("y", "zh"), 0, 0)
    both = lax.all_gather(spread, "core")
    share = width // rows_dp
    grad_weight, grad_star, grad_log = pl.pallas_call(
        final_kernel,
        out_shape=[
            jax.ShapeDtypeStruct((share, LANES), F32),
            jax.ShapeDtypeStruct((star_table.shape[0], share), F32),
            jax.ShapeDtypeStruct((1, share), F32),
        ],
        in_specs=[vmem],
        out_specs=[vmem] * 3,
        compiler_params=params,
        name="outputs",
    )(both)
    return grad_series, grad_weight, grad_star, grad_log.reshape(share)


def solution(mesh):
    fine = Mesh(mesh.devices.reshape(4, 4, 8, 2, 2), ("x", "zl", "y", "zh", "core"))
    dp, ctx = ("x", "zl"), ("y", "zh", "core")
    in_specs = (P(dp, ctx, None), P(dp, ctx, None), P(dp, ctx), P(dp, None), P(dp), P(), P(), P())
    out_specs = (P(dp, ctx, None), P(dp, None), P(None, dp), P(dp))
    return jax.shard_map(body, mesh=fine, in_specs=in_specs, out_specs=out_specs, check_vma=False)
```

time: 952 us -> 105 us (0.11)
  the two profiles are of different devices: /device:TPU:32 before, /device:TPU:1 now
where the time goes in v1:
time: 105 us; the launch traced here: 104 us
  blocking collectives  48.5 us (46%)
  starting transfers between devices  20.7 us (20%)
  waiting for transfers between devices  20.5 us (20%)
  Pallas kernels  8.04 us (8%)
  local copies, waits for them, and re-layouts  5.25 us (5%)
  between operations  1.36 us (1%)
    all_to_all x1, blocking collectives, body(): pieces = lax.all_to_all(pair, ('x', 'zl', 'zh'), 0, 0)  22.8 us
    all_to_all x1, blocking collectives, body(): spread = lax.all_to_all(piece, ('y', 'zh'), 0, 0)  20.7 us
    all_to_all x1, waiting for transfers between devices, body(): got = lax.all_to_all(ends, ('y', 'zh', 'core'), 0, 0)  19 us
    all_to_all x1, starting transfers between devices, body(): got = lax.all_to_all(ends, ('y', 'zh', 'core'), 0, 0)  17.3 us
    pallas_call x1, Pallas kernels, body(): pl.pallas_call(functools.partial(main_kernel, blocks, slabs, rows_dp), ou...  5.3 us
    unnamed x24, local copies, waits for them, and re-layouts  5.25 us
    all_gather x1, blocking collectives, body(): both = lax.all_gather(spread, 'core')  5.05 us
    ppermute x1, starting transfers between devices, body(): pair = keep + lax.ppermute(send, 'core', [(0, 1), (1, 0)])  3.33 us
  transfers between devices with their start and end apart: 2, of which 2 were waited for; matrix products, arithmetic and copies ran while one was open for 0% of the time, Pallas kernels for 0%

profile of v1, /device:TPU:1, one launch (start us, length us, event | category | flops | bytes accessed | tf_op | source)
XLA Modules:
  0.0 104.4 jit_solution(12392435366010763374)
XLA Ops:
  1.3 0.0 copy-start.10
  1.3 0.0 copy-start.11
  1.3 0.6 copy-done.10
  1.9 0.0 copy-done.11
  2.0 0.0 copy-start
  2.0 1.0 copy-done
  2.9 0.0 copy-start.2
  2.9 1.0 copy-done.2
  3.9 0.0 copy-start.4
  3.9 1.0 copy-done.4
  4.9 0.0 copy-start.6
  4.9 0.9 copy-done.6
  5.8 0.0 copy-start.8
  5.8 0.7 copy-done.8
  6.5 0.0 copy-start.5
  6.5 2.0 %slab_ends.1 = f32[32,32,128]{2,1,0:T(8,128)} custom-call(s32[1,4]{1,0:T(1,128)S(1)} %copy-done.10, s32[1]{0:T(128)S(6)} %copy.12.star_ref, f32[1,128]{1,0:T(1,128)S(1)} %copy-done.11, bf16[1,128,1536]{2,1,0:T(8,128)(2,1)S(1)} %copy-done, bf16[1,128,1536]{2,1,0:T(8,128)(2,1)S(1)} %copy-done.2, bf16[1536,128]{1,0:T(8,128)(2,1)S(1)} %copy-done.4, ...), custom_call_target="tpu_custom_call" | custom-call | tf_op jit(solution)/shard_map/slab_ends/pallas_call | solution.py:232
  8.5 0.0 copy-start.9
  8.5 0.0 copy-start.1
  8.5 0.0 copy-start.3
  8.5 0.0 copy-start.7
  8.5 17.3 %all-to-all-start = ((f32[32,32,128]{2,1,0:T(8,128)}), f32[32,32,128]{2,1,0:T(8,128)S(1)}, u32[]{:S(2)}, u32[]{:S(2)}) async-start(f32[32,32,128]{2,1,0:T(8,128)} %slab_ends.1), calls=%async_computation | async-start | bytes 1048576 | tf_op jit(solution)/shard_map/all_to_all | solution.py:241
  25.9 0.0 copy-done.9
  25.9 19.0 %all-to-all-done.got_ref = f32[32,32,128]{2,1,0:T(8,128)S(1)} async-done(((f32[32,32,128]{2,1,0:T(8,128)}), f32[32,32,128]{2,1,0:T(8,128)S(1)}, u32[]{:S(2)}, u32[]{:S(2)}) %all-to-all-start) | async-done | bytes 524320 | tf_op jit(solution)/shard_map/all_to_all | solution.py:241
  44.9 0.0 copy-done.5
  44.9 0.0 copy-done.1
  44.9 0.0 copy-done.3
  44.9 0.0 copy-done.7
  44.9 5.3 %gradients.1 = (bf16[1,128,1536]{2,1,0:T(8,128)(2,1)}, f32[32,32,128]{2,1,0:T(8,128)S(1)}, f32[32,32,128]{2,1,0:T(8,128)S(1)}) custom-call(s32[1,4]{1,0:T(1,128)S(1)} %copy-done.10, s32[1]{0:T(128)S(6)} %copy.12.star_ref, f32[1,128]{1,0:T(1,128)S(1)} %copy-done.11, bf16[1,128,1536]{2,1,0:T(8,128)(2,1)S(1)} %copy-done.1, bf16[1,128,1536]{2,1,0:T(8,128)(2,1)S(1)} %copy-done.3, ...), custom_call_target="tpu_custom_call" | custom-call | tf_op jit(solution)/shard_map/gradients/pallas_call | solution.py:242
  50.2 3.3 %collective-permute-start = (f32[32,32,128]{2,1,0:T(8,128)S(1)}, f32[32,32,128]{2,1,0:T(8,128)S(1)}, u32[]{:S(2)}, u32[]{:S(2)}) collective-permute-start(f32[32,32,128]{2,1,0:T(8,128)S(1)} %get-tuple-element.12), channel_id=1, source_target_pairs={{0,1},{1,0},{2,3},{3,2},{4,5},{5,4},{6,7},{7,6},{8,9},{9,8},{10,11... | collective-permute-start | bytes 1572872 | tf_op jit(solution)/shard_map/ppermute | solution.py:259
  53.6 1.5 %collective-permute-done = f32[32,32,128]{2,1,0:T(8,128)S(1)} collective-permute-done((f32[32,32,128]{2,1,0:T(8,128)S(1)}, f32[32,32,128]{2,1,0:T(8,128)S(1)}, u32[]{:S(2)}, u32[]{:S(2)}) %collective-permute-start) | collective-permute-done | bytes 524320 | tf_op jit(solution)/shard_map/ppermute | solution.py:259
  55.1 0.1 add.3
  55.2 22.8 %all_to_all.15.got_ref = f32[32,32,128]{2,1,0:T(8,128)S(1)} all-to-all(f32[32,32,128]{2,1,0:T(8,128)S(1)} %add.3), channel_id=1, replica_groups=mesh['x'=4,'zl'=4,'y'=8,'zh'=2,'core'=2] {'x','zl','zh'}, dimensions={0} | all-to-all | bytes 1048576 | tf_op jit(solution)/shard_map/all_to_all | solution.py:260
  77.9 0.1 sum_pieces.1
  78.0 20.7 %all_to_all.16 = f32[16,32,128]{2,1,0:T(8,128)S(1)} all-to-all(f32[16,32,128]{2,1,0:T(8,128)S(1)} %sum_pieces.1), channel_id=1, replica_groups=mesh['x'=4,'zl'=4,'y'=8,'zh'=2,'core'=2] {'y','zh'}, dimensions={0} | all-to-all | bytes 524288 | tf_op jit(solution)/shard_map/all_to_all | solution.py:269
  98.7 5.0 %all-gather = f32[32,32,128]{2,1,0:T(8,128)S(1)} all-gather(f32[16,32,128]{2,1,0:T(8,128)S(1)} %all_to_all.16), channel_id=2, replica_groups=mesh['x'=4,'zl'=4,'y'=8,'zh'=2,'core'=2] {'core'}, dimensions={0}, use_global_device_ids=true | all-gather | bytes 786432 | tf_op jit(solution)/shard_map/all_gather | solution.py:270
  103.8 0.7 outputs.1
  (1 shorter events, 0.0 us)
Async XLA Ops:
  1.3 0.7 copy-start.10
  1.3 0.7 copy-start.11
  2.0 1.0 copy-start
  2.9 1.0 copy-start.2
  3.9 1.0 copy-start.4
  4.9 0.9 copy-start.6
  5.8 0.7 copy-start.8
  6.5 38.4 %copy-start.5 = (bf16[1536,128]{1,0:T(8,128)(2,1)S(1)}, bf16[1536,128]{1,0:T(8,128)(2,1)}, u32[]{:S(2)}) copy-start(bf16[1536,128]{1,0:T(8,128)(2,1)} %w_ref.3) | copy-start | bytes 1179652
  8.5 17.4 %copy-start.9 = (f32[1536]{0:T(1024)S(1)}, f32[1536]{0:T(1024)}, u32[]{:S(2)}) copy-start(f32[1536]{0:T(1024)} %param.15) | copy-start | bytes 18436
  8.5 36.4 %copy-start.1 = (bf16[1,128,1536]{2,1,0:T(8,128)(2,1)S(1)}, bf16[1,128,1536]{2,1,0:T(8,128)(2,1)}, u32[]{:S(2)}) copy-start(bf16[1,128,1536]{2,1,0:T(8,128)(2,1)} %series_ref.3) | copy-start | bytes 1179652
  8.5 36.4 %copy-start.3 = (bf16[1,128,1536]{2,1,0:T(8,128)(2,1)S(1)}, bf16[1,128,1536]{2,1,0:T(8,128)(2,1)}, u32[]{:S(2)}) copy-start(bf16[1,128,1536]{2,1,0:T(8,128)(2,1)} %cot_ref.3) | copy-start | bytes 1179652
  8.5 36.4 %copy-start.7 = (f32[16,1536]{1,0:T(8,128)S(1)}, f32[16,1536]{1,0:T(8,128)}, u32[]{:S(2)}) copy-start(f32[16,1536]{1,0:T(8,128)} %table_ref.3) | copy-start | bytes 294916
  8.5 36.4 %all-to-all-start = ((f32[32,32,128]{2,1,0:T(8,128)}), f32[32,32,128]{2,1,0:T(8,128)S(1)}, u32[]{:S(2)}, u32[]{:S(2)}) async-start(f32[32,32,128]{2,1,0:T(8,128)} %slab_ends.1), calls=%async_computation | async-start | bytes 1048576 | tf_op jit(solution)/shard_map/all_to_all | solution.py:241
  50.2 4.9 %collective-permute-start = (f32[32,32,128]{2,1,0:T(8,128)S(1)}, f32[32,32,128]{2,1,0:T(8,128)S(1)}, u32[]{:S(2)}, u32[]{:S(2)}) collective-permute-start(f32[32,32,128]{2,1,0:T(8,128)S(1)} %get-tuple-element.12), channel_id=1, source_target_pairs={{0,1},{1,0},{2,3},{3,2},{4,5},{5,4},{6,7},{7,6},{8,9},{9,8},{10,11... | collective-permute-start | bytes 1572872 | tf_op jit(solution)/shard_map/ppermute | solution.py:259

commit v2 on v1

v2 whole, which is shorter than its diff:
```python
import functools
import jax
import jax.numpy as jnp
from jax import lax
from jax.experimental import pallas as pl
from jax.experimental.pallas import tpu as pltpu
from jax.sharding import Mesh, PartitionSpec as P

SLAB = 128
LANES = 128
CHUNKS = 8
STEPS = SLAB // CHUNKS
FAR = 1e9
F32 = jnp.float32
BF16 = jnp.bfloat16


def slab_index():
    return (lax.axis_index("y") * 2 + lax.axis_index("zh")) * 2 + lax.axis_index("core")


def elapsed_row(starts_ref, times_ref, me):
    position = lax.broadcasted_iota(jnp.int32, (1, SLAB), 1) + me * SLAB
    reset = position == starts_ref[0, 0]
    for k in range(1, starts_ref.shape[1]):
        reset = jnp.logical_or(reset, position == starts_ref[0, k])
    return jnp.where(reset, FAR, times_ref[...])


def ends_kernel(
    blocks, chips, starts_hbm, star_hbm, times_hbm, series_hbm, cot_hbm, w_hbm, table_hbm, lograte_hbm,
    out_ref, ends_ref, starts_ref, star_ref, times_ref, series_ref, cot_ref, w_ref, table_ref, lograte_ref, sems,
):
    sources = (starts_hbm, star_hbm, times_hbm, table_hbm, lograte_hbm, series_hbm, w_hbm, cot_hbm)
    targets = (starts_ref, star_ref, times_ref, table_ref, lograte_ref, series_ref, w_ref, cot_ref)
    copies = [pltpu.make_async_copy(a, b, sems.at[k]) for k, (a, b) in enumerate(zip(sources, targets))]
    for copy in copies:
        copy.start()
    core = lax.axis_index("core")
    me = slab_index()
    for copy in copies[:3]:
        copy.wait()
    elapsed = elapsed_row(starts_ref, times_ref, me)
    row = lax.broadcasted_iota(jnp.int32, (SLAB, SLAB), 0)
    lane = lax.broadcasted_iota(jnp.int32, (SLAB, SLAB), 1)
    spread = jnp.broadcast_to(elapsed, (SLAB, SLAB))
    to_end = jnp.sum(jnp.where(lane > row, spread, 0.0), axis=1, keepdims=True)
    from_start = jnp.sum(jnp.where(lane <= row, spread, 0.0), axis=1, keepdims=True)
    to_end = jnp.broadcast_to(to_end, (SLAB, LANES))
    from_start = jnp.broadcast_to(from_start, (SLAB, LANES))
    total = jnp.sum(elapsed, axis=1, keepdims=True)
    for copy in copies[3:]:
        copy.wait()
    bias = table_ref[pl.ds(star_ref[0], 1), :]
    for h in range(blocks):
        cols = slice(h * LANES, (h + 1) * LANES)
        proj = jnp.dot(series_ref[0, :, cols], w_ref[cols, :], preferred_element_type=F32) + bias[:, cols]
        grad = cot_ref[0, :, cols].astype(F32)
        slope = -jnp.exp(lograte_ref[h : h + 1, :])
        late = jnp.exp(slope * to_end)
        early = jnp.exp(slope * from_start)
        ends_ref[0, h : h + 1, :] = jnp.sum(late * proj, axis=0, keepdims=True)
        ends_ref[0, blocks + h : blocks + h + 1, :] = jnp.sum(late * grad, axis=0, keepdims=True)
        ends_ref[1, h : h + 1, :] = jnp.sum(early * proj, axis=0, keepdims=True)
        ends_ref[1, blocks + h : blocks + h + 1, :] = jnp.sum(early * grad, axis=0, keepdims=True)
    tail = jnp.broadcast_to(total, (8, LANES))
    ends_ref[0, 2 * blocks : 2 * blocks + 8, :] = tail
    ends_ref[1, 2 * blocks : 2 * blocks + 8, :] = tail
    for chip in range(chips):
        out_ref[chip] = ends_ref[jnp.where(2 * chip + 1 - core > me, 0, 1)]


def shift(x, k, fill, sublane):
    if k > 0:
        return jnp.where(sublane < k, fill, pltpu.roll(x, k, 0))
    return jnp.where(sublane >= CHUNKS + k, fill, pltpu.roll(x, CHUNKS + k, 0))


def chunk_entries(ends, through, carry, sublane, sign):
    for k in (1, 2, 4):
        ends = ends + through * shift(ends, sign * k, 0.0, sublane)
        through = through * shift(through, sign * k, 1.0, sublane)
    return shift(ends + through * carry, sign, jnp.broadcast_to(carry, ends.shape), sublane)


def local_kernel(
    blocks, starts_ref, star_ref, times_ref, series_ref, cot_ref, w_ref, table_ref, lograte_ref, gain_ref,
    base_ref, onward_ref, backward_ref, xt_ref, chunk_ref,
):
    me = slab_index()
    elapsed = elapsed_row(starts_ref, times_ref, me)
    row = lax.broadcasted_iota(jnp.int32, (SLAB, SLAB), 0)
    lane = lax.broadcasted_iota(jnp.int32, (SLAB, SLAB), 1)
    time_of_row = (row % CHUNKS) * STEPS + row // CHUNKS
    order = (lane == time_of_row).astype(F32).astype(BF16)
    gap = jnp.sum(jnp.where(lane == time_of_row, jnp.broadcast_to(elapsed, (SLAB, SLAB)), 0.0), axis=1, keepdims=True)
    gap = jnp.broadcast_to(gap, (SLAB, LANES))
    bias = table_ref[pl.ds(star_ref[0], 1), :]
    for h in range(blocks):
        cols = slice(h * LANES, (h + 1) * LANES)
        rate = jnp.exp(lograte_ref[h : h + 1, :])
        gain = gain_ref[h : h + 1, :]
        x = jnp.dot(order, series_ref[0, :, cols], preferred_element_type=F32)
        xt_ref[cols, :] = x.T.astype(BF16)
        grad = jnp.dot(order, cot_ref[0, :, cols], preferred_element_type=F32)
        proj = jnp.dot(x.astype(BF16), w_ref[cols, :], preferred_element_type=F32) + bias[:, cols]
        drive = gain * proj
        decay = jnp.exp(-rate * gap)
        tiles = lambda v: [v[j * CHUNKS : (j + 1) * CHUNKS, :] for j in range(STEPS)]
        a, d, g, pr, dt = tiles(decay), tiles(drive), tiles(grad), tiles(proj), tiles(gap)
        zero = jnp.zeros((CHUNKS, LANES), F32)
        before_d, before_g, through = [zero], [zero], [a[0]]
        state_d, state_g = d[0], g[0]
        for j in range(1, STEPS):
            before_d.append(a[j] * state_d)
            before_g.append(a[j] * state_g)
            state_d = before_d[j] + d[j]
            state_g = before_g[j] + g[j]
            through.append(a[j] * through[j - 1])
        after_d, after_g, back = [None] * STEPS, [None] * STEPS, [None] * STEPS
        after_d[-1], after_g[-1], back[-1] = d[-1], g[-1], jnp.ones((CHUNKS, LANES), F32)
        for j in reversed(range(STEPS - 1)):
            after_d[j] = a[j + 1] * after_d[j + 1] + d[j]
            after_g[j] = a[j + 1] * after_g[j + 1] + g[j]
            back[j] = a[j + 1] * back[j + 1]
        sums = [zero] * 12
        for j in range(STEPS):
            base = after_g[j] + before_g[j] + g[j]
            rows = slice(j * CHUNKS, (j + 1) * CHUNKS)
            base_ref[rows, cols] = base
            onward_ref[rows, cols] = through[j]
            backward_ref[rows, cols] = back[j]
            dt_on, dt_back = dt[j] * through[j], dt[j] * back[j]
            terms = (
                dt[j] * (after_g[j] * before_d[j] + before_g[j] * after_d[j]),
                dt_back * before_d[j],
                dt_on * after_g[j],
                dt_on * back[j],
                dt_back * before_g[j],
                dt_on * after_d[j],
                base,
                through[j],
                back[j],
                base * pr[j],
                through[j] * pr[j],
                back[j] * pr[j],
            )
            sums = [s + t for s, t in zip(sums, terms)]
        heads = [state_d, state_g, through[-1], a[0] * after_d[0], a[0] * after_g[0]]
        for k, v in enumerate(heads + sums):
            chunk_ref[k, :, cols] = v


def combine_kernel(
    blocks, slabs, rows_dp, lograte_ref, gain_ref, got_ref, chunk_hbm, base_hbm, onward_hbm, backward_hbm, xt_hbm,
    low_ref, keep_ref, send_ref, carry_ref, sums_ref, part_ref, chunk_ref, base_ref, onward_ref, backward_ref, xt_ref, sems,
):
    sources = (chunk_hbm, base_hbm, onward_hbm, backward_hbm, xt_hbm)
    targets = (chunk_ref, base_ref, onward_ref, backward_ref, xt_ref)
    copies = [pltpu.make_async_copy(a, b, sems.at[k]) for k, (a, b) in enumerate(zip(sources, targets))]
    for copy in copies:
        copy.start()
    me = slab_index()
    width = blocks * LANES
    sublane = lax.broadcasted_iota(jnp.int32, (CHUNKS, LANES), 0)
    slope = -jnp.exp(lograte_ref[...])
    slope2 = jnp.concatenate([slope, slope], axis=0)
    took = lambda s: got_ref[s % 2, s // 2, 2 * blocks : 2 * blocks + 1, :]
    between = [None] * slabs
    run = jnp.zeros((1, LANES), F32)
    for s in reversed(range(slabs)):
        between[s] = run
        run = jnp.where(s < me, run + took(s), 0.0)
    run = jnp.zeros((1, LANES), F32)
    carry_early = jnp.zeros((2 * blocks, LANES), F32)
    carry_late = jnp.zeros((2 * blocks, LANES), F32)
    for s in range(slabs):
        x = jnp.exp(slope2 * jnp.where(s < me, between[s], run)) * got_ref[s % 2, s // 2, 0 : 2 * blocks, :]
        carry_early = carry_early + jnp.where(s < me, x, 0.0)
        carry_late = carry_late + jnp.where(s > me, x, 0.0)
        run = jnp.where(s > me, run + took(s), 0.0)
    gains = jnp.concatenate([gain_ref[...], jnp.ones((blocks, LANES), F32)], axis=0)
    carry_ref[0] = carry_early * gains
    carry_ref[1] = carry_late * gains
    for copy in copies:
        copy.wait()

    for h in range(blocks):
        cols = slice(h * LANES, (h + 1) * LANES)
        rate = jnp.exp(lograte_ref[h : h + 1, :])
        gain = gain_ref[h : h + 1, :]
        end_d, end_g, through, head_d, head_g = [chunk_ref[k, :, cols] for k in range(5)]
        enter_d = chunk_entries(end_d, through, carry_ref[0, h : h + 1, :], sublane, 1)
        enter_g = chunk_entries(end_g, through, carry_ref[0, blocks + h : blocks + h + 1, :], sublane, 1)
        leave_d = chunk_entries(head_d, through, carry_ref[1, h : h + 1, :], sublane, -1)
        leave_g = chunk_entries(head_g, through, carry_ref[1, blocks + h : blocks + h + 1, :], sublane, -1)
        enter_low, leave_low = gain * enter_g, gain * leave_g
        low = []
        for j in range(STEPS):
            rows = slice(j * CHUNKS, (j + 1) * CHUNKS)
            low.append(gain * base_ref[rows, cols] + onward_ref[rows, cols] * enter_low + backward_ref[rows, cols] * leave_low)
        low = jnp.concatenate(low, axis=0).astype(BF16)
        low_ref[:, cols] = low
        product = jnp.dot(xt_ref[cols, :], low, preferred_element_type=F32)
        for k in range(LANES // 8):
            piece, third = divmod(h * (LANES // 8) + k, 3)
            dp, quarter = divmod(piece, 4)
            core, zh = divmod(quarter, 2)
            at = (dp * 2 + zh) * 24 + third * 8
            part_ref[core, at : at + 8, :] = product[k * 8 : k * 8 + 8, :]
        c = [chunk_ref[5 + k, :, cols] for k in range(12)]
        rate_sum = c[0] + leave_g * c[1] + enter_d * c[2] + (leave_g * enter_d + enter_g * leave_d) * c[3]
        rate_sum = rate_sum + leave_d * c[4] + enter_g * c[5]
        grad_sum = c[6] + enter_g * c[7] + leave_g * c[8]
        cross_sum = c[9] + enter_g * c[10] + leave_g * c[11]
        total = lambda v: jnp.sum(v, axis=0, keepdims=True)
        sums_ref[0:1, cols] = gain * total(grad_sum)
        sums_ref[1:2, cols] = rate * (jnp.exp(-2.0 * rate) / gain * total(cross_sum) - total(rate_sum))
    share = width // rows_dp
    half = width // 2
    sums_ref[0:2, width:] = jnp.zeros((2, sums_ref.shape[1] - width), F32)
    for dp in range(rows_dp):
        for k in range(2):
            window = sums_ref[k : k + 1, dp * share : dp * share + LANES]
            for core in range(2):
                part_ref[core, half + k * rows_dp + dp : half + k * rows_dp + dp + 1, :] = window
    core = lax.axis_index("core")
    keep_ref[...] = part_ref[core]
    send_ref[...] = part_ref[1 - core]


def pair_kernel(rows_dp, star_ref, keep_ref, sent_ref, out_ref):
    other = 1 - lax.axis_index("core")
    half = keep_ref.shape[0] - 2 * rows_dp
    star = jnp.broadcast_to(star_ref[0].astype(F32), (1, LANES))
    for dp in range(rows_dp):
        extra = []
        for k in range(2):
            at = slice(half + k * rows_dp + dp, half + k * rows_dp + dp + 1)
            extra.append(keep_ref[at, :] + sent_ref[other, at, :])
        tile = jnp.concatenate(extra + [star], axis=0)
        for zh in range(2):
            piece = dp * 2 + zh
            rows = slice(piece * 24, piece * 24 + 24)
            out_ref[piece, 0:24, :] = keep_ref[rows, :] + sent_ref[other, rows, :]
            out_ref[piece, 24:27, :] = tile


def series_kernel(blocks, low_ref, cot_ref, w_ref, dx_ref):
    row = lax.broadcasted_iota(jnp.int32, (SLAB, SLAB), 0)
    lane = lax.broadcasted_iota(jnp.int32, (SLAB, SLAB), 1)
    unorder = (row == (lane % CHUNKS) * STEPS + lane // CHUNKS).astype(F32).astype(BF16)
    for h in range(blocks):
        cols = slice(h * LANES, (h + 1) * LANES)
        low = jnp.dot(unorder, low_ref[:, cols], preferred_element_type=F32).astype(BF16)
        back = lax.dot_general(low, w_ref[cols, :], (((1,), (1,)), ((), ())), preferred_element_type=F32)
        dx_ref[0, :, cols] = (cot_ref[0, :, cols].astype(F32) + back).astype(BF16)


def piece_kernel(norm, got_ref, out_ref):
    first = (lax.axis_index("core") * 2 + lax.axis_index("zh")) * 4
    total = got_ref[0, 0:24, :]
    logs = got_ref[0, 25:26, :]
    stars = [jnp.zeros((1, LANES), F32)] * 4
    for s in range(got_ref.shape[0]):
        if s:
            total = total + got_ref[s, 0:24, :]
            logs = logs + got_ref[s, 25:26, :]
        for k in range(4):
            hit = got_ref[s, 26:27, :] == (first + k).astype(F32)
            stars[k] = stars[k] + jnp.where(hit, got_ref[s, 24:25, :], 0.0)
    total = total * norm
    tail = jnp.concatenate(stars + [logs] + [jnp.zeros((3, LANES), F32)], axis=0) * norm
    for d in range(out_ref.shape[0]):
        out_ref[d, 0:24, :] = total
        out_ref[d, 24:32, :] = tail


def final_kernel(got_ref, weight_ref, star_ref, log_ref):
    share = star_ref.shape[1]
    for core in range(2):
        for zh in range(2):
            q = core * 2 + zh
            total = got_ref[core, zh]
            for y in range(1, got_ref.shape[1] // 2):
                total = total + got_ref[core, y * 2 + zh]
            weight_ref[q * 24 : q * 24 + 24, :] = total[0:24, :]
            star_ref[q * 4 : q * 4 + 4, :] = total[24:28, 0:share]
            if q == 0:
                log_ref[...] = total[28:29, 0:share]


def body(series, cotangent, step_times, seg_starts, star_of_row, block_weight, star_table, log_rate):
    _, slab_len, width = series.shape
    blocks = width // LANES
    slabs = lax.axis_size(("y", "zh", "core"))
    rows_dp = lax.axis_size(("x", "zl"))
    norm = float(1.0 / (rows_dp * slabs * slab_len) ** 0.5)
    chips = slabs // 2
    log_blocks = log_rate.reshape(blocks, LANES)
    gain = jnp.sqrt(-jnp.expm1(-2.0 * jnp.exp(log_blocks)))
    smem = pl.BlockSpec(memory_space=pltpu.SMEM)
    vmem = pl.BlockSpec(memory_space=pltpu.VMEM)
    hbm = pl.BlockSpec(memory_space=pl.ANY)
    params = pltpu.CompilerParams(vmem_limit_bytes=24 * 1024 * 1024)
    big = pltpu.CompilerParams(vmem_limit_bytes=60 * 1024 * 1024)
    shape = jax.ShapeDtypeStruct
    common = (seg_starts, star_of_row, step_times, series, cotangent, block_weight, star_table, log_blocks)
    ends = pl.pallas_call(
        functools.partial(ends_kernel, blocks, chips),
        out_shape=shape((chips, 32, LANES), F32),
        in_specs=[hbm] * 8,
        out_specs=vmem,
        scratch_shapes=[pltpu.VMEM((2, 32, LANES), F32)]
        + [pltpu.SMEM(v.shape, v.dtype) for v in common[:2]]
        + [pltpu.VMEM(v.shape, v.dtype) for v in common[2:]]
        + [pltpu.SemaphoreType.DMA((8,))],
        compiler_params=big,
        name="slab_ends",
    )(*common)
    got = lax.all_gather(lax.all_to_all(ends, ("y", "zh"), 0, 0), "core")
    wide = shape((slab_len, width), F32)
    base, onward, backward, xt, chunk = pl.pallas_call(
        functools.partial(local_kernel, blocks),
        out_shape=[wide, wide, wide, shape((width, slab_len), BF16), shape((17, CHUNKS, width), F32)],
        in_specs=[smem, smem] + [vmem] * 7,
        out_specs=[vmem] * 5,
        compiler_params=params,
        cost_estimate=pl.CostEstimate(flops=20_000_000, bytes_accessed=4_000_000, transcendentals=200_000),
        name="local_scans",
    )(*common, gain)
    low, keep, send = pl.pallas_call(
        functools.partial(combine_kernel, blocks, slabs, rows_dp),
        out_shape=[shape((slab_len, width), BF16)] + [shape((width // 2 + 2 * rows_dp, LANES), F32)] * 2,
        in_specs=[vmem] * 3 + [hbm] * 5,
        out_specs=[vmem] * 3,
        scratch_shapes=[
            pltpu.VMEM((2, 2 * blocks, LANES), F32),
            pltpu.VMEM((8, width + LANES), F32),
            pltpu.VMEM((2, width // 2 + 2 * rows_dp, LANES), F32),
        ]
        + [pltpu.VMEM(v.shape, v.dtype) for v in (chunk, base, onward, backward, xt)]
        + [pltpu.SemaphoreType.DMA((5,))],
        compiler_params=big,
        name="gradients",
    )(log_blocks, gain, got, chunk, base, onward, backward, xt)
    sent = lax.all_gather(send, "core")
    pair = pl.pallas_call(
        functools.partial(pair_kernel, rows_dp),
        out_shape=shape((rows_dp * 2, 27, LANES), F32),
        in_specs=[smem, vmem, vmem],
        out_specs=vmem,
        compiler_params=params,
        name="pair_sum",
    )(star_of_row, keep, sent)
    grad_series = pl.pallas_call(
        functools.partial(series_kernel, blocks),
        out_shape=shape(series.shape, BF16),
        in_specs=[vmem] * 3,
        out_specs=vmem,
        compiler_params=params,
        cost_estimate=pl.CostEstimate(flops=100_000_000, bytes_accessed=1_600_000, transcendentals=0),
        name="series_gradient",
    )(low, cotangent, block_weight)
    pieces = lax.all_to_all(pair, ("x", "zl", "zh"), 0, 0)
    piece = pl.pallas_call(
        functools.partial(piece_kernel, norm),
        out_shape=jax.ShapeDtypeStruct((slabs // 2, 32, LANES), F32),
        in_specs=[vmem],
        out_specs=vmem,
        compiler_params=params,
        name="sum_pieces",
    )(pieces)
    spread = lax.all_to_all(piece, ("y", "zh"), 0, 0)
    both = lax.all_gather(spread, "core")
    share = width // rows_dp
    grad_weight, grad_star, grad_log = pl.pallas_call(
        final_kernel,
        out_shape=[
            jax.ShapeDtypeStruct((share, LANES), F32),
            jax.ShapeDtypeStruct((star_table.shape[0], share), F32),
            jax.ShapeDtypeStruct((1, share), F32),
        ],
        in_specs=[vmem],
        out_specs=[vmem] * 3,
        compiler_params=params,
        name="outputs",
    )(both)
    return grad_series, grad_weight, grad_star, grad_log.reshape(share)


def solution(mesh):
    fine = Mesh(mesh.devices.reshape(4, 4, 8, 2, 2), ("x", "zl", "y", "zh", "core"))
    dp, ctx = ("x", "zl"), ("y", "zh", "core")
    in_specs = (P(dp, ctx, None), P(dp, ctx, None), P(dp, ctx), P(dp, None), P(dp), P(), P(), P())
    out_specs = (P(dp, ctx, None), P(dp, None), P(None, dp), P(dp))
    return jax.shard_map(body, mesh=fine, in_specs=in_specs, out_specs=out_specs, check_vma=False)
```

time: 105 us -> 95.9 us (0.913)
  blocking collectives: 48.5 us -> 34.9 us
  Pallas kernels: 8.04 us -> 13 us
  waiting for transfers between devices: 20.5 us -> 19.2 us
  starting transfers between devices: 20.7 us -> 21.9 us
    all_to_all x1 -> x0, blocking collectives: 20.7 us -> none  [body(): spread = lax.all_to_all(piece, ('y', 'zh'), 0, 0)]
    all_gather x0 -> x2, blocking collectives: none -> 7.21 us  [the longest x1 4.48 us: body(): got = lax.all_gather(lax.all_to_all(ends, ('y', 'zh'), 0, 0), 'core')]
    all_to_all x1 -> x2, starting transfers between devices: 17.3 us -> 21.9 us  [the longest x1 16.3 us: body(): got = lax.all_gather(lax.all_to_all(ends, ('y', 'zh'), 0, 0), 'core')]
    pallas_call x2 -> x5, Pallas kernels: 7.3 us -> 11.6 us  [the longest x1 4.7 us: body(): pl.pallas_call(functools.partial(combine_kernel, blocks, slabs, rows_dp),...]
    ppermute x1 -> x0, starting transfers between devices: 3.33 us -> none  [body(): pair = keep + lax.ppermute(send, 'core', [(0, 1), (1, 0)])]
    ppermute x1 -> x0, waiting for transfers between devices: 1.51 us -> none  [body(): pair = keep + lax.ppermute(send, 'core', [(0, 1), (1, 0)])]
    unnamed x24 -> x30, local copies, waits for them, and re-layouts: 5.25 us -> 4.97 us
    all_to_all x1 -> x2, waiting for transfers between devices: 19 us -> 19.2 us  [the longest x1 12.1 us: body(): spread = lax.all_to_all(piece, ('y', 'zh'), 0, 0)]
  transfers between devices with their start and end apart: 2 -> 2, of which waited for: 2 -> 2; matrix products, arithmetic and copies ran while one was open for 0% -> 0% of each run, Pallas kernels for 0% -> 4%
where the time goes in v2:
time: 95.9 us; the launch traced here: 95.4 us
  blocking collectives  34.9 us (36%)
  starting transfers between devices  21.9 us (23%)
  waiting for transfers between devices  19.2 us (20%)
  Pallas kernels  13 us (14%)
  local copies, waits for them, and re-layouts  4.97 us (5%)
  between operations  1.47 us (2%)
    all_to_all x1, blocking collectives, body(): pieces = lax.all_to_all(pair, ('x', 'zl', 'zh'), 0, 0)  22.7 us
    all_to_all x1, starting transfers between devices, body(): got = lax.all_gather(lax.all_to_all(ends, ('y', 'zh'), 0, 0), 'core')  16.3 us
    all_to_all x1, waiting for transfers between devices, body(): spread = lax.all_to_all(piece, ('y', 'zh'), 0, 0)  12.1 us
    all_to_all x1, waiting for transfers between devices, body(): got = lax.all_gather(lax.all_to_all(ends, ('y', 'zh'), 0, 0), 'core')  7.05 us
    all_to_all x1, starting transfers between devices, body(): spread = lax.all_to_all(piece, ('y', 'zh'), 0, 0)  5.6 us
    unnamed x30, local copies, waits for them, and re-layouts  4.97 us
    all_gather x1, blocking collectives, body(): both = lax.all_gather(spread, 'core')  4.94 us
    pallas_call x1, Pallas kernels, body(): pl.pallas_call(functools.partial(combine_kernel, blocks, slabs, rows_dp),...  4.7 us
  transfers between devices with their start and end apart: 2, of which 2 were waited for; matrix products, arithmetic and copies ran while one was open for 0% of the time, Pallas kernels for 4%

profile of v2, /device:TPU:1, one launch (start us, length us, event | category | flops | bytes accessed | tf_op | source)
XLA Modules:
  0.0 95.4 jit_solution(6620351224507816478)
XLA Ops:
  1.3 0.0 copy-start.1
  1.3 0.0 copy-start.2
  1.3 2.8 %slab_ends.1 = f32[16,32,128]{2,1,0:T(8,128)} custom-call(s32[1,4]{1,0:T(1,128)} %starts_ref.1, s32[1]{0:T(128)S(6)} %copy.12.star_hbm.star_ref, f32[1,128]{1,0:T(1,128)} %times_ref.1, bf16[1,128,1536]{2,1,0:T(8,128)(2,1)} %series_ref.1, bf16[1,128,1536]{2,1,0:T(8,128)(2,1)} %cot_ref.3, bf16[1536,128]{1,0:T(8,128)(2,1)} %w_ref.3, f32[16,1536]{1,0:T(8,128)} %table_ref.1, ...), custom_call_target="tpu_custom_call" | custom-call | tf_op jit(solution)/shard_map/slab_ends/pallas_call | solution.py:309
  4.1 0.0 copy-start.11
  4.1 0.0 copy-start
  4.1 0.0 copy-start.9
  4.1 16.3 %all-to-all-start = ((f32[16,32,128]{2,1,0:T(8,128)}), f32[16,32,128]{2,1,0:T(8,128)S(1)}, u32[]{:S(2)}, u32[]{:S(2)}) async-start(f32[16,32,128]{2,1,0:T(8,128)} %slab_ends.1), calls=%async_computation | async-start | bytes 524288 | tf_op jit(solution)/shard_map/all_to_all | solution.py:321
  20.5 0.0 copy-done.11
  20.5 0.0 copy-start.13
  20.5 0.0 copy-start.14
  20.5 0.0 copy-done.1
  20.5 0.0 copy-done.2
  20.5 0.0 copy-done
  20.6 0.0 copy-done.9
  20.6 0.6 copy-done.13
  21.1 0.0 copy-done.14
  21.1 0.0 copy-start.12
  21.2 2.3 %local_scans.1 = (f32[128,1536]{1,0:T(8,128)S(1)}, f32[128,1536]{1,0:T(8,128)S(1)}, f32[128,1536]{1,0:T(8,128)S(1)}, bf16[1536,128]{1,0:T(8,128)(2,1)S(1)}, f32[17,8,1536]{2,1,0:T(8,128)S(1)}) custom-call(s32[1,4]{1,0:T(1,128)S(1)} %copy-done.13, s32[1]{0:T(128)S(6)} %copy.12.star_hbm.star_ref, f32[1,128]{1,0:T(1,128)S(1)} %copy-done.14, ...), custom_call_target="tpu_custom_call" | custom-call | flops 20000000 | bytes 4000000 | tf_op jit(solution)/shard_map/local_scans/pallas_call | solution.py:323
  23.5 0.0 copy-done.12
  23.5 0.0 copy-start.3
  23.5 0.9 copy-done.3
  24.4 0.0 copy-start.4
  24.4 0.9 copy-done.4
  25.3 0.0 copy-start.5
  25.3 0.9 copy-done.5
  26.2 0.0 copy-start.6
  26.2 0.9 copy-done.6
  27.1 0.0 copy-start.10
  27.1 0.7 copy-done.10
  27.8 7.1 %all-to-all-done = f32[16,32,128]{2,1,0:T(8,128)S(1)} async-done(((f32[16,32,128]{2,1,0:T(8,128)}), f32[16,32,128]{2,1,0:T(8,128)S(1)}, u32[]{:S(2)}, u32[]{:S(2)}) %all-to-all-start) | async-done | bytes 262176 | tf_op jit(solution)/shard_map/all_to_all | solution.py:321
  34.9 4.5 %all-gather = f32[32,32,128]{2,1,0:T(8,128)} all-gather(f32[16,32,128]{2,1,0:T(8,128)S(1)} %all-to-all-done), channel_id=2, replica_groups=mesh['x'=4,'zl'=4,'y'=8,'zh'=2,'core'=2] {'core'}, dimensions={0}, use_global_device_ids=true | all-gather | bytes 786432 | tf_op jit(solution)/shard_map/all_gather | solution.py:321
  39.4 4.7 %gradients.1 = (bf16[128,1536]{1,0:T(8,128)(2,1)}, f32[800,128]{1,0:T(8,128)}, f32[800,128]{1,0:T(8,128)}) custom-call(f32[12,128]{1,0:T(8,128)} %bitcast.9, f32[12,128]{1,0:T(8,128)} %copy-done.12, f32[2,16,32,128]{3,2,1,0:T(8,128)} %bitcast.11, f32[17,8,1536]{2,1,0:T(8,128)} %copy-done.3, f32[128,1536]{1,0:T(8,128)} %copy-done.4, f32[128,1536]{1,0:T(8,128)} %copy-done.5, ...), custom_call_target="tpu_custom_call" | custom-call | tf_op jit(solution)/shard_map/gradients/pallas_call | solution.py:332
  44.1 0.0 copy-start.7
  44.1 2.7 %all-gather.1 = f32[1600,128]{1,0:T(8,128)S(1)} all-gather(f32[800,128]{1,0:T(8,128)} %get-tuple-element.22), channel_id=3, replica_groups=mesh['x'=4,'zl'=4,'y'=8,'zh'=2,'core'=2] {'core'}, dimensions={0}, use_global_device_ids=true | all-gather | bytes 1228800 | tf_op jit(solution)/shard_map/all_gather | solution.py:347
  46.8 0.0 copy-done.7
  46.8 0.1 pair_sum.1
  46.9 22.7 %all_to_all.15.got_ref = f32[32,27,128]{2,1,0:T(8,128)S(1)} all-to-all(f32[32,27,128]{2,1,0:T(8,128)S(1)} %pair_sum.1), channel_id=1, replica_groups=mesh['x'=4,'zl'=4,'y'=8,'zh'=2,'core'=2] {'x','zl','zh'}, dimensions={0} | all-to-all | bytes 884736 | tf_op jit(solution)/shard_map/all_to_all | solution.py:365
  69.6 0.8 sum_pieces.1
  70.4 0.0 copy-start.8
  70.4 5.6 %all-to-all-start.2 = ((f32[16,32,128]{2,1,0:T(8,128)}), f32[16,32,128]{2,1,0:T(8,128)S(1)}, u32[]{:S(2)}, u32[]{:S(2)}) async-start(f32[16,32,128]{2,1,0:T(8,128)} %sum_pieces.1), calls=%async_computation.2 | async-start | bytes 524288 | tf_op jit(solution)/shard_map/all_to_all | solution.py:374
  76.0 0.0 copy-done.8
  76.0 1.7 %series_gradient.1 = bf16[1,128,1536]{2,1,0:T(8,128)(2,1)} custom-call(bf16[128,1536]{1,0:T(8,128)(2,1)S(1)} %copy-done.8, bf16[1,128,1536]{2,1,0:T(8,128)(2,1)S(1)} %copy-done, bf16[1536,128]{1,0:T(8,128)(2,1)S(1)} %copy-done.1), custom_call_target="tpu_custom_call" | custom-call | flops 100000000 | bytes 1600000 | tf_op jit(solution)/shard_map/series_gradient/pallas_call | solution.py:356
  77.7 12.1 %all-to-all-done.2 = f32[16,32,128]{2,1,0:T(8,128)S(1)} async-done(((f32[16,32,128]{2,1,0:T(8,128)}), f32[16,32,128]{2,1,0:T(8,128)S(1)}, u32[]{:S(2)}, u32[]{:S(2)}) %all-to-all-start.2) | async-done | bytes 262176 | tf_op jit(solution)/shard_map/all_to_all | solution.py:374
  89.9 4.9 %all-gather.2 = f32[32,32,128]{2,1,0:T(8,128)S(1)} all-gather(f32[16,32,128]{2,1,0:T(8,128)S(1)} %all-to-all-done.2), channel_id=4, replica_groups=mesh['x'=4,'zl'=4,'y'=8,'zh'=2,'core'=2] {'core'}, dimensions={0}, use_global_device_ids=true | all-gather | bytes 786432 | tf_op jit(solution)/shard_map/all_gather | solution.py:375
  94.8 0.7 outputs.1
  (1 shorter events, 0.0 us)
Async XLA Ops:
  1.3 19.2 %copy-start.1 = (bf16[1536,128]{1,0:T(8,128)(2,1)S(1)}, bf16[1536,128]{1,0:T(8,128)(2,1)}, u32[]{:S(2)}) copy-start(bf16[1536,128]{1,0:T(8,128)(2,1)} %w_ref.3) | copy-start | bytes 1179652
  1.3 19.2 %copy-start.2 = (bf16[1,128,1536]{2,1,0:T(8,128)(2,1)S(1)}, bf16[1,128,1536]{2,1,0:T(8,128)(2,1)}, u32[]{:S(2)}) copy-start(bf16[1,128,1536]{2,1,0:T(8,128)(2,1)} %series_ref.1) | copy-start | bytes 1179652
  4.1 16.4 %copy-start.11 = (f32[1536]{0:T(1024)S(1)}, f32[1536]{0:T(1024)}, u32[]{:S(2)}) copy-start(f32[1536]{0:T(1024)} %param.15) | copy-start | bytes 18436
  4.1 16.5 %copy-start = (bf16[1,128,1536]{2,1,0:T(8,128)(2,1)S(1)}, bf16[1,128,1536]{2,1,0:T(8,128)(2,1)}, u32[]{:S(2)}) copy-start(bf16[1,128,1536]{2,1,0:T(8,128)(2,1)} %cot_ref.3) | copy-start | bytes 1179652
  4.1 16.5 %copy-start.9 = (f32[16,1536]{1,0:T(8,128)S(1)}, f32[16,1536]{1,0:T(8,128)}, u32[]{:S(2)}) copy-start(f32[16,1536]{1,0:T(8,128)} %table_ref.1) | copy-start | bytes 294916
  4.1 30.8 %all-to-all-start = ((f32[16,32,128]{2,1,0:T(8,128)}), f32[16,32,128]{2,1,0:T(8,128)S(1)}, u32[]{:S(2)}, u32[]{:S(2)}) async-start(f32[16,32,128]{2,1,0:T(8,128)} %slab_ends.1), calls=%async_computation | async-start | bytes 524288 | tf_op jit(solution)/shard_map/all_to_all | solution.py:321
  20.5 0.7 copy-start.13
  20.5 0.7 copy-start.14
  21.1 2.3 %copy-start.12 = (f32[12,128]{1,0:T(8,128)}, f32[12,128]{1,0:T(8,128)S(1)}, u32[]{:S(2)}) copy-start(f32[12,128]{1,0:T(8,128)S(1)} %negate_sqrt_fusion.gain_ref) | copy-start | bytes 18436
  23.5 0.9 copy-start.3
  24.4 0.9 copy-start.4
  25.3 0.9 copy-start.5
  26.2 0.9 copy-start.6
  27.1 0.7 copy-start.10
  44.1 2.7 %copy-start.7 = (f32[800,128]{1,0:T(8,128)S(1)}, f32[800,128]{1,0:T(8,128)}, u32[]{:S(2)}) copy-start(f32[800,128]{1,0:T(8,128)} %get-tuple-element.21.keep_ref) | copy-start | bytes 1228804
  70.4 5.6 %copy-start.8 = (bf16[128,1536]{1,0:T(8,128)(2,1)S(1)}, bf16[128,1536]{1,0:T(8,128)(2,1)}, u32[]{:S(2)}) copy-start(bf16[128,1536]{1,0:T(8,128)(2,1)} %get-tuple-element.20.low_ref) | copy-start | bytes 1179652
  70.4 19.5 %all-to-all-start.2 = ((f32[16,32,128]{2,1,0:T(8,128)}), f32[16,32,128]{2,1,0:T(8,128)S(1)}, u32[]{:S(2)}, u32[]{:S(2)}) async-start(f32[16,32,128]{2,1,0:T(8,128)} %sum_pieces.1), calls=%async_computation.2 | async-start | bytes 524288 | tf_op jit(solution)/shard_map/all_to_all | solution.py:374

commit v3 on v2

--- a/solution.py
+++ b/solution.py
@@ -11,6 +11,7 @@
 CHUNKS = 8
 STEPS = SLAB // CHUNKS
 FAR = 1e9
+GROUPS = 4
 F32 = jnp.float32
 BF16 = jnp.bfloat16
 
@@ -76,21 +77,22 @@
     return jnp.where(sublane >= CHUNKS + k, fill, pltpu.roll(x, CHUNKS + k, 0))
 
 
-def chunk_entries(ends, through, carry, sublane, sign):
+def chunk_entries(ends, through, sublane, sign):
     for k in (1, 2, 4):
         ends = ends + through * shift(ends, sign * k, 0.0, sublane)
         through = through * shift(through, sign * k, 1.0, sublane)
-    return shift(ends + through * carry, sign, jnp.broadcast_to(carry, ends.shape), sublane)
+    return shift(ends, sign, 0.0, sublane), shift(through, sign, 1.0, sublane)
 
 
 def local_kernel(
     blocks, starts_ref, star_ref, times_ref, series_ref, cot_ref, w_ref, table_ref, lograte_ref, gain_ref,
-    base_ref, onward_ref, backward_ref, xt_ref, chunk_ref,
+    base_ref, onward_ref, backward_ref, xt_ref, table_sums_ref,
 ):
     me = slab_index()
     elapsed = elapsed_row(starts_ref, times_ref, me)
     row = lax.broadcasted_iota(jnp.int32, (SLAB, SLAB), 0)
     lane = lax.broadcasted_iota(jnp.int32, (SLAB, SLAB), 1)
+    sublane = lax.broadcasted_iota(jnp.int32, (CHUNKS, LANES), 0)
     time_of_row = (row % CHUNKS) * STEPS + row // CHUNKS
     order = (lane == time_of_row).astype(F32).astype(BF16)
     gap = jnp.sum(jnp.where(lane == time_of_row, jnp.broadcast_to(elapsed, (SLAB, SLAB)), 0.0), axis=1, keepdims=True)
@@ -123,46 +125,61 @@
             after_d[j] = a[j + 1] * after_d[j + 1] + d[j]
             after_g[j] = a[j + 1] * after_g[j + 1] + g[j]
             back[j] = a[j + 1] * back[j + 1]
+        enter_d, onto = chunk_entries(state_d, through[-1], sublane, 1)
+        enter_g, _ = chunk_entries(state_g, through[-1], sublane, 1)
+        leave_d, off = chunk_entries(a[0] * after_d[0], through[-1], sublane, -1)
+        leave_g, _ = chunk_entries(a[0] * after_g[0], through[-1], sublane, -1)
         sums = [zero] * 12
         for j in range(STEPS):
-            base = after_g[j] + before_g[j] + g[j]
-            rows = slice(j * CHUNKS, (j + 1) * CHUNKS)
-            base_ref[rows, cols] = base
-            onward_ref[rows, cols] = through[j]
-            backward_ref[rows, cols] = back[j]
-            dt_on, dt_back = dt[j] * through[j], dt[j] * back[j]
+            kept_d = before_d[j] + through[j] * enter_d
+            kept_g = before_g[j] + through[j] * enter_g
+            later_d = after_d[j] + back[j] * leave_d
+            later_g = after_g[j] + back[j] * leave_g
+            on, off_j = through[j] * onto, back[j] * off
+            base = later_g + kept_g + g[j]
+            rows = slice(h * LANES + j * CHUNKS, h * LANES + (j + 1) * CHUNKS)
+            base_ref[rows, :] = gain * base
+            onward_ref[rows, :] = gain * on
+            backward_ref[rows, :] = gain * off_j
+            dt_on, dt_off = dt[j] * on, dt[j] * off_j
             terms = (
-                dt[j] * (after_g[j] * before_d[j] + before_g[j] * after_d[j]),
-                dt_back * before_d[j],
-                dt_on * after_g[j],
-                dt_on * back[j],
-                dt_back * before_g[j],
-                dt_on * after_d[j],
+                dt[j] * (later_g * kept_d + kept_g * later_d),
+                dt_off * kept_d,
+                dt_on * later_g,
+                dt_on * off_j,
+                dt_off * kept_g,
+                dt_on * later_d,
                 base,
-                through[j],
-                back[j],
+                on,
+                off_j,
                 base * pr[j],
-                through[j] * pr[j],
-                back[j] * pr[j],
+                on * pr[j],
+                off_j * pr[j],
             )
             sums = [s + t for s, t in zip(sums, terms)]
-        heads = [state_d, state_g, through[-1], a[0] * after_d[0], a[0] * after_g[0]]
-        for k, v in enumerate(heads + sums):
-            chunk_ref[k, :, cols] = v
+        for k, v in enumerate(sums):
+            table_sums_ref[k, h : h + 1, :] = jnp.sum(v, axis=0, keepdims=True)
 
 
 def combine_kernel(
-    blocks, slabs, rows_dp, lograte_ref, gain_ref, got_ref, chunk_hbm, base_hbm, onward_hbm, backward_hbm, xt_hbm,
-    low_ref, keep_ref, send_ref, carry_ref, sums_ref, part_ref, chunk_ref, base_ref, onward_ref, backward_ref, xt_ref, sems,
+    blocks, slabs, rows_dp, lograte_ref, gain_ref, got_ref, sums_hbm, base_hbm, onward_hbm, backward_hbm, xt_hbm,
+    low_hbm, keep_hbm, send_hbm, part_ref, low_ref, sums_ref, base_ref, onward_ref, backward_ref, xt_ref, sum_sem, sems, out_sems,
 ):
-    sources = (chunk_hbm, base_hbm, onward_hbm, backward_hbm, xt_hbm)
-    targets = (chunk_ref, base_ref, onward_ref, backward_ref, xt_ref)
-    copies = [pltpu.make_async_copy(a, b, sems.at[k]) for k, (a, b) in enumerate(zip(sources, targets))]
-    for copy in copies:
-        copy.start()
+    groups = GROUPS
+    rows_in = blocks // groups * LANES
+    rows_out = rows_in // 2
+    half = blocks * LANES // 2
+    sums_copy = pltpu.make_async_copy(sums_hbm, sums_ref, sum_sem.at[0])
+    sums_copy.start()
+    pairs = ((base_hbm, base_ref), (onward_hbm, onward_ref), (backward_hbm, backward_ref), (xt_hbm, xt_ref))
+    loads = []
+    for group in range(groups):
+        rows = slice(group * rows_in, (group + 1) * rows_in)
+        loads.append([pltpu.make_async_copy(a.at[rows], b.at[rows], sems.at[group, k]) for k, (a, b) in enumerate(pairs)])
+        for copy in loads[-1]:
+            copy.start()
     me = slab_index()
-    width = blocks * LANES
-    sublane = lax.broadcasted_iota(jnp.int32, (CHUNKS, LANES), 0)
+    mine = lax.axis_index("core")
     slope = -jnp.exp(lograte_ref[...])
     slope2 = jnp.concatenate([slope, slope], axis=0)
     took = lambda s: got_ref[s % 2, s // 2, 2 * blocks : 2 * blocks + 1, :]
@@ -179,66 +196,64 @@
         carry_early = carry_early + jnp.where(s < me, x, 0.0)
         carry_late = carry_late + jnp.where(s > me, x, 0.0)
         run = jnp.where(s > me, run + took(s), 0.0)
-    gains = jnp.concatenate([gain_ref[...], jnp.ones((blocks, LANES), F32)], axis=0)
-    carry_ref[0] = carry_early * gains
-    carry_ref[1] = carry_late * gains
-    for copy in copies:
+    gain = gain_ref[...]
+    early_d, early_g = gain * carry_early[0:blocks], carry_early[blocks:]
+    late_d, late_g = gain * carry_late[0:blocks], carry_late[blocks:]
+    sums_copy.wait()
+    c = [sums_ref[k, 0:blocks, :] for k in range(12)]
+    rate_sum = c[0] + late_g * c[1] + early_d * c[2] + (late_g * early_d + early_g * late_d) * c[3]
+    rate_sum = rate_sum + late_d * c[4] + early_g * c[5]
+    grad_sum = c[6] + early_g * c[7] + late_g * c[8]
+    cross_sum = c[9] + early_g * c[10] + late_g * c[11]
+    proj_sum = gain * grad_sum
+    log_sum = jnp.exp(2.0 * slope) / gain * cross_sum - rate_sum
+    log_sum = -slope * log_sum
+    for core in range(2):
+        part_ref[core, half : half + blocks, :] = proj_sum
+        part_ref[core, half + 16 : half + 16 + blocks, :] = log_sum
+
+    stores = []
+    for group in range(groups):
+        for copy in loads[group]:
+            copy.wait()
+        for h in range(group * blocks // groups, (group + 1) * blocks // groups):
+            rows = slice(h * LANES, (h + 1) * LANES)
+            low = base_ref[rows, :] + onward_ref[rows, :] * early_g[h : h + 1, :] + backward_ref[rows, :] * late_g[h : h + 1, :]
+            low = low.astype(BF16)
+            low_ref[rows, :] = low
+            product = jnp.dot(xt_ref[rows, :], low, preferred_element_type=F32)
+            for k in range(LANES // 8):
+                piece, third = divmod(h * (LANES // 8) + k, 3)
+                dp, quarter = divmod(piece, 4)
+                core, zh = divmod(quarter, 2)
+                at = (dp * 2 + zh) * 24 + third * 8
+                part_ref[core, at : at + 8, :] = product[k * 8 : k * 8 + 8, :]
+        end = half + 32 if group == groups - 1 else (group + 1) * rows_out
+        rows = slice(group * rows_out, end)
+        stores.append(pltpu.make_async_copy(part_ref.at[1 - mine, rows], send_hbm.at[rows], out_sems.at[group, 0]))
+        stores.append(pltpu.make_async_copy(part_ref.at[mine, rows], keep_hbm.at[rows], out_sems.at[group, 1]))
+        rows = slice(group * rows_in, (group + 1) * rows_in)
+        stores.append(pltpu.make_async_copy(low_ref.at[rows], low_hbm.at[rows], out_sems.at[group, 2]))
+        for copy in stores[-3:]:
+            copy.start()
+    for copy in stores:
         copy.wait()
 
-    for h in range(blocks):
-        cols = slice(h * LANES, (h + 1) * LANES)
-        rate = jnp.exp(lograte_ref[h : h + 1, :])
-        gain = gain_ref[h : h + 1, :]
-        end_d, end_g, through, head_d, head_g = [chunk_ref[k, :, cols] for k in range(5)]
-        enter_d = chunk_entries(end_d, through, carry_ref[0, h : h + 1, :], sublane, 1)
-        enter_g = chunk_entries(end_g, through, carry_ref[0, blocks + h : blocks + h + 1, :], sublane, 1)
-        leave_d = chunk_entries(head_d, through, carry_ref[1, h : h + 1, :], sublane, -1)
-        leave_g = chunk_entries(head_g, through, carry_ref[1, blocks + h : blocks + h + 1, :], sublane, -1)
-        enter_low, leave_low = gain * enter_g, gain * leave_g
-        low = []
-        for j in range(STEPS):
-            rows = slice(j * CHUNKS, (j + 1) * CHUNKS)
-            low.append(gain * base_ref[rows, cols] + onward_ref[rows, cols] * enter_low + backward_ref[rows, cols] * leave_low)
-        low = jnp.concatenate(low, axis=0).astype(BF16)
-        low_ref[:, cols] = low
-        product = jnp.dot(xt_ref[cols, :], low, preferred_element_type=F32)
-        for k in range(LANES // 8):
-            piece, third = divmod(h * (LANES // 8) + k, 3)
-            dp, quarter = divmod(piece, 4)
-            core, zh = divmod(quarter, 2)
-            at = (dp * 2 + zh) * 24 + third * 8
-            part_ref[core, at : at + 8, :] = product[k * 8 : k * 8 + 8, :]
-        c = [chunk_ref[5 + k, :, cols] for k in range(12)]
-        rate_sum = c[0] + leave_g * c[1] + enter_d * c[2] + (leave_g * enter_d + enter_g * leave_d) * c[3]
-        rate_sum = rate_sum + leave_d * c[4] + enter_g * c[5]
-        grad_sum = c[6] + enter_g * c[7] + leave_g * c[8]
-        cross_sum = c[9] + enter_g * c[10] + leave_g * c[11]
-        total = lambda v: jnp.sum(v, axis=0, keepdims=True)
-        sums_ref[0:1, cols] = gain * total(grad_sum)
-        sums_ref[1:2, cols] = rate * (jnp.exp(-2.0 * rate) / gain * total(cross_sum) - total(rate_sum))
+
+def pair_kernel(rows_dp, star_ref, keep_ref, sent_ref, out_ref, flat_ref):
+    other = 1 - lax.axis_index("core")
+    half = keep_ref.shape[0] - 32
+    width = 2 * half
     share = width // rows_dp
-    half = width // 2
-    sums_ref[0:2, width:] = jnp.zeros((2, sums_ref.shape[1] - width), F32)
-    for dp in range(rows_dp):
-        for k in range(2):
-            window = sums_ref[k : k + 1, dp * share : dp * share + LANES]
-            for core in range(2):
-                part_ref[core, half + k * rows_dp + dp : half + k * rows_dp + dp + 1, :] = window
-    core = lax.axis_index("core")
-    keep_ref[...] = part_ref[core]
-    send_ref[...] = part_ref[1 - core]
-
-
-def pair_kernel(rows_dp, star_ref, keep_ref, sent_ref, out_ref):
-    other = 1 - lax.axis_index("core")
-    half = keep_ref.shape[0] - 2 * rows_dp
+    flat_ref[0:2, width:] = jnp.zeros((2, flat_ref.shape[1] - width), F32)
+    for k in range(2):
+        table = keep_ref[half + 16 * k : half + 16 * k + 16, :] + sent_ref[other, half + 16 * k : half + 16 * k + 16, :]
+        for h in range(width // LANES):
+            flat_ref[k : k + 1, h * LANES : (h + 1) * LANES] = table[h : h + 1, :]
     star = jnp.broadcast_to(star_ref[0].astype(F32), (1, LANES))
     for dp in range(rows_dp):
-        extra = []
-        for k in range(2):
-            at = slice(half + k * rows_dp + dp, half + k * rows_dp + dp + 1)
-            extra.append(keep_ref[at, :] + sent_ref[other, at, :])
-        tile = jnp.concatenate(extra + [star], axis=0)
+        window = flat_ref[0:2, dp * share : dp * share + LANES]
+        tile = jnp.concatenate([window, star], axis=0)
         for zh in range(2):
             piece = dp * 2 + zh
             rows = slice(piece * 24, piece * 24 + 24)
@@ -252,7 +267,7 @@
     unorder = (row == (lane % CHUNKS) * STEPS + lane // CHUNKS).astype(F32).astype(BF16)
     for h in range(blocks):
         cols = slice(h * LANES, (h + 1) * LANES)
-        low = jnp.dot(unorder, low_ref[:, cols], preferred_element_type=F32).astype(BF16)
+        low = jnp.dot(unorder, low_ref[cols, :], preferred_element_type=F32).astype(BF16)
         back = lax.dot_general(low, w_ref[cols, :], (((1,), (1,)), ((), ())), preferred_element_type=F32)
         dx_ref[0, :, cols] = (cot_ref[0, :, cols].astype(F32) + back).astype(BF16)
 
@@ -319,37 +334,44 @@
         name="slab_ends",
     )(*common)
     got = lax.all_gather(lax.all_to_all(ends, ("y", "zh"), 0, 0), "core")
-    wide = shape((slab_len, width), F32)
-    base, onward, backward, xt, chunk = pl.pallas_call(
+    wide = shape((width, slab_len), F32)
+    base, onward, backward, xt, sums = pl.pallas_call(
         functools.partial(local_kernel, blocks),
-        out_shape=[wide, wide, wide, shape((width, slab_len), BF16), shape((17, CHUNKS, width), F32)],
+        out_shape=[wide, wide, wide, shape((width, slab_len), BF16), shape((12, 16, LANES), F32)],
         in_specs=[smem, smem] + [vmem] * 7,
         out_specs=[vmem] * 5,
-        compiler_params=params,
+        compiler_params=big,
         cost_estimate=pl.CostEstimate(flops=20_000_000, bytes_accessed=4_000_000, transcendentals=200_000),
         name="local_scans",
     )(*common, gain)
+    loaded = (base, onward, backward, xt)
+    half_rows = width // 2 + 32
     low, keep, send = pl.pallas_call(
         functools.partial(combine_kernel, blocks, slabs, rows_dp),
-        out_shape=[shape((slab_len, width), BF16)] + [shape((width // 2 + 2 * rows_dp, LANES), F32)] * 2,
+        out_shape=[shape((width, slab_len), BF16)] + [shape((half_rows, LANES), F32)] * 2,
         in_specs=[vmem] * 3 + [hbm] * 5,
-        out_specs=[vmem] * 3,
+        out_specs=[hbm] * 3,
         scratch_shapes=[
-            pltpu.VMEM((2, 2 * blocks, LANES), F32),
-            pltpu.VMEM((8, width + LANES), F32),
-            pltpu.VMEM((2, width // 2 + 2 * rows_dp, LANES), F32),
+            pltpu.VMEM((2, half_rows, LANES), F32),
+            pltpu.VMEM((width, slab_len), BF16),
+            pltpu.VMEM(sums.shape, F32),
         ]
-        + [pltpu.VMEM(v.shape, v.dtype) for v in (chunk, base, onward, backward, xt)]
-        + [pltpu.SemaphoreType.DMA((5,))],
+        + [pltpu.VMEM(v.shape, v.dtype) for v in loaded]
+        + [
+            pltpu.SemaphoreType.DMA((1,)),
+            pltpu.SemaphoreType.DMA((GROUPS, len(loaded))),
+            pltpu.SemaphoreType.DMA((GROUPS, 3)),
+        ],
         compiler_params=big,
         name="gradients",
-    )(log_blocks, gain, got, chunk, base, onward, backward, xt)
+    )(log_blocks, gain, got, sums, *loaded)
     sent = lax.all_gather(send, "core")
     pair = pl.pallas_call(
         functools.partial(pair_kernel, rows_dp),
         out_shape=shape((rows_dp * 2, 27, LANES), F32),
         in_specs=[smem, vmem, vmem],
         out_specs=vmem,
+        scratch_shapes=[pltpu.VMEM((8, width + LANES), F32)],
         compiler_params=params,
         name="pair_sum",
     )(star_of_row, keep, sent)

time: 95.9 us -> 95.8 us (level)
  local copies, waits for them, and re-layouts: 4.97 us -> 0.02 us
  Pallas kernels: 13 us -> 15.6 us
  waiting for transfers between devices: 19.2 us -> 21 us
    unnamed x30 -> x10, local copies, waits for them, and re-layouts: 4.97 us -> 0.02 us
    pallas_call x1, Pallas kernels: 2.3 us -> 4.88 us  [body(): pl.pallas_call(functools.partial(local_kernel, blocks), out_shape=[wide,...]
    all_to_all x1, waiting for transfers between devices: 7.05 us -> 8.89 us  [body(): got = lax.all_gather(lax.all_to_all(ends, ('y', 'zh'), 0, 0), 'core')]
  transfers between devices with their start and end apart: 2 -> 2, of which waited for: 2 -> 2; matrix products, arithmetic and copies ran while one was open for 0% -> 1% of each run, Pallas kernels for 4% -> 7%
where the time goes in v3:
time: 95.8 us; the launch traced here: 95.3 us
  blocking collectives  34.9 us (36%)
  starting transfers between devices  21.8 us (23%)
  waiting for transfers between devices  21 us (22%)
  Pallas kernels  15.6 us (16%)
  between operations  1.37 us (1%)
    all_to_all x1, blocking collectives, body(): pieces = lax.all_to_all(pair, ('x', 'zl', 'zh'), 0, 0)  22.7 us
    all_to_all x1, starting transfers between devices, body(): got = lax.all_gather(lax.all_to_all(ends, ('y', 'zh'), 0, 0), 'core')  16.2 us
    all_to_all x1, waiting for transfers between devices, body(): spread = lax.all_to_all(piece, ('y', 'zh'), 0, 0)  12.1 us
    all_to_all x1, waiting for transfers between devices, body(): got = lax.all_gather(lax.all_to_all(ends, ('y', 'zh'), 0, 0), 'core')  8.89 us
    all_to_all x1, starting transfers between devices, body(): spread = lax.all_to_all(piece, ('y', 'zh'), 0, 0)  5.6 us
    all_gather x1, blocking collectives, body(): both = lax.all_gather(spread, 'core')  4.95 us
    pallas_call x1, Pallas kernels, body(): pl.pallas_call(functools.partial(local_kernel, blocks), out_shape=[wide,...  4.88 us
    pallas_call x1, Pallas kernels, body(): pl.pallas_call(functools.partial(combine_kernel, blocks, slabs, rows_dp),...  4.69 us
  transfers between devices with their start and end apart: 2, of which 2 were waited for; matrix products, arithmetic and copies ran while one was open for 1% of the time, Pallas kernels for 7%

profile of v3, /device:TPU:1, one launch (start us, length us, event | category | flops | bytes accessed | tf_op | source)
XLA Modules:
  0.0 95.3 jit_solution(4972484006667304309)
XLA Ops:
  1.3 2.7 %slab_ends.1 = f32[16,32,128]{2,1,0:T(8,128)} custom-call(s32[1,4]{1,0:T(1,128)} %starts_ref.1, s32[1]{0:T(128)S(6)} %copy.12.star_hbm.star_ref, f32[1,128]{1,0:T(1,128)} %times_ref.1, bf16[1,128,1536]{2,1,0:T(8,128)(2,1)} %series_ref.1, bf16[1,128,1536]{2,1,0:T(8,128)(2,1)} %cot_ref.3, bf16[1536,128]{1,0:T(8,128)(2,1)} %w_ref.3, f32[16,1536]{1,0:T(8,128)} %table_ref.1, ...), custom_call_target="tpu_custom_call" | custom-call | tf_op jit(solution)/shard_map/slab_ends/pallas_call | solution.py:324
  4.0 0.0 copy-start.4
  4.0 16.2 %all-to-all-start = ((f32[16,32,128]{2,1,0:T(8,128)}), f32[16,32,128]{2,1,0:T(8,128)S(1)}, u32[]{:S(2)}, u32[]{:S(2)}) async-start(f32[16,32,128]{2,1,0:T(8,128)} %slab_ends.1), calls=%async_computation | async-start | bytes 524288 | tf_op jit(solution)/shard_map/all_to_all | solution.py:336
  20.2 0.0 copy-done.4
  20.2 0.6 negate_sqrt_fusion.gain_ref
  20.8 4.9 %local_scans.1 = (f32[1536,128]{1,0:T(8,128)}, f32[1536,128]{1,0:T(8,128)}, f32[1536,128]{1,0:T(8,128)}, bf16[1536,128]{1,0:T(8,128)(2,1)}, f32[12,16,128]{2,1,0:T(8,128)}) custom-call(s32[1,4]{1,0:T(1,128)} %starts_ref.1, s32[1]{0:T(128)S(6)} %copy.12.star_hbm.star_ref, f32[1,128]{1,0:T(1,128)} %times_ref.1, bf16[1,128,1536]{2,1,0:T(8,128)(2,1)} %series_ref.1, ...), custom_call_target="tpu_custom_call" | custom-call | flops 20000000 | bytes 4000000 | tf_op jit(solution)/shard_map/local_scans/pallas_call | solution.py:338
  25.7 8.9 %all-to-all-done = f32[16,32,128]{2,1,0:T(8,128)S(1)} async-done(((f32[16,32,128]{2,1,0:T(8,128)}), f32[16,32,128]{2,1,0:T(8,128)S(1)}, u32[]{:S(2)}, u32[]{:S(2)}) %all-to-all-start) | async-done | bytes 262176 | tf_op jit(solution)/shard_map/all_to_all | solution.py:336
  34.6 4.5 %all-gather = f32[32,32,128]{2,1,0:T(8,128)} all-gather(f32[16,32,128]{2,1,0:T(8,128)S(1)} %all-to-all-done), channel_id=2, replica_groups=mesh['x'=4,'zl'=4,'y'=8,'zh'=2,'core'=2] {'core'}, dimensions={0}, use_global_device_ids=true | all-gather | bytes 786432 | tf_op jit(solution)/shard_map/all_gather | solution.py:336
  39.1 4.7 %gradients.1 = (bf16[1536,128]{1,0:T(8,128)(2,1)}, f32[800,128]{1,0:T(8,128)}, f32[800,128]{1,0:T(8,128)}) custom-call(f32[12,128]{1,0:T(8,128)} %bitcast.11, f32[12,128]{1,0:T(8,128)} %negate_sqrt_fusion.gain_ref, f32[2,16,32,128]{3,2,1,0:T(8,128)} %bitcast.8, f32[12,16,128]{2,1,0:T(8,128)} %get-tuple-element.15.sums_hbm, ...), custom_call_target="tpu_custom_call" | custom-call | tf_op jit(solution)/shard_map/gradients/pallas_call | solution.py:349
  43.8 0.0 copy-start.2
  43.8 2.7 %all-gather.1 = f32[1600,128]{1,0:T(8,128)S(1)} all-gather(f32[800,128]{1,0:T(8,128)} %get-tuple-element.22), channel_id=3, replica_groups=mesh['x'=4,'zl'=4,'y'=8,'zh'=2,'core'=2] {'core'}, dimensions={0}, use_global_device_ids=true | all-gather | bytes 1228800 | tf_op jit(solution)/shard_map/all_gather | solution.py:368
  46.6 0.0 copy-done.2
  46.6 0.1 pair_sum.1
  46.7 22.7 %all_to_all.15.got_ref = f32[32,27,128]{2,1,0:T(8,128)S(1)} all-to-all(f32[32,27,128]{2,1,0:T(8,128)S(1)} %pair_sum.1), channel_id=1, replica_groups=mesh['x'=4,'zl'=4,'y'=8,'zh'=2,'core'=2] {'x','zl','zh'}, dimensions={0} | all-to-all | bytes 884736 | tf_op jit(solution)/shard_map/all_to_all | solution.py:387
  69.4 0.0 copy-start.1
  69.4 0.0 copy-start.3
  69.4 0.8 sum_pieces.1
  70.2 0.0 copy-start
  70.2 5.6 %all-to-all-start.2 = ((f32[16,32,128]{2,1,0:T(8,128)}), f32[16,32,128]{2,1,0:T(8,128)S(1)}, u32[]{:S(2)}, u32[]{:S(2)}) async-start(f32[16,32,128]{2,1,0:T(8,128)} %sum_pieces.1), calls=%async_computation.2 | async-start | bytes 524288 | tf_op jit(solution)/shard_map/all_to_all | solution.py:396
  75.8 0.0 copy-done.1
  75.8 0.0 copy-done.3
  75.8 0.0 copy-done
  75.8 1.8 %series_gradient.1 = bf16[1,128,1536]{2,1,0:T(8,128)(2,1)} custom-call(bf16[1536,128]{1,0:T(8,128)(2,1)S(1)} %copy-done.3, bf16[1,128,1536]{2,1,0:T(8,128)(2,1)S(1)} %copy-done, bf16[1536,128]{1,0:T(8,128)(2,1)S(1)} %copy-done.1), custom_call_target="tpu_custom_call" | custom-call | flops 100000000 | bytes 1600000 | tf_op jit(solution)/shard_map/series_gradient/pallas_call | solution.py:378
  77.6 12.1 %all-to-all-done.2 = f32[16,32,128]{2,1,0:T(8,128)S(1)} async-done(((f32[16,32,128]{2,1,0:T(8,128)}), f32[16,32,128]{2,1,0:T(8,128)S(1)}, u32[]{:S(2)}, u32[]{:S(2)}) %all-to-all-start.2) | async-done | bytes 262176 | tf_op jit(solution)/shard_map/all_to_all | solution.py:396
  89.7 4.9 %all-gather.2 = f32[32,32,128]{2,1,0:T(8,128)S(1)} all-gather(f32[16,32,128]{2,1,0:T(8,128)S(1)} %all-to-all-done.2), channel_id=4, replica_groups=mesh['x'=4,'zl'=4,'y'=8,'zh'=2,'core'=2] {'core'}, dimensions={0}, use_global_device_ids=true | all-gather | bytes 786432 | tf_op jit(solution)/shard_map/all_gather | solution.py:397
  94.6 0.7 outputs.1
Async XLA Ops:
  4.0 16.2 %copy-start.4 = (f32[1536]{0:T(1024)S(1)}, f32[1536]{0:T(1024)}, u32[]{:S(2)}) copy-start(f32[1536]{0:T(1024)} %param.15) | copy-start | bytes 18436
  4.0 30.6 %all-to-all-start = ((f32[16,32,128]{2,1,0:T(8,128)}), f32[16,32,128]{2,1,0:T(8,128)S(1)}, u32[]{:S(2)}, u32[]{:S(2)}) async-start(f32[16,32,128]{2,1,0:T(8,128)} %slab_ends.1), calls=%async_computation | async-start | bytes 524288 | tf_op jit(solution)/shard_map/all_to_all | solution.py:336
  43.8 2.8 %copy-start.2 = (f32[800,128]{1,0:T(8,128)S(1)}, f32[800,128]{1,0:T(8,128)}, u32[]{:S(2)}) copy-start(f32[800,128]{1,0:T(8,128)} %get-tuple-element.21.keep_ref) | copy-start | bytes 1228804
  69.4 6.4 %copy-start.1 = (bf16[1536,128]{1,0:T(8,128)(2,1)S(1)}, bf16[1536,128]{1,0:T(8,128)(2,1)}, u32[]{:S(2)}) copy-start(bf16[1536,128]{1,0:T(8,128)(2,1)} %w_ref.3) | copy-start | bytes 1179652
  69.4 6.4 %copy-start.3 = (bf16[1536,128]{1,0:T(8,128)(2,1)S(1)}, bf16[1536,128]{1,0:T(8,128)(2,1)}, u32[]{:S(2)}) copy-start(bf16[1536,128]{1,0:T(8,128)(2,1)} %get-tuple-element.20.low_ref) | copy-start | bytes 1179652
  70.2 5.6 %copy-start = (bf16[1,128,1536]{2,1,0:T(8,128)(2,1)S(1)}, bf16[1,128,1536]{2,1,0:T(8,128)(2,1)}, u32[]{:S(2)}) copy-start(bf16[1,128,1536]{2,1,0:T(8,128)(2,1)} %cot_ref.3) | copy-start | bytes 1179652
  70.2 19.5 %all-to-all-start.2 = ((f32[16,32,128]{2,1,0:T(8,128)}), f32[16,32,128]{2,1,0:T(8,128)S(1)}, u32[]{:S(2)}, u32[]{:S(2)}) async-start(f32[16,32,128]{2,1,0:T(8,128)} %sum_pieces.1), calls=%async_computation.2 | async-start | bytes 524288 | tf_op jit(solution)/shard_map/all_to_all | solution.py:396

commit v4 on v3

--- a/solution.py
+++ b/solution.py
@@ -17,7 +17,8 @@
 
 
 def slab_index():
-    return (lax.axis_index("y") * 2 + lax.axis_index("zh")) * 2 + lax.axis_index("core")
+    chip = (lax.axis_index("yh") * 2 + lax.axis_index("yl")) * 2 + lax.axis_index("zh")
+    return chip * 2 + lax.axis_index("core")
 
 
 def elapsed_row(starts_ref, times_ref, me):
@@ -30,12 +31,22 @@
 
 def ends_kernel(
     blocks, chips, starts_hbm, star_hbm, times_hbm, series_hbm, cot_hbm, w_hbm, table_hbm, lograte_hbm,
-    out_ref, ends_ref, starts_ref, star_ref, times_ref, series_ref, cot_ref, w_ref, table_ref, lograte_ref, sems,
+    out_ref, ends_ref, starts_ref, star_ref, times_ref, series_ref, cot_ref, w_ref, table_ref, lograte_ref, sems, group_sems,
 ):
-    sources = (starts_hbm, star_hbm, times_hbm, table_hbm, lograte_hbm, series_hbm, w_hbm, cot_hbm)
-    targets = (starts_ref, star_ref, times_ref, table_ref, lograte_ref, series_ref, w_ref, cot_ref)
+    sources = (starts_hbm, star_hbm, times_hbm, table_hbm, lograte_hbm)
+    targets = (starts_ref, star_ref, times_ref, table_ref, lograte_ref)
     copies = [pltpu.make_async_copy(a, b, sems.at[k]) for k, (a, b) in enumerate(zip(sources, targets))]
-    for copy in copies:
+    span = blocks // GROUPS * LANES
+    loads = []
+    for group in range(GROUPS):
+        part = slice(group * span, (group + 1) * span)
+        views = (
+            (series_hbm.at[:, :, part], series_ref.at[:, :, part]),
+            (w_hbm.at[part], w_ref.at[part]),
+            (cot_hbm.at[:, :, part], cot_ref.at[:, :, part]),
+        )
+        loads.append([pltpu.make_async_copy(a, b, group_sems.at[group, k]) for k, (a, b) in enumerate(views)])
+    for copy in copies + sum(loads, []):
         copy.start()
     core = lax.axis_index("core")
     me = slab_index()
@@ -54,6 +65,9 @@
         copy.wait()
     bias = table_ref[pl.ds(star_ref[0], 1), :]
     for h in range(blocks):
+        if h % (blocks // GROUPS) == 0:
+            for copy in loads[h // (blocks // GROUPS)]:
+                copy.wait()
         cols = slice(h * LANES, (h + 1) * LANES)
         proj = jnp.dot(series_ref[0, :, cols], w_ref[cols, :], preferred_element_type=F32) + bias[:, cols]
         grad = cot_ref[0, :, cols].astype(F32)
@@ -86,7 +100,7 @@
 
 def local_kernel(
     blocks, starts_ref, star_ref, times_ref, series_ref, cot_ref, w_ref, table_ref, lograte_ref, gain_ref,
-    base_ref, onward_ref, backward_ref, xt_ref, table_sums_ref,
+    base_ref, xt_ref, table_sums_ref, reach_ref,
 ):
     me = slab_index()
     elapsed = elapsed_row(starts_ref, times_ref, me)
@@ -97,6 +111,10 @@
     order = (lane == time_of_row).astype(F32).astype(BF16)
     gap = jnp.sum(jnp.where(lane == time_of_row, jnp.broadcast_to(elapsed, (SLAB, SLAB)), 0.0), axis=1, keepdims=True)
     gap = jnp.broadcast_to(gap, (SLAB, LANES))
+    spread = jnp.broadcast_to(elapsed, (SLAB, SLAB))
+    for k, mask in enumerate((lane <= time_of_row, lane > time_of_row)):
+        reach = jnp.sum(jnp.where(mask, spread, 0.0), axis=1, keepdims=True)
+        reach_ref[k] = jnp.broadcast_to(reach, (SLAB, LANES))
     bias = table_ref[pl.ds(star_ref[0], 1), :]
     for h in range(blocks):
         cols = slice(h * LANES, (h + 1) * LANES)
@@ -139,8 +157,6 @@
             base = later_g + kept_g + g[j]
             rows = slice(h * LANES + j * CHUNKS, h * LANES + (j + 1) * CHUNKS)
             base_ref[rows, :] = gain * base
-            onward_ref[rows, :] = gain * on
-            backward_ref[rows, :] = gain * off_j
             dt_on, dt_off = dt[j] * on, dt[j] * off_j
             terms = (
                 dt[j] * (later_g * kept_d + kept_g * later_d),
@@ -162,22 +178,10 @@
 
 
 def combine_kernel(
-    blocks, slabs, rows_dp, lograte_ref, gain_ref, got_ref, sums_hbm, base_hbm, onward_hbm, backward_hbm, xt_hbm,
-    low_hbm, keep_hbm, send_hbm, part_ref, low_ref, sums_ref, base_ref, onward_ref, backward_ref, xt_ref, sum_sem, sems, out_sems,
+    blocks, slabs, rows_dp, lograte_ref, gain_ref, got_ref, sums_ref, base_ref, xt_ref, reach_ref,
+    low_ref, keep_ref, send_ref, part_ref,
 ):
-    groups = GROUPS
-    rows_in = blocks // groups * LANES
-    rows_out = rows_in // 2
     half = blocks * LANES // 2
-    sums_copy = pltpu.make_async_copy(sums_hbm, sums_ref, sum_sem.at[0])
-    sums_copy.start()
-    pairs = ((base_hbm, base_ref), (onward_hbm, onward_ref), (backward_hbm, backward_ref), (xt_hbm, xt_ref))
-    loads = []
-    for group in range(groups):
-        rows = slice(group * rows_in, (group + 1) * rows_in)
-        loads.append([pltpu.make_async_copy(a.at[rows], b.at[rows], sems.at[group, k]) for k, (a, b) in enumerate(pairs)])
-        for copy in loads[-1]:
-            copy.start()
     me = slab_index()
     mine = lax.axis_index("core")
     slope = -jnp.exp(lograte_ref[...])
@@ -199,7 +203,6 @@
     gain = gain_ref[...]
     early_d, early_g = gain * carry_early[0:blocks], carry_early[blocks:]
     late_d, late_g = gain * carry_late[0:blocks], carry_late[blocks:]
-    sums_copy.wait()
     c = [sums_ref[k, 0:blocks, :] for k in range(12)]
     rate_sum = c[0] + late_g * c[1] + early_d * c[2] + (late_g * early_d + early_g * late_d) * c[3]
     rate_sum = rate_sum + late_d * c[4] + early_g * c[5]
@@ -212,32 +215,23 @@
         part_ref[core, half : half + blocks, :] = proj_sum
         part_ref[core, half + 16 : half + 16 + blocks, :] = log_sum
 
-    stores = []
-    for group in range(groups):
-        for copy in loads[group]:
-            copy.wait()
-        for h in range(group * blocks // groups, (group + 1) * blocks // groups):
-            rows = slice(h * LANES, (h + 1) * LANES)
-            low = base_ref[rows, :] + onward_ref[rows, :] * early_g[h : h + 1, :] + backward_ref[rows, :] * late_g[h : h + 1, :]
-            low = low.astype(BF16)
-            low_ref[rows, :] = low
-            product = jnp.dot(xt_ref[rows, :], low, preferred_element_type=F32)
-            for k in range(LANES // 8):
-                piece, third = divmod(h * (LANES // 8) + k, 3)
-                dp, quarter = divmod(piece, 4)
-                core, zh = divmod(quarter, 2)
-                at = (dp * 2 + zh) * 24 + third * 8
-                part_ref[core, at : at + 8, :] = product[k * 8 : k * 8 + 8, :]
-        end = half + 32 if group == groups - 1 else (group + 1) * rows_out
-        rows = slice(group * rows_out, end)
-        stores.append(pltpu.make_async_copy(part_ref.at[1 - mine, rows], send_hbm.at[rows], out_sems.at[group, 0]))
-        stores.append(pltpu.make_async_copy(part_ref.at[mine, rows], keep_hbm.at[rows], out_sems.at[group, 1]))
-        rows = slice(group * rows_in, (group + 1) * rows_in)
-        stores.append(pltpu.make_async_copy(low_ref.at[rows], low_hbm.at[rows], out_sems.at[group, 2]))
-        for copy in stores[-3:]:
-            copy.start()
-    for copy in stores:
-        copy.wait()
+    enter, leave = gain * early_g, gain * late_g
+    from_start, to_end = reach_ref[0], reach_ref[1]
+    for h in range(blocks):
+        rows = slice(h * LANES, (h + 1) * LANES)
+        row = slice(h, h + 1)
+        low = base_ref[rows, :] + jnp.exp(slope[row] * from_start) * enter[row] + jnp.exp(slope[row] * to_end) * leave[row]
+        low = low.astype(BF16)
+        low_ref[rows, :] = low
+        product = jnp.dot(xt_ref[rows, :], low, preferred_element_type=F32)
+        for k in range(LANES // 8):
+            piece, third = divmod(h * (LANES // 8) + k, 3)
+            dp, quarter = divmod(piece, 4)
+            core, yl = divmod(quarter, 2)
+            at = (dp * 2 + yl) * 24 + third * 8
+            part_ref[core, at : at + 8, :] = product[k * 8 : k * 8 + 8, :]
+    keep_ref[...] = part_ref[mine]
+    send_ref[...] = part_ref[1 - mine]
 
 
 def pair_kernel(rows_dp, star_ref, keep_ref, sent_ref, out_ref, flat_ref):
@@ -254,8 +248,8 @@
     for dp in range(rows_dp):
         window = flat_ref[0:2, dp * share : dp * share + LANES]
         tile = jnp.concatenate([window, star], axis=0)
-        for zh in range(2):
-            piece = dp * 2 + zh
+        for yl in range(2):
+            piece = dp * 2 + yl
             rows = slice(piece * 24, piece * 24 + 24)
             out_ref[piece, 0:24, :] = keep_ref[rows, :] + sent_ref[other, rows, :]
             out_ref[piece, 24:27, :] = tile
@@ -273,7 +267,7 @@
 
 
 def piece_kernel(norm, got_ref, out_ref):
-    first = (lax.axis_index("core") * 2 + lax.axis_index("zh")) * 4
+    first = (lax.axis_index("core") * 2 + lax.axis_index("yl")) * 4
     total = got_ref[0, 0:24, :]
     logs = got_ref[0, 25:26, :]
     stars = [jnp.zeros((1, LANES), F32)] * 4
@@ -294,11 +288,12 @@
 def final_kernel(got_ref, weight_ref, star_ref, log_ref):
     share = star_ref.shape[1]
     for core in range(2):
-        for zh in range(2):
-            q = core * 2 + zh
-            total = got_ref[core, zh]
-            for y in range(1, got_ref.shape[1] // 2):
-                total = total + got_ref[core, y * 2 + zh]
+        for yl in range(2):
+            q = core * 2 + yl
+            total = None
+            for source in range(got_ref.shape[1]):
+                if source // 2 % 2 == yl:
+                    total = got_ref[core, source] if total is None else total + got_ref[core, source]
             weight_ref[q * 24 : q * 24 + 24, :] = total[0:24, :]
             star_ref[q * 4 : q * 4 + 4, :] = total[24:28, 0:share]
             if q == 0:
@@ -308,7 +303,7 @@
 def body(series, cotangent, step_times, seg_starts, star_of_row, block_weight, star_table, log_rate):
     _, slab_len, width = series.shape
     blocks = width // LANES
-    slabs = lax.axis_size(("y", "zh", "core"))
+    slabs = lax.axis_size(("yh", "yl", "zh", "core"))
     rows_dp = lax.axis_size(("x", "zl"))
     norm = float(1.0 / (rows_dp * slabs * slab_len) ** 0.5)
     chips = slabs // 2
@@ -329,42 +324,35 @@
         scratch_shapes=[pltpu.VMEM((2, 32, LANES), F32)]
         + [pltpu.SMEM(v.shape, v.dtype) for v in common[:2]]
         + [pltpu.VMEM(v.shape, v.dtype) for v in common[2:]]
-        + [pltpu.SemaphoreType.DMA((8,))],
+        + [pltpu.SemaphoreType.DMA((5,)), pltpu.SemaphoreType.DMA((GROUPS, 3))],
         compiler_params=big,
         name="slab_ends",
     )(*common)
-    got = lax.all_gather(lax.all_to_all(ends, ("y", "zh"), 0, 0), "core")
-    wide = shape((width, slab_len), F32)
-    base, onward, backward, xt, sums = pl.pallas_call(
+    got = lax.all_gather(lax.all_to_all(ends, ("yh", "yl", "zh"), 0, 0), "core")
+    base, xt, sums, reach = pl.pallas_call(
         functools.partial(local_kernel, blocks),
-        out_shape=[wide, wide, wide, shape((width, slab_len), BF16), shape((12, 16, LANES), F32)],
+        out_shape=[
+            shape((width, slab_len), F32),
+            shape((width, slab_len), BF16),
+            shape((12, 16, LANES), F32),
+            shape((2, slab_len, LANES), F32),
+        ],
         in_specs=[smem, smem] + [vmem] * 7,
-        out_specs=[vmem] * 5,
-        compiler_params=big,
+        out_specs=[vmem] * 4,
+        compiler_params=params,
         cost_estimate=pl.CostEstimate(flops=20_000_000, bytes_accessed=4_000_000, transcendentals=200_000),
         name="local_scans",
     )(*common, gain)
-    loaded = (base, onward, backward, xt)
     half_rows = width // 2 + 32
     low, keep, send = pl.pallas_call(
         functools.partial(combine_kernel, blocks, slabs, rows_dp),
         out_shape=[shape((width, slab_len), BF16)] + [shape((half_rows, LANES), F32)] * 2,
-        in_specs=[vmem] * 3 + [hbm] * 5,
-        out_specs=[hbm] * 3,
-        scratch_shapes=[
-            pltpu.VMEM((2, half_rows, LANES), F32),
-            pltpu.VMEM((width, slab_len), BF16),
-            pltpu.VMEM(sums.shape, F32),
-        ]
-        + [pltpu.VMEM(v.shape, v.dtype) for v in loaded]
-        + [
-            pltpu.SemaphoreType.DMA((1,)),
-            pltpu.SemaphoreType.DMA((GROUPS, len(loaded))),
-            pltpu.SemaphoreType.DMA((GROUPS, 3)),
-        ],
-        compiler_params=big,
+        in_specs=[vmem] * 7,
+        out_specs=[vmem] * 3,
+        scratch_shapes=[pltpu.VMEM((2, half_rows, LANES), F32)],
+        compiler_params=params,
         name="gradients",
-    )(log_blocks, gain, got, sums, *loaded)
+    )(log_blocks, gain, got, sums, base, xt, reach)
     sent = lax.all_gather(send, "core")
     pair = pl.pallas_call(
         functools.partial(pair_kernel, rows_dp),
@@ -384,7 +372,7 @@
         cost_estimate=pl.CostEstimate(flops=100_000_000, bytes_accessed=1_600_000, transcendentals=0),
         name="series_gradient",
     )(low, cotangent, block_weight)
-    pieces = lax.all_to_all(pair, ("x", "zl", "zh"), 0, 0)
+    pieces = lax.all_to_all(pair, ("x", "zl", "yl"), 0, 0)
     piece = pl.pallas_call(
         functools.partial(piece_kernel, norm),
         out_shape=jax.ShapeDtypeStruct((slabs // 2, 32, LANES), F32),
@@ -393,7 +381,7 @@
         compiler_params=params,
         name="sum_pieces",
     )(pieces)
-    spread = lax.all_to_all(piece, ("y", "zh"), 0, 0)
+    spread = lax.all_to_all(piece, ("yh", "yl", "zh"), 0, 0)
     both = lax.all_gather(spread, "core")
     share = width // rows_dp
     grad_weight, grad_star, grad_log = pl.pallas_call(
@@ -412,8 +400,8 @@
 
 
 def solution(mesh):
-    fine = Mesh(mesh.devices.reshape(4, 4, 8, 2, 2), ("x", "zl", "y", "zh", "core"))
-    dp, ctx = ("x", "zl"), ("y", "zh", "core")
+    fine = Mesh(mesh.devices.reshape(4, 4, 4, 2, 2, 2), ("x", "zl", "yh", "yl", "zh", "core"))
+    dp, ctx = ("x", "zl"), ("yh", "yl", "zh", "core")
     in_specs = (P(dp, ctx, None), P(dp, ctx, None), P(dp, ctx), P(dp, None), P(dp), P(), P(), P())
     out_specs = (P(dp, ctx, None), P(dp, None), P(None, dp), P(dp))
     return jax.shard_map(body, mesh=fine, in_specs=in_specs, out_specs=out_specs, check_vma=False)

time: 95.8 us -> 89.1 us (0.930)
  Pallas kernels: 15.6 us -> 9.82 us
  starting transfers between devices: 21.8 us -> 19.9 us
  waiting for transfers between devices: 21 us -> 22.9 us
  blocking collectives: 34.9 us -> 33.9 us
    pallas_call x1, Pallas kernels: 4.69 us -> 0.81 us  [body(): pl.pallas_call(functools.partial(combine_kernel, blocks, slabs, rows_dp),...]
    pallas_call x1, Pallas kernels: 4.88 us -> 2.64 us  [body(): pl.pallas_call(functools.partial(local_kernel, blocks), out_shape=[shape(...]
    all_to_all x2, waiting for transfers between devices: 21 us -> 22.9 us  [the longest x1 11.9 us: body(): spread = lax.all_to_all(piece, ('yh', 'yl', 'zh'), 0, 0)]
    all_to_all x2, starting transfers between devices: 21.8 us -> 19.9 us  [the longest x1 16.3 us: body(): got = lax.all_gather(lax.all_to_all(ends, ('yh', 'yl', 'zh'), 0, 0), 'core')]
  transfers between devices with their start and end apart: 2 -> 2, of which waited for: 2 -> 2; matrix products, arithmetic and copies ran while one was open for 1% -> 0% of each run, Pallas kernels for 7% -> 5%
where the time goes in v4:
time: 89.1 us; the launch traced here: 88.6 us
  blocking collectives  33.9 us (38%)
  waiting for transfers between devices  22.9 us (26%)
  starting transfers between devices  19.9 us (22%)
  Pallas kernels  9.82 us (11%)
  between operations  1.43 us (2%)
    all_to_all x1, blocking collectives, body(): pieces = lax.all_to_all(pair, ('x', 'zl', 'yl'), 0, 0)  22 us
    all_to_all x1, starting transfers between devices, body(): got = lax.all_gather(lax.all_to_all(ends, ('yh', 'yl', 'zh'), 0, 0), 'core')  16.3 us
    all_to_all x1, waiting for transfers between devices, body(): spread = lax.all_to_all(piece, ('yh', 'yl', 'zh'), 0, 0)  11.9 us
    all_to_all x1, waiting for transfers between devices, body(): got = lax.all_gather(lax.all_to_all(ends, ('yh', 'yl', 'zh'), 0, 0), 'core')  11.1 us
    all_gather x1, blocking collectives, body(): both = lax.all_gather(spread, 'core')  5.19 us
    all_gather x1, blocking collectives, body(): got = lax.all_gather(lax.all_to_all(ends, ('yh', 'yl', 'zh'), 0, 0), 'core')  4.35 us
    all_to_all x1, starting transfers between devices, body(): spread = lax.all_to_all(piece, ('yh', 'yl', 'zh'), 0, 0)  3.54 us
    pallas_call x1, Pallas kernels, body(): pl.pallas_call(functools.partial(ends_kernel, blocks, chips), out_shape=s...  3.03 us
  transfers between devices with their start and end apart: 2, of which 2 were waited for; matrix products, arithmetic and copies ran while one was open for 0% of the time, Pallas kernels for 5%

profile of v4, /device:TPU:1, one launch (start us, length us, event | category | flops | bytes accessed | tf_op | source)
XLA Modules:
  0.0 88.6 jit_solution(1447604886338243867)
XLA Ops:
  1.3 0.0 copy-start.1
  1.3 0.0 copy-start.2
  1.3 3.0 %slab_ends.1 = f32[16,32,128]{2,1,0:T(8,128)} custom-call(s32[1,4]{1,0:T(1,128)} %starts_ref.1, s32[1]{0:T(128)S(6)} %copy.12.star_hbm.star_ref, f32[1,128]{1,0:T(1,128)} %times_ref.1, bf16[1,128,1536]{2,1,0:T(8,128)(2,1)} %series_ref.1, bf16[1,128,1536]{2,1,0:T(8,128)(2,1)} %cot_ref.3, bf16[1536,128]{1,0:T(8,128)(2,1)} %w_ref.3, f32[16,1536]{1,0:T(8,128)} %table_ref.1, ...), custom_call_target="tpu_custom_call" | custom-call | tf_op jit(solution)/shard_map/slab_ends/pallas_call | solution.py:319
  4.3 0.0 copy-start.4
  4.3 0.0 copy-start
  4.4 0.0 copy-start.3
  4.4 16.3 %all-to-all-start = ((f32[16,32,128]{2,1,0:T(8,128)}), f32[16,32,128]{2,1,0:T(8,128)S(1)}, u32[]{:S(2)}, u32[]{:S(2)}) async-start(f32[16,32,128]{2,1,0:T(8,128)} %slab_ends.1), calls=%async_computation | async-start | bytes 524288 | tf_op jit(solution)/shard_map/all_to_all | solution.py:331
  20.7 0.0 copy-done.4
  20.7 0.0 copy-start.5
  20.7 0.0 copy-start.6
  20.8 0.0 copy-done.1
  20.8 0.0 copy-done.2
  20.8 0.0 copy-done
  20.8 0.0 copy-done.3
  20.8 0.6 copy-done.5
  21.4 0.0 copy-done.6
  21.4 2.6 %local_scans.1 = (f32[1536,128]{1,0:T(8,128)S(1)}, bf16[1536,128]{1,0:T(8,128)(2,1)S(1)}, f32[12,16,128]{2,1,0:T(8,128)S(1)}, f32[2,128,128]{2,1,0:T(8,128)S(1)}) custom-call(s32[1,4]{1,0:T(1,128)S(1)} %copy-done.5, s32[1]{0:T(128)S(6)} %copy.12.star_hbm.star_ref, f32[1,128]{1,0:T(1,128)S(1)} %copy-done.6, bf16[1,128,1536]{2,1,0:T(8,128)(2,1)S(1)} %copy-done.2, ...), custom_call_target="tpu_custom_call" | custom-call | flops 20000000 | bytes 4000000 | tf_op jit(solution)/shard_map/local_scans/pallas_call | solution.py:332
  24.1 11.1 %all-to-all-done = f32[16,32,128]{2,1,0:T(8,128)S(1)} async-done(((f32[16,32,128]{2,1,0:T(8,128)}), f32[16,32,128]{2,1,0:T(8,128)S(1)}, u32[]{:S(2)}, u32[]{:S(2)}) %all-to-all-start) | async-done | bytes 262176 | tf_op jit(solution)/shard_map/all_to_all | solution.py:331
  35.1 4.4 %all-gather = f32[32,32,128]{2,1,0:T(8,128)S(1)} all-gather(f32[16,32,128]{2,1,0:T(8,128)S(1)} %all-to-all-done), channel_id=2, replica_groups=mesh['x'=4,'zl'=4,'yh'=4,'yl'=2,'zh'=2,'core'=2] {'core'}, dimensions={0}, use_global_device_ids=true | all-gather | bytes 786432 | tf_op jit(solution)/shard_map/all_gather | solution.py:331
  39.5 0.8 gradients.1
  40.3 2.4 %all-gather.1 = f32[1600,128]{1,0:T(8,128)S(1)} all-gather(f32[800,128]{1,0:T(8,128)S(1)} %get-tuple-element.20), channel_id=3, replica_groups=mesh['x'=4,'zl'=4,'yh'=4,'yl'=2,'zh'=2,'core'=2] {'core'}, dimensions={0}, use_global_device_ids=true | all-gather | bytes 1228800 | tf_op jit(solution)/shard_map/all_gather | solution.py:356
  42.7 0.1 pair_sum.1
  42.8 22.0 %all_to_all.15.got_ref = f32[32,27,128]{2,1,0:T(8,128)S(1)} all-to-all(f32[32,27,128]{2,1,0:T(8,128)S(1)} %pair_sum.1), channel_id=1, replica_groups=mesh['x'=4,'zl'=4,'yh'=4,'yl'=2,'zh'=2,'core'=2] {'x','zl','yl'}, dimensions={0} | all-to-all | bytes 884736 | tf_op jit(solution)/shard_map/all_to_all | solution.py:375
  64.8 0.8 sum_pieces.1
  65.6 3.5 %all-to-all-start.2 = ((f32[16,32,128]{2,1,0:T(8,128)}), f32[16,32,128]{2,1,0:T(8,128)S(1)}, u32[]{:S(2)}, u32[]{:S(2)}) async-start(f32[16,32,128]{2,1,0:T(8,128)} %sum_pieces.1), calls=%async_computation.2 | async-start | bytes 524288 | tf_op jit(solution)/shard_map/all_to_all | solution.py:384
  69.2 1.8 %series_gradient.1 = bf16[1,128,1536]{2,1,0:T(8,128)(2,1)} custom-call(bf16[1536,128]{1,0:T(8,128)(2,1)S(1)} %get-tuple-element.18.low_ref, bf16[1,128,1536]{2,1,0:T(8,128)(2,1)S(1)} %copy-done, bf16[1536,128]{1,0:T(8,128)(2,1)S(1)} %copy-done.1), custom_call_target="tpu_custom_call" | custom-call | flops 100000000 | bytes 1600000 | tf_op jit(solution)/shard_map/series_gradient/pallas_call | solution.py:366
  70.9 11.9 %all-to-all-done.2 = f32[16,32,128]{2,1,0:T(8,128)S(1)} async-done(((f32[16,32,128]{2,1,0:T(8,128)}), f32[16,32,128]{2,1,0:T(8,128)S(1)}, u32[]{:S(2)}, u32[]{:S(2)}) %all-to-all-start.2) | async-done | bytes 262176 | tf_op jit(solution)/shard_map/all_to_all | solution.py:384
  82.8 5.2 %all-gather.2 = f32[32,32,128]{2,1,0:T(8,128)S(1)} all-gather(f32[16,32,128]{2,1,0:T(8,128)S(1)} %all-to-all-done.2), channel_id=4, replica_groups=mesh['x'=4,'zl'=4,'yh'=4,'yl'=2,'zh'=2,'core'=2] {'core'}, dimensions={0}, use_global_device_ids=true | all-gather | bytes 786432 | tf_op jit(solution)/shard_map/all_gather | solution.py:385
  88.0 0.7 outputs.1
  (1 shorter events, 0.0 us)
Async XLA Ops:
  1.3 19.5 %copy-start.1 = (bf16[1536,128]{1,0:T(8,128)(2,1)S(1)}, bf16[1536,128]{1,0:T(8,128)(2,1)}, u32[]{:S(2)}) copy-start(bf16[1536,128]{1,0:T(8,128)(2,1)} %w_ref.3) | copy-start | bytes 1179652
  1.3 19.5 %copy-start.2 = (bf16[1,128,1536]{2,1,0:T(8,128)(2,1)S(1)}, bf16[1,128,1536]{2,1,0:T(8,128)(2,1)}, u32[]{:S(2)}) copy-start(bf16[1,128,1536]{2,1,0:T(8,128)(2,1)} %series_ref.1) | copy-start | bytes 1179652
  4.3 16.4 %copy-start.4 = (f32[1536]{0:T(1024)S(1)}, f32[1536]{0:T(1024)}, u32[]{:S(2)}) copy-start(f32[1536]{0:T(1024)} %param.15) | copy-start | bytes 18436
  4.3 16.5 %copy-start = (bf16[1,128,1536]{2,1,0:T(8,128)(2,1)S(1)}, bf16[1,128,1536]{2,1,0:T(8,128)(2,1)}, u32[]{:S(2)}) copy-start(bf16[1,128,1536]{2,1,0:T(8,128)(2,1)} %cot_ref.3) | copy-start | bytes 1179652
  4.4 16.5 %copy-start.3 = (f32[16,1536]{1,0:T(8,128)S(1)}, f32[16,1536]{1,0:T(8,128)}, u32[]{:S(2)}) copy-start(f32[16,1536]{1,0:T(8,128)} %table_ref.1) | copy-start | bytes 294916
  4.4 30.8 %all-to-all-start = ((f32[16,32,128]{2,1,0:T(8,128)}), f32[16,32,128]{2,1,0:T(8,128)S(1)}, u32[]{:S(2)}, u32[]{:S(2)}) async-start(f32[16,32,128]{2,1,0:T(8,128)} %slab_ends.1), calls=%async_computation | async-start | bytes 524288 | tf_op jit(solution)/shard_map/all_to_all | solution.py:331
  20.7 0.7 copy-start.5
  20.7 0.7 copy-start.6
  65.6 17.2 %all-to-all-start.2 = ((f32[16,32,128]{2,1,0:T(8,128)}), f32[16,32,128]{2,1,0:T(8,128)S(1)}, u32[]{:S(2)}, u32[]{:S(2)}) async-start(f32[16,32,128]{2,1,0:T(8,128)} %sum_pieces.1), calls=%async_computation.2 | async-start | bytes 524288 | tf_op jit(solution)/shard_map/all_to_all | solution.py:384

commit v5 on v4

--- a/solution.py
+++ b/solution.py
@@ -12,6 +12,7 @@
 STEPS = SLAB // CHUNKS
 FAR = 1e9
 GROUPS = 4
+PIECE = 26
 F32 = jnp.float32
 BF16 = jnp.bfloat16
 
@@ -244,15 +245,16 @@
         table = keep_ref[half + 16 * k : half + 16 * k + 16, :] + sent_ref[other, half + 16 * k : half + 16 * k + 16, :]
         for h in range(width // LANES):
             flat_ref[k : k + 1, h * LANES : (h + 1) * LANES] = table[h : h + 1, :]
-    star = jnp.broadcast_to(star_ref[0].astype(F32), (1, LANES))
+    lane = lax.broadcasted_iota(jnp.int32, (2, LANES), 1)
+    star = jnp.broadcast_to(star_ref[0].astype(F32), (2, LANES))
     for dp in range(rows_dp):
-        window = flat_ref[0:2, dp * share : dp * share + LANES]
-        tile = jnp.concatenate([window, star], axis=0)
+        tile = jnp.where(lane < share, flat_ref[0:2, dp * share : dp * share + LANES], star)
         for yl in range(2):
             piece = dp * 2 + yl
             rows = slice(piece * 24, piece * 24 + 24)
-            out_ref[piece, 0:24, :] = keep_ref[rows, :] + sent_ref[other, rows, :]
-            out_ref[piece, 24:27, :] = tile
+            at = piece * PIECE
+            out_ref[at : at + 24, :] = keep_ref[rows, :] + sent_ref[other, rows, :]
+            out_ref[at + 24 : at + 26, :] = tile
 
 
 def series_kernel(blocks, low_ref, cot_ref, w_ref, dx_ref):
@@ -266,18 +268,17 @@
         dx_ref[0, :, cols] = (cot_ref[0, :, cols].astype(F32) + back).astype(BF16)
 
 
-def piece_kernel(norm, got_ref, out_ref):
+def piece_kernel(norm, share, got_ref, out_ref):
     first = (lax.axis_index("core") * 2 + lax.axis_index("yl")) * 4
-    total = got_ref[0, 0:24, :]
-    logs = got_ref[0, 25:26, :]
-    stars = [jnp.zeros((1, LANES), F32)] * 4
-    for s in range(got_ref.shape[0]):
-        if s:
-            total = total + got_ref[s, 0:24, :]
-            logs = logs + got_ref[s, 25:26, :]
-        for k in range(4):
-            hit = got_ref[s, 26:27, :] == (first + k).astype(F32)
-            stars[k] = stars[k] + jnp.where(hit, got_ref[s, 24:25, :], 0.0)
+    sources = got_ref.shape[0] // PIECE
+    total = got_ref[0:24, :]
+    for s in range(1, sources):
+        total = total + got_ref[s * PIECE : s * PIECE + 24, :]
+    terms = got_ref[pl.ds(24, sources, stride=PIECE), :]
+    logs = jnp.sum(got_ref[pl.ds(25, sources, stride=PIECE), :], axis=0, keepdims=True)
+    star = jnp.broadcast_to(terms[:, share : share + 1], terms.shape)
+    hits = [star == (first + k).astype(F32) for k in range(4)]
+    stars = [jnp.sum(jnp.where(hit, terms, 0.0), axis=0, keepdims=True) for hit in hits]
     total = total * norm
     tail = jnp.concatenate(stars + [logs] + [jnp.zeros((3, LANES), F32)], axis=0) * norm
     for d in range(out_ref.shape[0]):
@@ -356,7 +357,7 @@
     sent = lax.all_gather(send, "core")
     pair = pl.pallas_call(
         functools.partial(pair_kernel, rows_dp),
-        out_shape=shape((rows_dp * 2, 27, LANES), F32),
+        out_shape=shape((rows_dp * 2 * PIECE, LANES), F32),
         in_specs=[smem, vmem, vmem],
         out_specs=vmem,
         scratch_shapes=[pltpu.VMEM((8, width + LANES), F32)],
@@ -372,9 +373,10 @@
         cost_estimate=pl.CostEstimate(flops=100_000_000, bytes_accessed=1_600_000, transcendentals=0),
         name="series_gradient",
     )(low, cotangent, block_weight)
-    pieces = lax.all_to_all(pair, ("x", "zl", "yl"), 0, 0)
+    pair = pair.reshape(rows_dp * 2, 1, PIECE * LANES)
+    pieces = lax.all_to_all(pair, ("x", "zl", "yl"), 0, 0).reshape(rows_dp * 2 * PIECE, LANES)
     piece = pl.pallas_call(
-        functools.partial(piece_kernel, norm),
+        functools.partial(piece_kernel, norm, width // rows_dp),
         out_shape=jax.ShapeDtypeStruct((slabs // 2, 32, LANES), F32),
         in_specs=[vmem],
         out_specs=vmem,

time: 89.1 us -> 86.8 us (0.974)
  blocking collectives: 33.9 us -> 31.4 us
    all_to_all x1, blocking collectives: 22 us -> 18.8 us  [body(): lax.all_to_all(pair, ('x', 'zl', 'yl'), 0, 0)]
where the time goes in v5:
time: 86.8 us; the launch traced here: 86.4 us
  blocking collectives  31.4 us (36%)
  waiting for transfers between devices  23 us (26%)
  starting transfers between devices  20.1 us (23%)
  Pallas kernels  9.81 us (11%)
  between operations  1.43 us (2%)
    all_to_all x1, blocking collectives, body(): lax.all_to_all(pair, ('x', 'zl', 'yl'), 0, 0)  18.8 us
    all_to_all x1, starting transfers between devices, body(): got = lax.all_gather(lax.all_to_all(ends, ('yh', 'yl', 'zh'), 0, 0), 'core')  16.3 us
    all_to_all x1, waiting for transfers between devices, body(): spread = lax.all_to_all(piece, ('yh', 'yl', 'zh'), 0, 0)  11.9 us
    all_to_all x1, waiting for transfers between devices, body(): got = lax.all_gather(lax.all_to_all(ends, ('yh', 'yl', 'zh'), 0, 0), 'core')  11.1 us
    all_gather x1, blocking collectives, body(): both = lax.all_gather(spread, 'core')  5.87 us
    all_gather x1, blocking collectives, body(): got = lax.all_gather(lax.all_to_all(ends, ('yh', 'yl', 'zh'), 0, 0), 'core')  4.35 us
    all_to_all x1, starting transfers between devices, body(): spread = lax.all_to_all(piece, ('yh', 'yl', 'zh'), 0, 0)  3.8 us
    pallas_call x1, Pallas kernels, body(): pl.pallas_call(functools.partial(ends_kernel, blocks, chips), out_shape=s...  3.03 us
  transfers between devices with their start and end apart: 2, of which 2 were waited for; matrix products, arithmetic and copies ran while one was open for 0% of the time, Pallas kernels for 5%

profile of v5, /device:TPU:1, one launch (start us, length us, event | category | flops | bytes accessed | tf_op | source)
XLA Modules:
  0.0 86.4 jit_solution(16255265256574123793)
XLA Ops:
  1.3 0.0 copy-start.1
  1.3 0.0 copy-start.2
  1.3 3.0 %slab_ends.1 = f32[16,32,128]{2,1,0:T(8,128)} custom-call(s32[1,4]{1,0:T(1,128)} %starts_ref.1, s32[1]{0:T(128)S(6)} %copy.13.star_hbm.star_ref, f32[1,128]{1,0:T(1,128)} %times_ref.1, bf16[1,128,1536]{2,1,0:T(8,128)(2,1)} %series_ref.1, bf16[1,128,1536]{2,1,0:T(8,128)(2,1)} %cot_ref.3, bf16[1536,128]{1,0:T(8,128)(2,1)} %w_ref.3, f32[16,1536]{1,0:T(8,128)} %table_ref.1, ...), custom_call_target="tpu_custom_call" | custom-call | tf_op jit(solution)/shard_map/slab_ends/pallas_call | solution.py:320
  4.3 0.0 copy-start.4
  4.3 0.0 copy-start
  4.4 0.0 copy-start.3
  4.4 16.3 %all-to-all-start = ((f32[16,32,128]{2,1,0:T(8,128)}), f32[16,32,128]{2,1,0:T(8,128)S(1)}, u32[]{:S(2)}, u32[]{:S(2)}) async-start(f32[16,32,128]{2,1,0:T(8,128)} %slab_ends.1), calls=%async_computation | async-start | bytes 524288 | tf_op jit(solution)/shard_map/all_to_all | solution.py:332
  20.7 0.0 copy-done.4
  20.7 0.0 copy-start.5
  20.7 0.0 copy-start.6
  20.8 0.0 copy-done.1
  20.8 0.0 copy-done.2
  20.8 0.0 copy-done
  20.8 0.0 copy-done.3
  20.8 0.6 copy-done.5
  21.4 0.0 copy-done.6
  21.4 2.6 %local_scans.1 = (f32[1536,128]{1,0:T(8,128)S(1)}, bf16[1536,128]{1,0:T(8,128)(2,1)S(1)}, f32[12,16,128]{2,1,0:T(8,128)S(1)}, f32[2,128,128]{2,1,0:T(8,128)S(1)}) custom-call(s32[1,4]{1,0:T(1,128)S(1)} %copy-done.5, s32[1]{0:T(128)S(6)} %copy.13.star_hbm.star_ref, f32[1,128]{1,0:T(1,128)S(1)} %copy-done.6, bf16[1,128,1536]{2,1,0:T(8,128)(2,1)S(1)} %copy-done.2, ...), custom_call_target="tpu_custom_call" | custom-call | flops 20000000 | bytes 4000000 | tf_op jit(solution)/shard_map/local_scans/pallas_call | solution.py:333
  24.1 11.1 %all-to-all-done = f32[16,32,128]{2,1,0:T(8,128)S(1)} async-done(((f32[16,32,128]{2,1,0:T(8,128)}), f32[16,32,128]{2,1,0:T(8,128)S(1)}, u32[]{:S(2)}, u32[]{:S(2)}) %all-to-all-start) | async-done | bytes 262176 | tf_op jit(solution)/shard_map/all_to_all | solution.py:332
  35.1 4.4 %all-gather = f32[32,32,128]{2,1,0:T(8,128)S(1)} all-gather(f32[16,32,128]{2,1,0:T(8,128)S(1)} %all-to-all-done), channel_id=2, replica_groups=mesh['x'=4,'zl'=4,'yh'=4,'yl'=2,'zh'=2,'core'=2] {'core'}, dimensions={0}, use_global_device_ids=true | all-gather | bytes 786432 | tf_op jit(solution)/shard_map/all_gather | solution.py:332
  39.5 0.8 gradients.1
  40.3 2.4 %all-gather.1 = f32[1600,128]{1,0:T(8,128)S(1)} all-gather(f32[800,128]{1,0:T(8,128)S(1)} %get-tuple-element.20), channel_id=3, replica_groups=mesh['x'=4,'zl'=4,'yh'=4,'yl'=2,'zh'=2,'core'=2] {'core'}, dimensions={0}, use_global_device_ids=true | all-gather | bytes 1228800 | tf_op jit(solution)/shard_map/all_gather | solution.py:357
  42.7 0.1 pair_sum.1
  42.8 18.8 %all_to_all.15 = f32[32,1,3328]{2,1,0:T(1,128)S(1)} all-to-all(f32[32,1,3328]{2,1,0:T(1,128)S(1)} %bitcast.11), channel_id=1, replica_groups=mesh['x'=4,'zl'=4,'yh'=4,'yl'=2,'zh'=2,'core'=2] {'x','zl','yl'}, dimensions={0} | all-to-all | bytes 851968 | tf_op jit(solution)/shard_map/all_to_all | solution.py:377
  61.6 0.8 sum_pieces.1
  62.4 3.8 %all-to-all-start.2 = ((f32[16,32,128]{2,1,0:T(8,128)}), f32[16,32,128]{2,1,0:T(8,128)S(1)}, u32[]{:S(2)}, u32[]{:S(2)}) async-start(f32[16,32,128]{2,1,0:T(8,128)} %sum_pieces.1), calls=%async_computation.2 | async-start | bytes 524288 | tf_op jit(solution)/shard_map/all_to_all | solution.py:386
  66.2 1.8 %series_gradient.1 = bf16[1,128,1536]{2,1,0:T(8,128)(2,1)} custom-call(bf16[1536,128]{1,0:T(8,128)(2,1)S(1)} %get-tuple-element.18.low_ref, bf16[1,128,1536]{2,1,0:T(8,128)(2,1)S(1)} %copy-done, bf16[1536,128]{1,0:T(8,128)(2,1)S(1)} %copy-done.1), custom_call_target="tpu_custom_call" | custom-call | flops 100000000 | bytes 1600000 | tf_op jit(solution)/shard_map/series_gradient/pallas_call | solution.py:367
  68.0 11.9 %all-to-all-done.2 = f32[16,32,128]{2,1,0:T(8,128)S(1)} async-done(((f32[16,32,128]{2,1,0:T(8,128)}), f32[16,32,128]{2,1,0:T(8,128)S(1)}, u32[]{:S(2)}, u32[]{:S(2)}) %all-to-all-start.2) | async-done | bytes 262176 | tf_op jit(solution)/shard_map/all_to_all | solution.py:386
  79.9 5.9 %all-gather.2 = f32[32,32,128]{2,1,0:T(8,128)S(1)} all-gather(f32[16,32,128]{2,1,0:T(8,128)S(1)} %all-to-all-done.2), channel_id=4, replica_groups=mesh['x'=4,'zl'=4,'yh'=4,'yl'=2,'zh'=2,'core'=2] {'core'}, dimensions={0}, use_global_device_ids=true | all-gather | bytes 786432 | tf_op jit(solution)/shard_map/all_gather | solution.py:387
  85.8 0.7 outputs.1
  (1 shorter events, 0.0 us)
Async XLA Ops:
  1.3 19.5 %copy-start.1 = (bf16[1536,128]{1,0:T(8,128)(2,1)S(1)}, bf16[1536,128]{1,0:T(8,128)(2,1)}, u32[]{:S(2)}) copy-start(bf16[1536,128]{1,0:T(8,128)(2,1)} %w_ref.3) | copy-start | bytes 1179652
  1.3 19.5 %copy-start.2 = (bf16[1,128,1536]{2,1,0:T(8,128)(2,1)S(1)}, bf16[1,128,1536]{2,1,0:T(8,128)(2,1)}, u32[]{:S(2)}) copy-start(bf16[1,128,1536]{2,1,0:T(8,128)(2,1)} %series_ref.1) | copy-start | bytes 1179652
  4.3 16.4 %copy-start.4 = (f32[1536]{0:T(1024)S(1)}, f32[1536]{0:T(1024)}, u32[]{:S(2)}) copy-start(f32[1536]{0:T(1024)} %param.15) | copy-start | bytes 18436
  4.3 16.5 %copy-start = (bf16[1,128,1536]{2,1,0:T(8,128)(2,1)S(1)}, bf16[1,128,1536]{2,1,0:T(8,128)(2,1)}, u32[]{:S(2)}) copy-start(bf16[1,128,1536]{2,1,0:T(8,128)(2,1)} %cot_ref.3) | copy-start | bytes 1179652
  4.4 16.5 %copy-start.3 = (f32[16,1536]{1,0:T(8,128)S(1)}, f32[16,1536]{1,0:T(8,128)}, u32[]{:S(2)}) copy-start(f32[16,1536]{1,0:T(8,128)} %table_ref.1) | copy-start | bytes 294916
  4.4 30.8 %all-to-all-start = ((f32[16,32,128]{2,1,0:T(8,128)}), f32[16,32,128]{2,1,0:T(8,128)S(1)}, u32[]{:S(2)}, u32[]{:S(2)}) async-start(f32[16,32,128]{2,1,0:T(8,128)} %slab_ends.1), calls=%async_computation | async-start | bytes 524288 | tf_op jit(solution)/shard_map/all_to_all | solution.py:332
  20.7 0.7 copy-start.5
  20.7 0.7 copy-start.6
  62.4 17.5 %all-to-all-start.2 = ((f32[16,32,128]{2,1,0:T(8,128)}), f32[16,32,128]{2,1,0:T(8,128)S(1)}, u32[]{:S(2)}, u32[]{:S(2)}) async-start(f32[16,32,128]{2,1,0:T(8,128)} %sum_pieces.1), calls=%async_computation.2 | async-start | bytes 524288 | tf_op jit(solution)/shard_map/all_to_all | solution.py:386

commit v6 on v5

--- a/solution.py
+++ b/solution.py
@@ -11,7 +11,8 @@
 CHUNKS = 8
 STEPS = SLAB // CHUNKS
 FAR = 1e9
-GROUPS = 4
+CARRY = 25
+SHARE = 29
 PIECE = 26
 F32 = jnp.float32
 BF16 = jnp.bfloat16
@@ -32,22 +33,14 @@
 
 def ends_kernel(
     blocks, chips, starts_hbm, star_hbm, times_hbm, series_hbm, cot_hbm, w_hbm, table_hbm, lograte_hbm,
-    out_ref, ends_ref, starts_ref, star_ref, times_ref, series_ref, cot_ref, w_ref, table_ref, lograte_ref, sems, group_sems,
+    out_ref, ends_ref, starts_ref, star_ref, times_ref, series_ref, cot_ref, w_ref, table_ref, lograte_ref, sems, load_sems,
 ):
     sources = (starts_hbm, star_hbm, times_hbm, table_hbm, lograte_hbm)
     targets = (starts_ref, star_ref, times_ref, table_ref, lograte_ref)
     copies = [pltpu.make_async_copy(a, b, sems.at[k]) for k, (a, b) in enumerate(zip(sources, targets))]
-    span = blocks // GROUPS * LANES
-    loads = []
-    for group in range(GROUPS):
-        part = slice(group * span, (group + 1) * span)
-        views = (
-            (series_hbm.at[:, :, part], series_ref.at[:, :, part]),
-            (w_hbm.at[part], w_ref.at[part]),
-            (cot_hbm.at[:, :, part], cot_ref.at[:, :, part]),
-        )
-        loads.append([pltpu.make_async_copy(a, b, group_sems.at[group, k]) for k, (a, b) in enumerate(views)])
-    for copy in copies + sum(loads, []):
+    sources, targets = (series_hbm, w_hbm, cot_hbm), (series_ref, w_ref, cot_ref)
+    loads = [pltpu.make_async_copy(a, b, load_sems.at[k]) for k, (a, b) in enumerate(zip(sources, targets))]
+    for copy in copies[:3] + loads + copies[3:]:
         copy.start()
     core = lax.axis_index("core")
     me = slab_index()
@@ -62,13 +55,10 @@
     to_end = jnp.broadcast_to(to_end, (SLAB, LANES))
     from_start = jnp.broadcast_to(from_start, (SLAB, LANES))
     total = jnp.sum(elapsed, axis=1, keepdims=True)
-    for copy in copies[3:]:
+    for copy in copies[3:] + loads:
         copy.wait()
     bias = table_ref[pl.ds(star_ref[0], 1), :]
     for h in range(blocks):
-        if h % (blocks // GROUPS) == 0:
-            for copy in loads[h // (blocks // GROUPS)]:
-                copy.wait()
         cols = slice(h * LANES, (h + 1) * LANES)
         proj = jnp.dot(series_ref[0, :, cols], w_ref[cols, :], preferred_element_type=F32) + bias[:, cols]
         grad = cot_ref[0, :, cols].astype(F32)
@@ -83,7 +73,7 @@
     ends_ref[0, 2 * blocks : 2 * blocks + 8, :] = tail
     ends_ref[1, 2 * blocks : 2 * blocks + 8, :] = tail
     for chip in range(chips):
-        out_ref[chip] = ends_ref[jnp.where(2 * chip + 1 - core > me, 0, 1)]
+        out_ref[chip * CARRY : (chip + 1) * CARRY, :] = ends_ref[jnp.where(2 * chip + 1 - core > me, 0, 1), 0:CARRY, :]
 
 
 def shift(x, k, fill, sublane):
@@ -187,7 +177,8 @@
     mine = lax.axis_index("core")
     slope = -jnp.exp(lograte_ref[...])
     slope2 = jnp.concatenate([slope, slope], axis=0)
-    took = lambda s: got_ref[s % 2, s // 2, 2 * blocks : 2 * blocks + 1, :]
+    start = lambda s: (s % 2 * (slabs // 2) + s // 2) * CARRY
+    took = lambda s: got_ref[start(s) + 2 * blocks : start(s) + 2 * blocks + 1, :]
     between = [None] * slabs
     run = jnp.zeros((1, LANES), F32)
     for s in reversed(range(slabs)):
@@ -197,7 +188,7 @@
     carry_early = jnp.zeros((2 * blocks, LANES), F32)
     carry_late = jnp.zeros((2 * blocks, LANES), F32)
     for s in range(slabs):
-        x = jnp.exp(slope2 * jnp.where(s < me, between[s], run)) * got_ref[s % 2, s // 2, 0 : 2 * blocks, :]
+        x = jnp.exp(slope2 * jnp.where(s < me, between[s], run)) * got_ref[start(s) : start(s) + 2 * blocks, :]
         carry_early = carry_early + jnp.where(s < me, x, 0.0)
         carry_late = carry_late + jnp.where(s > me, x, 0.0)
         run = jnp.where(s > me, run + took(s), 0.0)
@@ -280,21 +271,22 @@
     hits = [star == (first + k).astype(F32) for k in range(4)]
     stars = [jnp.sum(jnp.where(hit, terms, 0.0), axis=0, keepdims=True) for hit in hits]
     total = total * norm
-    tail = jnp.concatenate(stars + [logs] + [jnp.zeros((3, LANES), F32)], axis=0) * norm
-    for d in range(out_ref.shape[0]):
-        out_ref[d, 0:24, :] = total
-        out_ref[d, 24:32, :] = tail
+    tail = jnp.concatenate(stars + [logs], axis=0) * norm
+    for d in range(out_ref.shape[0] // SHARE):
+        out_ref[d * SHARE : d * SHARE + 24, :] = total
+        out_ref[d * SHARE + 24 : d * SHARE + 29, :] = tail
 
 
 def final_kernel(got_ref, weight_ref, star_ref, log_ref):
     share = star_ref.shape[1]
+    chips = got_ref.shape[0] // SHARE // 2
     for core in range(2):
         for yl in range(2):
             q = core * 2 + yl
-            total = None
-            for source in range(got_ref.shape[1]):
-                if source // 2 % 2 == yl:
-                    total = got_ref[core, source] if total is None else total + got_ref[core, source]
+            parts = [(core * chips + chip) * SHARE for chip in range(chips) if chip // 2 % 2 == yl]
+            total = got_ref[parts[0] : parts[0] + SHARE, :]
+            for at in parts[1:]:
+                total = total + got_ref[at : at + SHARE, :]
             weight_ref[q * 24 : q * 24 + 24, :] = total[0:24, :]
             star_ref[q * 4 : q * 4 + 4, :] = total[24:28, 0:share]
             if q == 0:
@@ -319,17 +311,18 @@
     common = (seg_starts, star_of_row, step_times, series, cotangent, block_weight, star_table, log_blocks)
     ends = pl.pallas_call(
         functools.partial(ends_kernel, blocks, chips),
-        out_shape=shape((chips, 32, LANES), F32),
+        out_shape=shape((chips * CARRY, LANES), F32),
         in_specs=[hbm] * 8,
         out_specs=vmem,
         scratch_shapes=[pltpu.VMEM((2, 32, LANES), F32)]
         + [pltpu.SMEM(v.shape, v.dtype) for v in common[:2]]
         + [pltpu.VMEM(v.shape, v.dtype) for v in common[2:]]
-        + [pltpu.SemaphoreType.DMA((5,)), pltpu.SemaphoreType.DMA((GROUPS, 3))],
+        + [pltpu.SemaphoreType.DMA((5,)), pltpu.SemaphoreType.DMA((3,))],
         compiler_params=big,
         name="slab_ends",
     )(*common)
-    got = lax.all_gather(lax.all_to_all(ends, ("yh", "yl", "zh"), 0, 0), "core")
+    ends = ends.reshape(chips, 1, CARRY * LANES)
+    got = lax.all_gather(lax.all_to_all(ends, ("yh", "yl", "zh"), 0, 0), "core").reshape(slabs * CARRY, LANES)
     base, xt, sums, reach = pl.pallas_call(
         functools.partial(local_kernel, blocks),
         out_shape=[
@@ -377,14 +370,14 @@
     pieces = lax.all_to_all(pair, ("x", "zl", "yl"), 0, 0).reshape(rows_dp * 2 * PIECE, LANES)
     piece = pl.pallas_call(
         functools.partial(piece_kernel, norm, width // rows_dp),
-        out_shape=jax.ShapeDtypeStruct((slabs // 2, 32, LANES), F32),
+        out_shape=shape((chips * SHARE, LANES), F32),
         in_specs=[vmem],
         out_specs=vmem,
         compiler_params=params,
         name="sum_pieces",
     )(pieces)
-    spread = lax.all_to_all(piece, ("yh", "yl", "zh"), 0, 0)
-    both = lax.all_gather(spread, "core")
+    spread = lax.all_to_all(piece.reshape(chips, 1, SHARE * LANES), ("yh", "yl", "zh"), 0, 0)
+    both = lax.all_gather(spread, "core").reshape(slabs * SHARE, LANES)
     share = width // rows_dp
     grad_weight, grad_star, grad_log = pl.pallas_call(
         final_kernel,

time: 86.8 us -> 85 us (0.979)
  waiting for transfers between devices: 23 us -> 21.6 us
    all_to_all x2, waiting for transfers between devices: 23 us -> 21.6 us  [the longest x1 11.6 us: body(): lax.all_to_all(piece.reshape(chips, 1, SHARE * LANES), ('yh', 'yl', 'zh')...]
where the time goes in v6:
time: 85 us; the launch traced here: 84.6 us
  blocking collectives  31.5 us (37%)
  waiting for transfers between devices  21.6 us (25%)
  starting transfers between devices  19.9 us (23%)
  Pallas kernels  9.49 us (11%)
  between operations  1.43 us (2%)
    all_to_all x1, blocking collectives, body(): lax.all_to_all(pair, ('x', 'zl', 'yl'), 0, 0)  18.8 us
    all_to_all x1, starting transfers between devices, body(): lax.all_to_all(ends, ('yh', 'yl', 'zh'), 0, 0)  16.3 us
    all_to_all x1, waiting for transfers between devices, body(): lax.all_to_all(piece.reshape(chips, 1, SHARE * LANES), ('yh', 'yl', 'zh')...  11.6 us
    all_to_all x1, waiting for transfers between devices, body(): lax.all_to_all(ends, ('yh', 'yl', 'zh'), 0, 0)  9.99 us
    all_gather x1, blocking collectives, body(): both = lax.all_gather(spread, 'core').reshape(slabs * SHARE, LANES)  5.91 us
    all_gather x1, blocking collectives, body(): lax.all_gather(lax.all_to_all(ends, ('yh', 'yl', 'zh'), 0, 0), 'core')  4.35 us
    all_to_all x1, starting transfers between devices, body(): lax.all_to_all(piece.reshape(chips, 1, SHARE * LANES), ('yh', 'yl', 'zh')...  3.59 us
    pallas_call x1, Pallas kernels, body(): pl.pallas_call(functools.partial(ends_kernel, blocks, chips), out_shape=s...  2.71 us
  transfers between devices with their start and end apart: 2, of which 2 were waited for; matrix products, arithmetic and copies ran while one was open for 0% of the time, Pallas kernels for 5%

profile of v6, /device:TPU:1, one launch (start us, length us, event | category | flops | bytes accessed | tf_op | source)
XLA Modules:
  0.0 84.6 jit_solution(11285115732453425410)
XLA Ops:
  1.3 0.0 copy-start.1
  1.3 0.0 copy-start.2
  1.3 0.0 copy-start.3
  1.3 2.7 %slab_ends.1 = f32[400,128]{1,0:T(8,128)} custom-call(s32[1,4]{1,0:T(1,128)} %starts_ref.1, s32[1]{0:T(128)S(6)} %copy.18.star_hbm.star_ref, f32[1,128]{1,0:T(1,128)} %times_ref.1, bf16[1,128,1536]{2,1,0:T(8,128)(2,1)} %series_ref.1, bf16[1,128,1536]{2,1,0:T(8,128)(2,1)} %cot_ref.3, bf16[1536,128]{1,0:T(8,128)(2,1)} %w_ref.3, f32[16,1536]{1,0:T(8,128)} %table_ref.1, ...), custom_call_target="tpu_custom_call" | custom-call | tf_op jit(solution)/shard_map/slab_ends/pallas_call | solution.py:312
  4.0 0.0 copy-start
  4.0 0.0 copy-start.4
  4.0 16.3 %all-to-all-start = ((f32[16,1,3200]{2,1,0:T(1,128)}), f32[16,1,3200]{2,1,0:T(1,128)S(1)}, u32[]{:S(2)}, u32[]{:S(2)}) async-start(f32[16,1,3200]{2,1,0:T(1,128)} %bitcast.18), calls=%async_computation | async-start | bytes 409600 | tf_op jit(solution)/shard_map/all_to_all | solution.py:325
  20.4 0.0 copy-done.4
  20.4 0.0 copy-start.5
  20.4 0.0 copy-start.6
  20.5 0.0 copy-done.1
  20.5 0.0 copy-done.2
  20.5 0.0 copy-done.3
  20.5 0.0 copy-done
  20.5 0.6 copy-done.5
  21.1 0.0 copy-done.6
  21.1 2.6 %local_scans.1 = (f32[1536,128]{1,0:T(8,128)S(1)}, bf16[1536,128]{1,0:T(8,128)(2,1)S(1)}, f32[12,16,128]{2,1,0:T(8,128)S(1)}, f32[2,128,128]{2,1,0:T(8,128)S(1)}) custom-call(s32[1,4]{1,0:T(1,128)S(1)} %copy-done.5, s32[1]{0:T(128)S(6)} %copy.18.star_hbm.star_ref, f32[1,128]{1,0:T(1,128)S(1)} %copy-done.6, bf16[1,128,1536]{2,1,0:T(8,128)(2,1)S(1)} %copy-done.2, ...), custom_call_target="tpu_custom_call" | custom-call | flops 20000000 | bytes 4000000 | tf_op jit(solution)/shard_map/local_scans/pallas_call | solution.py:326
  23.7 10.0 %all-to-all-done = f32[16,1,3200]{2,1,0:T(1,128)S(1)} async-done(((f32[16,1,3200]{2,1,0:T(1,128)}), f32[16,1,3200]{2,1,0:T(1,128)S(1)}, u32[]{:S(2)}, u32[]{:S(2)}) %all-to-all-start) | async-done | bytes 204832 | tf_op jit(solution)/shard_map/all_to_all | solution.py:325
  33.7 4.3 %all-gather = f32[32,1,3200]{2,1,0:T(1,128)S(1)} all-gather(f32[16,1,3200]{2,1,0:T(1,128)S(1)} %all-to-all-done), channel_id=2, replica_groups=mesh['x'=4,'zl'=4,'yh'=4,'yl'=2,'zh'=2,'core'=2] {'core'}, dimensions={0}, use_global_device_ids=true | all-gather | bytes 614400 | tf_op jit(solution)/shard_map/all_gather | solution.py:325
  38.1 0.8 gradients.1
  38.9 2.4 %all-gather.1 = f32[1600,128]{1,0:T(8,128)S(1)} all-gather(f32[800,128]{1,0:T(8,128)S(1)} %get-tuple-element.20), channel_id=3, replica_groups=mesh['x'=4,'zl'=4,'yh'=4,'yl'=2,'zh'=2,'core'=2] {'core'}, dimensions={0}, use_global_device_ids=true | all-gather | bytes 1228800 | tf_op jit(solution)/shard_map/all_gather | solution.py:350
  41.3 0.1 pair_sum.1
  41.4 18.8 %all_to_all.15 = f32[32,1,3328]{2,1,0:T(1,128)S(1)} all-to-all(f32[32,1,3328]{2,1,0:T(1,128)S(1)} %bitcast.12), channel_id=1, replica_groups=mesh['x'=4,'zl'=4,'yh'=4,'yl'=2,'zh'=2,'core'=2] {'x','zl','yl'}, dimensions={0} | all-to-all | bytes 851968 | tf_op jit(solution)/shard_map/all_to_all | solution.py:370
  60.2 0.8 sum_pieces.1
  61.0 3.6 %all-to-all-start.2 = ((f32[16,1,3712]{2,1,0:T(1,128)}), f32[16,1,3712]{2,1,0:T(1,128)S(1)}, u32[]{:S(2)}, u32[]{:S(2)}) async-start(f32[16,1,3712]{2,1,0:T(1,128)} %bitcast.6), calls=%async_computation.2 | async-start | bytes 475136 | tf_op jit(solution)/shard_map/all_to_all | solution.py:379
  64.6 1.8 %series_gradient.1 = bf16[1,128,1536]{2,1,0:T(8,128)(2,1)} custom-call(bf16[1536,128]{1,0:T(8,128)(2,1)S(1)} %get-tuple-element.18.low_ref, bf16[1,128,1536]{2,1,0:T(8,128)(2,1)S(1)} %copy-done, bf16[1536,128]{1,0:T(8,128)(2,1)S(1)} %copy-done.1), custom_call_target="tpu_custom_call" | custom-call | flops 100000000 | bytes 1600000 | tf_op jit(solution)/shard_map/series_gradient/pallas_call | solution.py:360
  66.4 11.6 %all-to-all-done.2 = f32[16,1,3712]{2,1,0:T(1,128)S(1)} async-done(((f32[16,1,3712]{2,1,0:T(1,128)}), f32[16,1,3712]{2,1,0:T(1,128)S(1)}, u32[]{:S(2)}, u32[]{:S(2)}) %all-to-all-start.2) | async-done | bytes 237600 | tf_op jit(solution)/shard_map/all_to_all | solution.py:379
  78.0 5.9 %all-gather.2 = f32[32,1,3712]{2,1,0:T(1,128)S(1)} all-gather(f32[16,1,3712]{2,1,0:T(1,128)S(1)} %all-to-all-done.2), channel_id=4, replica_groups=mesh['x'=4,'zl'=4,'yh'=4,'yl'=2,'zh'=2,'core'=2] {'core'}, dimensions={0}, use_global_device_ids=true | all-gather | bytes 712704 | tf_op jit(solution)/shard_map/all_gather | solution.py:380
  83.9 0.7 outputs.1
  (1 shorter events, 0.0 us)
Async XLA Ops:
  1.3 19.2 %copy-start.1 = (bf16[1536,128]{1,0:T(8,128)(2,1)S(1)}, bf16[1536,128]{1,0:T(8,128)(2,1)}, u32[]{:S(2)}) copy-start(bf16[1536,128]{1,0:T(8,128)(2,1)} %w_ref.3) | copy-start | bytes 1179652
  1.3 19.2 %copy-start.2 = (bf16[1,128,1536]{2,1,0:T(8,128)(2,1)S(1)}, bf16[1,128,1536]{2,1,0:T(8,128)(2,1)}, u32[]{:S(2)}) copy-start(bf16[1,128,1536]{2,1,0:T(8,128)(2,1)} %series_ref.1) | copy-start | bytes 1179652
  1.3 19.2 %copy-start.3 = (f32[16,1536]{1,0:T(8,128)S(1)}, f32[16,1536]{1,0:T(8,128)}, u32[]{:S(2)}) copy-start(f32[16,1536]{1,0:T(8,128)} %table_ref.1) | copy-start | bytes 294916
  4.0 16.5 %copy-start = (bf16[1,128,1536]{2,1,0:T(8,128)(2,1)S(1)}, bf16[1,128,1536]{2,1,0:T(8,128)(2,1)}, u32[]{:S(2)}) copy-start(bf16[1,128,1536]{2,1,0:T(8,128)(2,1)} %cot_ref.3) | copy-start | bytes 1179652
  4.0 16.4 %copy-start.4 = (f32[1536]{0:T(1024)S(1)}, f32[1536]{0:T(1024)}, u32[]{:S(2)}) copy-start(f32[1536]{0:T(1024)} %param.15) | copy-start | bytes 18436
  4.0 29.7 %all-to-all-start = ((f32[16,1,3200]{2,1,0:T(1,128)}), f32[16,1,3200]{2,1,0:T(1,128)S(1)}, u32[]{:S(2)}, u32[]{:S(2)}) async-start(f32[16,1,3200]{2,1,0:T(1,128)} %bitcast.18), calls=%async_computation | async-start | bytes 409600 | tf_op jit(solution)/shard_map/all_to_all | solution.py:325
  20.4 0.7 copy-start.5
  20.4 0.7 copy-start.6
  61.0 17.0 %all-to-all-start.2 = ((f32[16,1,3712]{2,1,0:T(1,128)}), f32[16,1,3712]{2,1,0:T(1,128)S(1)}, u32[]{:S(2)}, u32[]{:S(2)}) async-start(f32[16,1,3712]{2,1,0:T(1,128)} %bitcast.6), calls=%async_computation.2 | async-start | bytes 475136 | tf_op jit(solution)/shard_map/all_to_all | solution.py:379

commit v7 on v6

--- a/solution.py
+++ b/solution.py
@@ -21,6 +21,10 @@
 def slab_index():
     chip = (lax.axis_index("yh") * 2 + lax.axis_index("yl")) * 2 + lax.axis_index("zh")
     return chip * 2 + lax.axis_index("core")
+
+
+def chip_slot(chip, chips):
+    return chip % 2 * (chips // 2) + chip // 2
 
 
 def elapsed_row(starts_ref, times_ref, me):
@@ -73,7 +77,8 @@
     ends_ref[0, 2 * blocks : 2 * blocks + 8, :] = tail
     ends_ref[1, 2 * blocks : 2 * blocks + 8, :] = tail
     for chip in range(chips):
-        out_ref[chip * CARRY : (chip + 1) * CARRY, :] = ends_ref[jnp.where(2 * chip + 1 - core > me, 0, 1), 0:CARRY, :]
+        at = chip_slot(chip, chips) * CARRY
+        out_ref[at : at + CARRY, :] = ends_ref[jnp.where(2 * chip + 1 - core > me, 0, 1), 0:CARRY, :]
 
 
 def shift(x, k, fill, sublane):
@@ -177,7 +182,7 @@
     mine = lax.axis_index("core")
     slope = -jnp.exp(lograte_ref[...])
     slope2 = jnp.concatenate([slope, slope], axis=0)
-    start = lambda s: (s % 2 * (slabs // 2) + s // 2) * CARRY
+    start = lambda s: (s % 2 * (slabs // 2) + chip_slot(s // 2, slabs // 2)) * CARRY
     took = lambda s: got_ref[start(s) + 2 * blocks : start(s) + 2 * blocks + 1, :]
     between = [None] * slabs
     run = jnp.zeros((1, LANES), F32)
@@ -243,7 +248,7 @@
         for yl in range(2):
             piece = dp * 2 + yl
             rows = slice(piece * 24, piece * 24 + 24)
-            at = piece * PIECE
+            at = ((yl * 4 + dp % 4) * 4 + dp // 4) * PIECE
             out_ref[at : at + 24, :] = keep_ref[rows, :] + sent_ref[other, rows, :]
             out_ref[at + 24 : at + 26, :] = tile
 
@@ -283,7 +288,7 @@
     for core in range(2):
         for yl in range(2):
             q = core * 2 + yl
-            parts = [(core * chips + chip) * SHARE for chip in range(chips) if chip // 2 % 2 == yl]
+            parts = [(core * chips + chip) * SHARE for chip in range(chips) if chip % 2 == yl]
             total = got_ref[parts[0] : parts[0] + SHARE, :]
             for at in parts[1:]:
                 total = total + got_ref[at : at + SHARE, :]
@@ -322,7 +327,7 @@
         name="slab_ends",
     )(*common)
     ends = ends.reshape(chips, 1, CARRY * LANES)
-    got = lax.all_gather(lax.all_to_all(ends, ("yh", "yl", "zh"), 0, 0), "core").reshape(slabs * CARRY, LANES)
+    got = lax.all_gather(lax.all_to_all(ends, ("zh", "yh", "yl"), 0, 0), "core").reshape(slabs * CARRY, LANES)
     base, xt, sums, reach = pl.pallas_call(
         functools.partial(local_kernel, blocks),
         out_shape=[
@@ -367,7 +372,7 @@
         name="series_gradient",
     )(low, cotangent, block_weight)
     pair = pair.reshape(rows_dp * 2, 1, PIECE * LANES)
-    pieces = lax.all_to_all(pair, ("x", "zl", "yl"), 0, 0).reshape(rows_dp * 2 * PIECE, LANES)
+    pieces = lax.all_to_all(pair, ("yl", "zl", "x"), 0, 0).reshape(rows_dp * 2 * PIECE, LANES)
     piece = pl.pallas_call(
         functools.partial(piece_kernel, norm, width // rows_dp),
         out_shape=shape((chips * SHARE, LANES), F32),
@@ -376,7 +381,7 @@
         compiler_params=params,
         name="sum_pieces",
     )(pieces)
-    spread = lax.all_to_all(piece.reshape(chips, 1, SHARE * LANES), ("yh", "yl", "zh"), 0, 0)
+    spread = lax.all_to_all(piece.reshape(chips, 1, SHARE * LANES), ("zh", "yh", "yl"), 0, 0)
     both = lax.all_gather(spread, "core").reshape(slabs * SHARE, LANES)
     share = width // rows_dp
     grad_weight, grad_star, grad_log = pl.pallas_call(

time: 85 us -> 83.7 us (0.985)
  waiting for transfers between devices: 21.6 us -> 18.5 us
  blocking collectives: 31.5 us -> 32.5 us
    all_to_all x2, waiting for transfers between devices: 21.6 us -> 18.5 us  [the longest x1 9.82 us: body(): lax.all_to_all(piece.reshape(chips, 1, SHARE * LANES), ('zh', 'yh', 'yl')...]
    all_to_all x1, blocking collectives: 18.8 us -> 21.6 us  [body(): lax.all_to_all(pair, ('yl', 'zl', 'x'), 0, 0)]
    all_gather x1, blocking collectives: 5.91 us -> 4.61 us  [body(): both = lax.all_gather(spread, 'core').reshape(slabs * SHARE, LANES)]
where the time goes in v7:
time: 83.7 us; the launch traced here: 83.2 us
  blocking collectives  32.5 us (39%)
  starting transfers between devices  20.7 us (25%)
  waiting for transfers between devices  18.5 us (22%)
  Pallas kernels  9.49 us (11%)
  between operations  1.43 us (2%)
    all_to_all x1, blocking collectives, body(): lax.all_to_all(pair, ('yl', 'zl', 'x'), 0, 0)  21.6 us
    all_to_all x1, starting transfers between devices, body(): lax.all_to_all(ends, ('zh', 'yh', 'yl'), 0, 0)  16.3 us
    all_to_all x1, waiting for transfers between devices, body(): lax.all_to_all(piece.reshape(chips, 1, SHARE * LANES), ('zh', 'yh', 'yl')...  9.82 us
    all_to_all x1, waiting for transfers between devices, body(): lax.all_to_all(ends, ('zh', 'yh', 'yl'), 0, 0)  8.64 us
    all_gather x1, blocking collectives, body(): both = lax.all_gather(spread, 'core').reshape(slabs * SHARE, LANES)  4.61 us
    all_to_all x1, starting transfers between devices, body(): lax.all_to_all(piece.reshape(chips, 1, SHARE * LANES), ('zh', 'yh', 'yl')...  4.31 us
    all_gather x1, blocking collectives, body(): lax.all_gather(lax.all_to_all(ends, ('zh', 'yh', 'yl'), 0, 0), 'core')  3.92 us
    pallas_call x1, Pallas kernels, body(): pl.pallas_call(functools.partial(ends_kernel, blocks, chips), out_shape=s...  2.71 us
  transfers between devices with their start and end apart: 2, of which 2 were waited for; matrix products, arithmetic and copies ran while one was open for 0% of the time, Pallas kernels for 5%

profile of v7, /device:TPU:1, one launch (start us, length us, event | category | flops | bytes accessed | tf_op | source)
XLA Modules:
  0.0 83.2 jit_solution(16447573424502842166)
XLA Ops:
  1.3 0.0 copy-start.1
  1.3 0.0 copy-start.2
  1.3 0.0 copy-start.3
  1.3 2.7 %slab_ends.1 = f32[400,128]{1,0:T(8,128)} custom-call(s32[1,4]{1,0:T(1,128)} %starts_ref.1, s32[1]{0:T(128)S(6)} %copy.18.star_hbm.star_ref, f32[1,128]{1,0:T(1,128)} %times_ref.1, bf16[1,128,1536]{2,1,0:T(8,128)(2,1)} %series_ref.1, bf16[1,128,1536]{2,1,0:T(8,128)(2,1)} %cot_ref.3, bf16[1536,128]{1,0:T(8,128)(2,1)} %w_ref.3, f32[16,1536]{1,0:T(8,128)} %table_ref.1, ...), custom_call_target="tpu_custom_call" | custom-call | tf_op jit(solution)/shard_map/slab_ends/pallas_call | solution.py:317
  4.0 0.0 copy-start
  4.0 0.0 copy-start.4
  4.0 16.3 %all-to-all-start = ((f32[16,1,3200]{2,1,0:T(1,128)}), f32[16,1,3200]{2,1,0:T(1,128)S(1)}, u32[]{:S(2)}, u32[]{:S(2)}) async-start(f32[16,1,3200]{2,1,0:T(1,128)} %bitcast.18), calls=%async_computation | async-start | bytes 409600 | tf_op jit(solution)/shard_map/all_to_all | solution.py:330
  20.4 0.0 copy-done.4
  20.4 0.0 copy-start.5
  20.4 0.0 copy-start.6
  20.5 0.0 copy-done.1
  20.5 0.0 copy-done.2
  20.5 0.0 copy-done.3
  20.5 0.0 copy-done
  20.5 0.6 copy-done.5
  21.1 0.0 copy-done.6
  21.1 2.6 %local_scans.1 = (f32[1536,128]{1,0:T(8,128)S(1)}, bf16[1536,128]{1,0:T(8,128)(2,1)S(1)}, f32[12,16,128]{2,1,0:T(8,128)S(1)}, f32[2,128,128]{2,1,0:T(8,128)S(1)}) custom-call(s32[1,4]{1,0:T(1,128)S(1)} %copy-done.5, s32[1]{0:T(128)S(6)} %copy.18.star_hbm.star_ref, f32[1,128]{1,0:T(1,128)S(1)} %copy-done.6, bf16[1,128,1536]{2,1,0:T(8,128)(2,1)S(1)} %copy-done.2, ...), custom_call_target="tpu_custom_call" | custom-call | flops 20000000 | bytes 4000000 | tf_op jit(solution)/shard_map/local_scans/pallas_call | solution.py:331
  23.7 8.6 %all-to-all-done = f32[16,1,3200]{2,1,0:T(1,128)S(1)} async-done(((f32[16,1,3200]{2,1,0:T(1,128)}), f32[16,1,3200]{2,1,0:T(1,128)S(1)}, u32[]{:S(2)}, u32[]{:S(2)}) %all-to-all-start) | async-done | bytes 204832 | tf_op jit(solution)/shard_map/all_to_all | solution.py:330
  32.4 3.9 %all-gather = f32[32,1,3200]{2,1,0:T(1,128)S(1)} all-gather(f32[16,1,3200]{2,1,0:T(1,128)S(1)} %all-to-all-done), channel_id=2, replica_groups=mesh['x'=4,'zl'=4,'yh'=4,'yl'=2,'zh'=2,'core'=2] {'core'}, dimensions={0}, use_global_device_ids=true | all-gather | bytes 614400 | tf_op jit(solution)/shard_map/all_gather | solution.py:330
  36.3 0.8 gradients.1
  37.1 2.4 %all-gather.1 = f32[1600,128]{1,0:T(8,128)S(1)} all-gather(f32[800,128]{1,0:T(8,128)S(1)} %get-tuple-element.20), channel_id=3, replica_groups=mesh['x'=4,'zl'=4,'yh'=4,'yl'=2,'zh'=2,'core'=2] {'core'}, dimensions={0}, use_global_device_ids=true | all-gather | bytes 1228800 | tf_op jit(solution)/shard_map/all_gather | solution.py:355
  39.5 0.1 pair_sum.1
  39.6 21.6 %all_to_all.15 = f32[32,1,3328]{2,1,0:T(1,128)S(1)} all-to-all(f32[32,1,3328]{2,1,0:T(1,128)S(1)} %bitcast.12), channel_id=1, replica_groups=mesh['x'=4,'zl'=4,'yh'=4,'yl'=2,'zh'=2,'core'=2] {'yl','zl','x'}, dimensions={0} | all-to-all | bytes 851968 | tf_op jit(solution)/shard_map/all_to_all | solution.py:375
  61.3 0.8 sum_pieces.1
  62.0 4.3 %all-to-all-start.2 = ((f32[16,1,3712]{2,1,0:T(1,128)}), f32[16,1,3712]{2,1,0:T(1,128)S(1)}, u32[]{:S(2)}, u32[]{:S(2)}) async-start(f32[16,1,3712]{2,1,0:T(1,128)} %bitcast.6), calls=%async_computation.2 | async-start | bytes 475136 | tf_op jit(solution)/shard_map/all_to_all | solution.py:384
  66.4 1.8 %series_gradient.1 = bf16[1,128,1536]{2,1,0:T(8,128)(2,1)} custom-call(bf16[1536,128]{1,0:T(8,128)(2,1)S(1)} %get-tuple-element.18.low_ref, bf16[1,128,1536]{2,1,0:T(8,128)(2,1)S(1)} %copy-done, bf16[1536,128]{1,0:T(8,128)(2,1)S(1)} %copy-done.1), custom_call_target="tpu_custom_call" | custom-call | flops 100000000 | bytes 1600000 | tf_op jit(solution)/shard_map/series_gradient/pallas_call | solution.py:365
  68.1 9.8 %all-to-all-done.2 = f32[16,1,3712]{2,1,0:T(1,128)S(1)} async-done(((f32[16,1,3712]{2,1,0:T(1,128)}), f32[16,1,3712]{2,1,0:T(1,128)S(1)}, u32[]{:S(2)}, u32[]{:S(2)}) %all-to-all-start.2) | async-done | bytes 237600 | tf_op jit(solution)/shard_map/all_to_all | solution.py:384
  77.9 4.6 %all-gather.2 = f32[32,1,3712]{2,1,0:T(1,128)S(1)} all-gather(f32[16,1,3712]{2,1,0:T(1,128)S(1)} %all-to-all-done.2), channel_id=4, replica_groups=mesh['x'=4,'zl'=4,'yh'=4,'yl'=2,'zh'=2,'core'=2] {'core'}, dimensions={0}, use_global_device_ids=true | all-gather | bytes 712704 | tf_op jit(solution)/shard_map/all_gather | solution.py:385
  82.5 0.7 outputs.1
  (1 shorter events, 0.0 us)
Async XLA Ops:
  1.3 19.2 %copy-start.1 = (bf16[1536,128]{1,0:T(8,128)(2,1)S(1)}, bf16[1536,128]{1,0:T(8,128)(2,1)}, u32[]{:S(2)}) copy-start(bf16[1536,128]{1,0:T(8,128)(2,1)} %w_ref.3) | copy-start | bytes 1179652
  1.3 19.2 %copy-start.2 = (bf16[1,128,1536]{2,1,0:T(8,128)(2,1)S(1)}, bf16[1,128,1536]{2,1,0:T(8,128)(2,1)}, u32[]{:S(2)}) copy-start(bf16[1,128,1536]{2,1,0:T(8,128)(2,1)} %series_ref.1) | copy-start | bytes 1179652
  1.3 19.2 %copy-start.3 = (f32[16,1536]{1,0:T(8,128)S(1)}, f32[16,1536]{1,0:T(8,128)}, u32[]{:S(2)}) copy-start(f32[16,1536]{1,0:T(8,128)} %table_ref.1) | copy-start | bytes 294916
  4.0 16.5 %copy-start = (bf16[1,128,1536]{2,1,0:T(8,128)(2,1)S(1)}, bf16[1,128,1536]{2,1,0:T(8,128)(2,1)}, u32[]{:S(2)}) copy-start(bf16[1,128,1536]{2,1,0:T(8,128)(2,1)} %cot_ref.3) | copy-start | bytes 1179652
  4.0 16.4 %copy-start.4 = (f32[1536]{0:T(1024)S(1)}, f32[1536]{0:T(1024)}, u32[]{:S(2)}) copy-start(f32[1536]{0:T(1024)} %param.15) | copy-start | bytes 18436
  4.0 28.3 %all-to-all-start = ((f32[16,1,3200]{2,1,0:T(1,128)}), f32[16,1,3200]{2,1,0:T(1,128)S(1)}, u32[]{:S(2)}, u32[]{:S(2)}) async-start(f32[16,1,3200]{2,1,0:T(1,128)} %bitcast.18), calls=%async_computation | async-start | bytes 409600 | tf_op jit(solution)/shard_map/all_to_all | solution.py:330
  20.4 0.7 copy-start.5
  20.4 0.7 copy-start.6
  62.0 15.9 %all-to-all-start.2 = ((f32[16,1,3712]{2,1,0:T(1,128)}), f32[16,1,3712]{2,1,0:T(1,128)S(1)}, u32[]{:S(2)}, u32[]{:S(2)}) async-start(f32[16,1,3712]{2,1,0:T(1,128)} %bitcast.6), calls=%async_computation.2 | async-start | bytes 475136 | tf_op jit(solution)/shard_map/all_to_all | solution.py:384

commit v8 on v7

--- a/solution.py
+++ b/solution.py
@@ -248,7 +248,7 @@
         for yl in range(2):
             piece = dp * 2 + yl
             rows = slice(piece * 24, piece * 24 + 24)
-            at = ((yl * 4 + dp % 4) * 4 + dp // 4) * PIECE
+            at = piece * PIECE
             out_ref[at : at + 24, :] = keep_ref[rows, :] + sent_ref[other, rows, :]
             out_ref[at + 24 : at + 26, :] = tile
 
@@ -372,7 +372,7 @@
         name="series_gradient",
     )(low, cotangent, block_weight)
     pair = pair.reshape(rows_dp * 2, 1, PIECE * LANES)
-    pieces = lax.all_to_all(pair, ("yl", "zl", "x"), 0, 0).reshape(rows_dp * 2 * PIECE, LANES)
+    pieces = lax.all_to_all(pair, ("x", "zl", "yl"), 0, 0).reshape(rows_dp * 2 * PIECE, LANES)
     piece = pl.pallas_call(
         functools.partial(piece_kernel, norm, width // rows_dp),
         out_shape=shape((chips * SHARE, LANES), F32),

time: 83.7 us -> 83.2 us (level)
    all_gather x1, blocking collectives: 4.61 us -> 5.99 us  [body(): both = lax.all_gather(spread, 'core').reshape(slabs * SHARE, LANES)]
    all_to_all x1, blocking collectives: 21.6 us -> 20.2 us  [body(): lax.all_to_all(pair, ('x', 'zl', 'yl'), 0, 0)]
where the time goes in v8:
time: 83.2 us; the launch traced here: 82.7 us
  blocking collectives  32.5 us (39%)
  starting transfers between devices  20.1 us (24%)
  waiting for transfers between devices  18.6 us (22%)
  Pallas kernels  9.49 us (11%)
  between operations  1.43 us (2%)
    all_to_all x1, blocking collectives, body(): lax.all_to_all(pair, ('x', 'zl', 'yl'), 0, 0)  20.2 us
    all_to_all x1, starting transfers between devices, body(): lax.all_to_all(ends, ('zh', 'yh', 'yl'), 0, 0)  16.3 us
    all_to_all x1, waiting for transfers between devices, body(): lax.all_to_all(piece.reshape(chips, 1, SHARE * LANES), ('zh', 'yh', 'yl')...  9.91 us
    all_to_all x1, waiting for transfers between devices, body(): lax.all_to_all(ends, ('zh', 'yh', 'yl'), 0, 0)  8.64 us
    all_gather x1, blocking collectives, body(): both = lax.all_gather(spread, 'core').reshape(slabs * SHARE, LANES)  5.99 us
    all_gather x1, blocking collectives, body(): lax.all_gather(lax.all_to_all(ends, ('zh', 'yh', 'yl'), 0, 0), 'core')  3.92 us
    all_to_all x1, starting transfers between devices, body(): lax.all_to_all(piece.reshape(chips, 1, SHARE * LANES), ('zh', 'yh', 'yl')...  3.74 us
    pallas_call x1, Pallas kernels, body(): pl.pallas_call(functools.partial(ends_kernel, blocks, chips), out_shape=s...  2.71 us
  transfers between devices with their start and end apart: 2, of which 2 were waited for; matrix products, arithmetic and copies ran while one was open for 0% of the time, Pallas kernels for 5%

profile of v8, /device:TPU:1, one launch (start us, length us, event | category | flops | bytes accessed | tf_op | source)
XLA Modules:
  0.0 82.7 jit_solution(5214306776822312264)
XLA Ops:
  1.3 0.0 copy-start.1
  1.3 0.0 copy-start.2
  1.3 0.0 copy-start.3
  1.3 2.7 %slab_ends.1 = f32[400,128]{1,0:T(8,128)} custom-call(s32[1,4]{1,0:T(1,128)} %starts_ref.1, s32[1]{0:T(128)S(6)} %copy.18.star_hbm.star_ref, f32[1,128]{1,0:T(1,128)} %times_ref.1, bf16[1,128,1536]{2,1,0:T(8,128)(2,1)} %series_ref.1, bf16[1,128,1536]{2,1,0:T(8,128)(2,1)} %cot_ref.3, bf16[1536,128]{1,0:T(8,128)(2,1)} %w_ref.3, f32[16,1536]{1,0:T(8,128)} %table_ref.1, ...), custom_call_target="tpu_custom_call" | custom-call | tf_op jit(solution)/shard_map/slab_ends/pallas_call | solution.py:317
  4.0 0.0 copy-start
  4.0 0.0 copy-start.4
  4.0 16.3 %all-to-all-start = ((f32[16,1,3200]{2,1,0:T(1,128)}), f32[16,1,3200]{2,1,0:T(1,128)S(1)}, u32[]{:S(2)}, u32[]{:S(2)}) async-start(f32[16,1,3200]{2,1,0:T(1,128)} %bitcast.18), calls=%async_computation | async-start | bytes 409600 | tf_op jit(solution)/shard_map/all_to_all | solution.py:330
  20.4 0.0 copy-done.4
  20.4 0.0 copy-start.5
  20.4 0.0 copy-start.6
  20.5 0.0 copy-done.1
  20.5 0.0 copy-done.2
  20.5 0.0 copy-done.3
  20.5 0.0 copy-done
  20.5 0.6 copy-done.5
  21.1 0.0 copy-done.6
  21.1 2.6 %local_scans.1 = (f32[1536,128]{1,0:T(8,128)S(1)}, bf16[1536,128]{1,0:T(8,128)(2,1)S(1)}, f32[12,16,128]{2,1,0:T(8,128)S(1)}, f32[2,128,128]{2,1,0:T(8,128)S(1)}) custom-call(s32[1,4]{1,0:T(1,128)S(1)} %copy-done.5, s32[1]{0:T(128)S(6)} %copy.18.star_hbm.star_ref, f32[1,128]{1,0:T(1,128)S(1)} %copy-done.6, bf16[1,128,1536]{2,1,0:T(8,128)(2,1)S(1)} %copy-done.2, ...), custom_call_target="tpu_custom_call" | custom-call | flops 20000000 | bytes 4000000 | tf_op jit(solution)/shard_map/local_scans/pallas_call | solution.py:331
  23.7 8.6 %all-to-all-done = f32[16,1,3200]{2,1,0:T(1,128)S(1)} async-done(((f32[16,1,3200]{2,1,0:T(1,128)}), f32[16,1,3200]{2,1,0:T(1,128)S(1)}, u32[]{:S(2)}, u32[]{:S(2)}) %all-to-all-start) | async-done | bytes 204832 | tf_op jit(solution)/shard_map/all_to_all | solution.py:330
  32.4 3.9 %all-gather = f32[32,1,3200]{2,1,0:T(1,128)S(1)} all-gather(f32[16,1,3200]{2,1,0:T(1,128)S(1)} %all-to-all-done), channel_id=2, replica_groups=mesh['x'=4,'zl'=4,'yh'=4,'yl'=2,'zh'=2,'core'=2] {'core'}, dimensions={0}, use_global_device_ids=true | all-gather | bytes 614400 | tf_op jit(solution)/shard_map/all_gather | solution.py:330
  36.3 0.8 gradients.1
  37.1 2.4 %all-gather.1 = f32[1600,128]{1,0:T(8,128)S(1)} all-gather(f32[800,128]{1,0:T(8,128)S(1)} %get-tuple-element.20), channel_id=3, replica_groups=mesh['x'=4,'zl'=4,'yh'=4,'yl'=2,'zh'=2,'core'=2] {'core'}, dimensions={0}, use_global_device_ids=true | all-gather | bytes 1228800 | tf_op jit(solution)/shard_map/all_gather | solution.py:355
  39.5 0.1 pair_sum.1
  39.6 20.2 %all_to_all.15 = f32[32,1,3328]{2,1,0:T(1,128)S(1)} all-to-all(f32[32,1,3328]{2,1,0:T(1,128)S(1)} %bitcast.12), channel_id=1, replica_groups=mesh['x'=4,'zl'=4,'yh'=4,'yl'=2,'zh'=2,'core'=2] {'x','zl','yl'}, dimensions={0} | all-to-all | bytes 851968 | tf_op jit(solution)/shard_map/all_to_all | solution.py:375
  59.9 0.8 sum_pieces.1
  60.7 3.7 %all-to-all-start.2 = ((f32[16,1,3712]{2,1,0:T(1,128)}), f32[16,1,3712]{2,1,0:T(1,128)S(1)}, u32[]{:S(2)}, u32[]{:S(2)}) async-start(f32[16,1,3712]{2,1,0:T(1,128)} %bitcast.6), calls=%async_computation.2 | async-start | bytes 475136 | tf_op jit(solution)/shard_map/all_to_all | solution.py:384
  64.4 1.8 %series_gradient.1 = bf16[1,128,1536]{2,1,0:T(8,128)(2,1)} custom-call(bf16[1536,128]{1,0:T(8,128)(2,1)S(1)} %get-tuple-element.18.low_ref, bf16[1,128,1536]{2,1,0:T(8,128)(2,1)S(1)} %copy-done, bf16[1536,128]{1,0:T(8,128)(2,1)S(1)} %copy-done.1), custom_call_target="tpu_custom_call" | custom-call | flops 100000000 | bytes 1600000 | tf_op jit(solution)/shard_map/series_gradient/pallas_call | solution.py:365
  66.2 9.9 %all-to-all-done.2 = f32[16,1,3712]{2,1,0:T(1,128)S(1)} async-done(((f32[16,1,3712]{2,1,0:T(1,128)}), f32[16,1,3712]{2,1,0:T(1,128)S(1)}, u32[]{:S(2)}, u32[]{:S(2)}) %all-to-all-start.2) | async-done | bytes 237600 | tf_op jit(solution)/shard_map/all_to_all | solution.py:384
  76.1 6.0 %all-gather.2 = f32[32,1,3712]{2,1,0:T(1,128)S(1)} all-gather(f32[16,1,3712]{2,1,0:T(1,128)S(1)} %all-to-all-done.2), channel_id=4, replica_groups=mesh['x'=4,'zl'=4,'yh'=4,'yl'=2,'zh'=2,'core'=2] {'core'}, dimensions={0}, use_global_device_ids=true | all-gather | bytes 712704 | tf_op jit(solution)/shard_map/all_gather | solution.py:385
  82.1 0.7 outputs.1
  (1 shorter events, 0.0 us)
Async XLA Ops:
  1.3 19.2 %copy-start.1 = (bf16[1536,128]{1,0:T(8,128)(2,1)S(1)}, bf16[1536,128]{1,0:T(8,128)(2,1)}, u32[]{:S(2)}) copy-start(bf16[1536,128]{1,0:T(8,128)(2,1)} %w_ref.3) | copy-start | bytes 1179652
  1.3 19.2 %copy-start.2 = (bf16[1,128,1536]{2,1,0:T(8,128)(2,1)S(1)}, bf16[1,128,1536]{2,1,0:T(8,128)(2,1)}, u32[]{:S(2)}) copy-start(bf16[1,128,1536]{2,1,0:T(8,128)(2,1)} %series_ref.1) | copy-start | bytes 1179652
  1.3 19.2 %copy-start.3 = (f32[16,1536]{1,0:T(8,128)S(1)}, f32[16,1536]{1,0:T(8,128)}, u32[]{:S(2)}) copy-start(f32[16,1536]{1,0:T(8,128)} %table_ref.1) | copy-start | bytes 294916
  4.0 16.5 %copy-start = (bf16[1,128,1536]{2,1,0:T(8,128)(2,1)S(1)}, bf16[1,128,1536]{2,1,0:T(8,128)(2,1)}, u32[]{:S(2)}) copy-start(bf16[1,128,1536]{2,1,0:T(8,128)(2,1)} %cot_ref.3) | copy-start | bytes 1179652
  4.0 16.4 %copy-start.4 = (f32[1536]{0:T(1024)S(1)}, f32[1536]{0:T(1024)}, u32[]{:S(2)}) copy-start(f32[1536]{0:T(1024)} %param.15) | copy-start | bytes 18436
  4.0 28.3 %all-to-all-start = ((f32[16,1,3200]{2,1,0:T(1,128)}), f32[16,1,3200]{2,1,0:T(1,128)S(1)}, u32[]{:S(2)}, u32[]{:S(2)}) async-start(f32[16,1,3200]{2,1,0:T(1,128)} %bitcast.18), calls=%async_computation | async-start | bytes 409600 | tf_op jit(solution)/shard_map/all_to_all | solution.py:330
  20.4 0.7 copy-start.5
  20.4 0.7 copy-start.6
  60.7 15.4 %all-to-all-start.2 = ((f32[16,1,3712]{2,1,0:T(1,128)}), f32[16,1,3712]{2,1,0:T(1,128)S(1)}, u32[]{:S(2)}, u32[]{:S(2)}) async-start(f32[16,1,3712]{2,1,0:T(1,128)} %bitcast.6), calls=%async_computation.2 | async-start | bytes 475136 | tf_op jit(solution)/shard_map/all_to_all | solution.py:384

commit v9 on v8

--- a/solution.py
+++ b/solution.py
@@ -12,8 +12,9 @@
 STEPS = SLAB // CHUNKS
 FAR = 1e9
 CARRY = 25
-SHARE = 29
-PIECE = 26
+SHARE = 57
+ROWS = 48
+PIECE = 50
 F32 = jnp.float32
 BF16 = jnp.bfloat16
 
@@ -245,12 +246,10 @@
     star = jnp.broadcast_to(star_ref[0].astype(F32), (2, LANES))
     for dp in range(rows_dp):
         tile = jnp.where(lane < share, flat_ref[0:2, dp * share : dp * share + LANES], star)
-        for yl in range(2):
-            piece = dp * 2 + yl
-            rows = slice(piece * 24, piece * 24 + 24)
-            at = piece * PIECE
-            out_ref[at : at + 24, :] = keep_ref[rows, :] + sent_ref[other, rows, :]
-            out_ref[at + 24 : at + 26, :] = tile
+        rows = slice(dp * ROWS, (dp + 1) * ROWS)
+        at = dp * PIECE
+        out_ref[at : at + ROWS, :] = keep_ref[rows, :] + sent_ref[other, rows, :]
+        out_ref[at + ROWS : at + ROWS + 2, :] = tile
 
 
 def series_kernel(blocks, low_ref, cot_ref, w_ref, dx_ref):
@@ -265,37 +264,35 @@
 
 
 def piece_kernel(norm, share, got_ref, out_ref):
-    first = (lax.axis_index("core") * 2 + lax.axis_index("yl")) * 4
+    first = lax.axis_index("core") * 8
     sources = got_ref.shape[0] // PIECE
-    total = got_ref[0:24, :]
+    total = got_ref[0:ROWS, :]
     for s in range(1, sources):
-        total = total + got_ref[s * PIECE : s * PIECE + 24, :]
-    terms = got_ref[pl.ds(24, sources, stride=PIECE), :]
-    logs = jnp.sum(got_ref[pl.ds(25, sources, stride=PIECE), :], axis=0, keepdims=True)
+        total = total + got_ref[s * PIECE : s * PIECE + ROWS, :]
+    terms = got_ref[pl.ds(ROWS, sources, stride=PIECE), :]
+    logs = jnp.sum(got_ref[pl.ds(ROWS + 1, sources, stride=PIECE), :], axis=0, keepdims=True)
     star = jnp.broadcast_to(terms[:, share : share + 1], terms.shape)
-    hits = [star == (first + k).astype(F32) for k in range(4)]
+    hits = [star == (first + k).astype(F32) for k in range(8)]
     stars = [jnp.sum(jnp.where(hit, terms, 0.0), axis=0, keepdims=True) for hit in hits]
     total = total * norm
     tail = jnp.concatenate(stars + [logs], axis=0) * norm
     for d in range(out_ref.shape[0] // SHARE):
-        out_ref[d * SHARE : d * SHARE + 24, :] = total
-        out_ref[d * SHARE + 24 : d * SHARE + 29, :] = tail
+        out_ref[d * SHARE : d * SHARE + ROWS, :] = total
+        out_ref[d * SHARE + ROWS : (d + 1) * SHARE, :] = tail
 
 
 def final_kernel(got_ref, weight_ref, star_ref, log_ref):
     share = star_ref.shape[1]
     chips = got_ref.shape[0] // SHARE // 2
     for core in range(2):
-        for yl in range(2):
-            q = core * 2 + yl
-            parts = [(core * chips + chip) * SHARE for chip in range(chips) if chip % 2 == yl]
-            total = got_ref[parts[0] : parts[0] + SHARE, :]
-            for at in parts[1:]:
-                total = total + got_ref[at : at + SHARE, :]
-            weight_ref[q * 24 : q * 24 + 24, :] = total[0:24, :]
-            star_ref[q * 4 : q * 4 + 4, :] = total[24:28, 0:share]
-            if q == 0:
-                log_ref[...] = total[28:29, 0:share]
+        parts = [(core * chips + chip) * SHARE for chip in range(chips)]
+        total = got_ref[parts[0] : parts[0] + SHARE, :]
+        for at in parts[1:]:
+            total = total + got_ref[at : at + SHARE, :]
+        weight_ref[core * ROWS : (core + 1) * ROWS, :] = total[0:ROWS, :]
+        star_ref[core * 8 : core * 8 + 8, :] = total[ROWS : ROWS + 8, 0:share]
+        if core == 0:
+            log_ref[...] = total[ROWS + 8 : ROWS + 9, 0:share]
 
 
 def body(series, cotangent, step_times, seg_starts, star_of_row, block_weight, star_table, log_rate):
@@ -355,7 +352,7 @@
     sent = lax.all_gather(send, "core")
     pair = pl.pallas_call(
         functools.partial(pair_kernel, rows_dp),
-        out_shape=shape((rows_dp * 2 * PIECE, LANES), F32),
+        out_shape=shape((rows_dp * PIECE, LANES), F32),
         in_specs=[smem, vmem, vmem],
         out_specs=vmem,
         scratch_shapes=[pltpu.VMEM((8, width + LANES), F32)],
@@ -371,8 +368,8 @@
         cost_estimate=pl.CostEstimate(flops=100_000_000, bytes_accessed=1_600_000, transcendentals=0),
         name="series_gradient",
     )(low, cotangent, block_weight)
-    pair = pair.reshape(rows_dp * 2, 1, PIECE * LANES)
-    pieces = lax.all_to_all(pair, ("x", "zl", "yl"), 0, 0).reshape(rows_dp * 2 * PIECE, LANES)
+    pair = pair.reshape(rows_dp, 1, PIECE * LANES)
+    pieces = lax.all_to_all(pair, ("x", "zl"), 0, 0).reshape(rows_dp * PIECE, LANES)
     piece = pl.pallas_call(
         functools.partial(piece_kernel, norm, width // rows_dp),
         out_shape=shape((chips * SHARE, LANES), F32),

time: 83.2 us -> 86.3 us (1.037)
  waiting for transfers between devices: 18.6 us -> 22.6 us
  blocking collectives: 32.5 us -> 31.2 us
    all_to_all x1, waiting for transfers between devices: 9.91 us -> 14 us  [body(): lax.all_to_all(piece.reshape(chips, 1, SHARE * LANES), ('zh', 'yh', 'yl')...]
where the time goes in v9:
time: 86.3 us; the launch traced here: 85.9 us
  blocking collectives  31.2 us (36%)
  waiting for transfers between devices  22.6 us (26%)
  starting transfers between devices  20.4 us (24%)
  Pallas kernels  9.59 us (11%)
  between operations  1.43 us (2%)
    all_to_all x1, blocking collectives, body(): lax.all_to_all(pair, ('x', 'zl'), 0, 0).reshape(rows_dp * PIECE, LANES)  19.7 us
    all_to_all x1, starting transfers between devices, body(): lax.all_to_all(ends, ('zh', 'yh', 'yl'), 0, 0)  16.3 us
    all_to_all x1, waiting for transfers between devices, body(): lax.all_to_all(piece.reshape(chips, 1, SHARE * LANES), ('zh', 'yh', 'yl')...  14 us
    all_to_all x1, waiting for transfers between devices, body(): lax.all_to_all(ends, ('zh', 'yh', 'yl'), 0, 0)  8.64 us
    all_gather x1, blocking collectives, body(): both = lax.all_gather(spread, 'core').reshape(slabs * SHARE, LANES)  5.23 us
    all_to_all x1, starting transfers between devices, body(): lax.all_to_all(piece.reshape(chips, 1, SHARE * LANES), ('zh', 'yh', 'yl')...  4.06 us
    all_gather x1, blocking collectives, body(): lax.all_gather(lax.all_to_all(ends, ('zh', 'yh', 'yl'), 0, 0), 'core')  3.92 us
    pallas_call x1, Pallas kernels, body(): pl.pallas_call(functools.partial(ends_kernel, blocks, chips), out_shape=s...  2.71 us
  transfers between devices with their start and end apart: 2, of which 2 were waited for; matrix products, arithmetic and copies ran while one was open for 0% of the time, Pallas kernels for 5%

profile of v9, /device:TPU:1, one launch (start us, length us, event | category | flops | bytes accessed | tf_op | source)
XLA Modules:
  0.0 85.9 jit_solution(2869051385914018588)
XLA Ops:
  1.3 0.0 copy-start.1
  1.3 0.0 copy-start.2
  1.3 0.0 copy-start.3
  1.3 2.7 %slab_ends.1 = f32[400,128]{1,0:T(8,128)} custom-call(s32[1,4]{1,0:T(1,128)} %starts_ref.1, s32[1]{0:T(128)S(6)} %copy.18.star_hbm.star_ref, f32[1,128]{1,0:T(1,128)} %times_ref.1, bf16[1,128,1536]{2,1,0:T(8,128)(2,1)} %series_ref.1, bf16[1,128,1536]{2,1,0:T(8,128)(2,1)} %cot_ref.3, bf16[1536,128]{1,0:T(8,128)(2,1)} %w_ref.3, f32[16,1536]{1,0:T(8,128)} %table_ref.1, ...), custom_call_target="tpu_custom_call" | custom-call | tf_op jit(solution)/shard_map/slab_ends/pallas_call | solution.py:314
  4.0 0.0 copy-start
  4.0 0.0 copy-start.4
  4.0 16.3 %all-to-all-start = ((f32[16,1,3200]{2,1,0:T(1,128)}), f32[16,1,3200]{2,1,0:T(1,128)S(1)}, u32[]{:S(2)}, u32[]{:S(2)}) async-start(f32[16,1,3200]{2,1,0:T(1,128)} %bitcast.18), calls=%async_computation | async-start | bytes 409600 | tf_op jit(solution)/shard_map/all_to_all | solution.py:327
  20.4 0.0 copy-done.4
  20.4 0.0 copy-start.5
  20.4 0.0 copy-start.6
  20.5 0.0 copy-done.1
  20.5 0.0 copy-done.2
  20.5 0.0 copy-done.3
  20.5 0.0 copy-done
  20.5 0.6 copy-done.5
  21.1 0.0 copy-done.6
  21.1 2.6 %local_scans.1 = (f32[1536,128]{1,0:T(8,128)S(1)}, bf16[1536,128]{1,0:T(8,128)(2,1)S(1)}, f32[12,16,128]{2,1,0:T(8,128)S(1)}, f32[2,128,128]{2,1,0:T(8,128)S(1)}) custom-call(s32[1,4]{1,0:T(1,128)S(1)} %copy-done.5, s32[1]{0:T(128)S(6)} %copy.18.star_hbm.star_ref, f32[1,128]{1,0:T(1,128)S(1)} %copy-done.6, bf16[1,128,1536]{2,1,0:T(8,128)(2,1)S(1)} %copy-done.2, ...), custom_call_target="tpu_custom_call" | custom-call | flops 20000000 | bytes 4000000 | tf_op jit(solution)/shard_map/local_scans/pallas_call | solution.py:328
  23.7 8.6 %all-to-all-done = f32[16,1,3200]{2,1,0:T(1,128)S(1)} async-done(((f32[16,1,3200]{2,1,0:T(1,128)}), f32[16,1,3200]{2,1,0:T(1,128)S(1)}, u32[]{:S(2)}, u32[]{:S(2)}) %all-to-all-start) | async-done | bytes 204832 | tf_op jit(solution)/shard_map/all_to_all | solution.py:327
  32.4 3.9 %all-gather = f32[32,1,3200]{2,1,0:T(1,128)S(1)} all-gather(f32[16,1,3200]{2,1,0:T(1,128)S(1)} %all-to-all-done), channel_id=2, replica_groups=mesh['x'=4,'zl'=4,'yh'=4,'yl'=2,'zh'=2,'core'=2] {'core'}, dimensions={0}, use_global_device_ids=true | all-gather | bytes 614400 | tf_op jit(solution)/shard_map/all_gather | solution.py:327
  36.3 0.8 gradients.1
  37.1 2.4 %all-gather.1 = f32[1600,128]{1,0:T(8,128)S(1)} all-gather(f32[800,128]{1,0:T(8,128)S(1)} %get-tuple-element.20), channel_id=3, replica_groups=mesh['x'=4,'zl'=4,'yh'=4,'yl'=2,'zh'=2,'core'=2] {'core'}, dimensions={0}, use_global_device_ids=true | all-gather | bytes 1228800 | tf_op jit(solution)/shard_map/all_gather | solution.py:352
  39.5 0.1 pair_sum.1
  39.6 19.7 %all_to_all.15 = f32[16,1,6400]{2,1,0:T(1,128)S(1)} all-to-all(f32[16,1,6400]{2,1,0:T(1,128)S(1)} %bitcast.13), channel_id=1, replica_groups=mesh['x'=4,'zl'=4,'yh'=4,'yl'=2,'zh'=2,'core'=2] {'x','zl'}, dimensions={0} | all-to-all | bytes 819200 | tf_op jit(solution)/shard_map/all_to_all | solution.py:372
  59.3 0.9 %sum_pieces.1 = f32[912,128]{1,0:T(8,128)} custom-call(f32[800,128]{1,0:T(8,128)S(1)} %bitcast.14), custom_call_target="tpu_custom_call" | custom-call | tf_op jit(solution)/shard_map/sum_pieces/pallas_call | solution.py:373
  60.2 4.1 %all-to-all-start.2 = ((f32[16,1,7296]{2,1,0:T(1,128)}), f32[16,1,7296]{2,1,0:T(1,128)S(1)}, u32[]{:S(2)}, u32[]{:S(2)}) async-start(f32[16,1,7296]{2,1,0:T(1,128)} %bitcast.6), calls=%async_computation.2 | async-start | bytes 933888 | tf_op jit(solution)/shard_map/all_to_all | solution.py:381
  64.3 1.8 %series_gradient.1 = bf16[1,128,1536]{2,1,0:T(8,128)(2,1)} custom-call(bf16[1536,128]{1,0:T(8,128)(2,1)S(1)} %get-tuple-element.18.low_ref, bf16[1,128,1536]{2,1,0:T(8,128)(2,1)S(1)} %copy-done, bf16[1536,128]{1,0:T(8,128)(2,1)S(1)} %copy-done.1), custom_call_target="tpu_custom_call" | custom-call | flops 100000000 | bytes 1600000 | tf_op jit(solution)/shard_map/series_gradient/pallas_call | solution.py:362
  66.0 14.0 %all-to-all-done.2 = f32[16,1,7296]{2,1,0:T(1,128)S(1)} async-done(((f32[16,1,7296]{2,1,0:T(1,128)}), f32[16,1,7296]{2,1,0:T(1,128)S(1)}, u32[]{:S(2)}, u32[]{:S(2)}) %all-to-all-start.2) | async-done | bytes 466976 | tf_op jit(solution)/shard_map/all_to_all | solution.py:381
  80.0 5.2 %all-gather.2 = f32[32,1,7296]{2,1,0:T(1,128)S(1)} all-gather(f32[16,1,7296]{2,1,0:T(1,128)S(1)} %all-to-all-done.2), channel_id=4, replica_groups=mesh['x'=4,'zl'=4,'yh'=4,'yl'=2,'zh'=2,'core'=2] {'core'}, dimensions={0}, use_global_device_ids=true | all-gather | bytes 1400832 | tf_op jit(solution)/shard_map/all_gather | solution.py:382
  85.3 0.7 outputs.1
  (1 shorter events, 0.0 us)
Async XLA Ops:
  1.3 19.2 %copy-start.1 = (bf16[1536,128]{1,0:T(8,128)(2,1)S(1)}, bf16[1536,128]{1,0:T(8,128)(2,1)}, u32[]{:S(2)}) copy-start(bf16[1536,128]{1,0:T(8,128)(2,1)} %w_ref.3) | copy-start | bytes 1179652
  1.3 19.2 %copy-start.2 = (bf16[1,128,1536]{2,1,0:T(8,128)(2,1)S(1)}, bf16[1,128,1536]{2,1,0:T(8,128)(2,1)}, u32[]{:S(2)}) copy-start(bf16[1,128,1536]{2,1,0:T(8,128)(2,1)} %series_ref.1) | copy-start | bytes 1179652
  1.3 19.2 %copy-start.3 = (f32[16,1536]{1,0:T(8,128)S(1)}, f32[16,1536]{1,0:T(8,128)}, u32[]{:S(2)}) copy-start(f32[16,1536]{1,0:T(8,128)} %table_ref.1) | copy-start | bytes 294916
  4.0 16.5 %copy-start = (bf16[1,128,1536]{2,1,0:T(8,128)(2,1)S(1)}, bf16[1,128,1536]{2,1,0:T(8,128)(2,1)}, u32[]{:S(2)}) copy-start(bf16[1,128,1536]{2,1,0:T(8,128)(2,1)} %cot_ref.3) | copy-start | bytes 1179652
  4.0 16.4 %copy-start.4 = (f32[1536]{0:T(1024)S(1)}, f32[1536]{0:T(1024)}, u32[]{:S(2)}) copy-start(f32[1536]{0:T(1024)} %param.15) | copy-start | bytes 18436
  4.0 28.3 %all-to-all-start = ((f32[16,1,3200]{2,1,0:T(1,128)}), f32[16,1,3200]{2,1,0:T(1,128)S(1)}, u32[]{:S(2)}, u32[]{:S(2)}) async-start(f32[16,1,3200]{2,1,0:T(1,128)} %bitcast.18), calls=%async_computation | async-start | bytes 409600 | tf_op jit(solution)/shard_map/all_to_all | solution.py:327
  20.4 0.7 copy-start.5
  20.4 0.7 copy-start.6
  60.2 19.8 %all-to-all-start.2 = ((f32[16,1,7296]{2,1,0:T(1,128)}), f32[16,1,7296]{2,1,0:T(1,128)S(1)}, u32[]{:S(2)}, u32[]{:S(2)}) async-start(f32[16,1,7296]{2,1,0:T(1,128)} %bitcast.6), calls=%async_computation.2 | async-start | bytes 933888 | tf_op jit(solution)/shard_map/all_to_all | solution.py:381

commit v10 on v8

--- a/solution.py
+++ b/solution.py
@@ -12,7 +12,7 @@
 STEPS = SLAB // CHUNKS
 FAR = 1e9
 CARRY = 25
-SHARE = 29
+SHARE = 28
 PIECE = 26
 F32 = jnp.float32
 BF16 = jnp.bfloat16
@@ -36,19 +36,19 @@
 
 
 def ends_kernel(
-    blocks, chips, starts_hbm, star_hbm, times_hbm, series_hbm, cot_hbm, w_hbm, table_hbm, lograte_hbm,
-    out_ref, ends_ref, starts_ref, star_ref, times_ref, series_ref, cot_ref, w_ref, table_ref, lograte_ref, sems, load_sems,
+    blocks, chips, star_ref, starts_hbm, times_hbm, series_hbm, cot_hbm, w_hbm, table_hbm, lograte_hbm,
+    out_ref, ends_ref, starts_ref, times_ref, series_ref, cot_ref, w_ref, table_ref, lograte_ref, sems, load_sems,
 ):
-    sources = (starts_hbm, star_hbm, times_hbm, table_hbm, lograte_hbm)
-    targets = (starts_ref, star_ref, times_ref, table_ref, lograte_ref)
+    sources = (starts_hbm, times_hbm, table_hbm.at[pl.ds(star_ref[0], 1)], lograte_hbm)
+    targets = (starts_ref, times_ref, table_ref, lograte_ref)
     copies = [pltpu.make_async_copy(a, b, sems.at[k]) for k, (a, b) in enumerate(zip(sources, targets))]
     sources, targets = (series_hbm, w_hbm, cot_hbm), (series_ref, w_ref, cot_ref)
     loads = [pltpu.make_async_copy(a, b, load_sems.at[k]) for k, (a, b) in enumerate(zip(sources, targets))]
-    for copy in copies[:3] + loads + copies[3:]:
+    for copy in copies[:2] + loads + copies[2:]:
         copy.start()
     core = lax.axis_index("core")
     me = slab_index()
-    for copy in copies[:3]:
+    for copy in copies[:2]:
         copy.wait()
     elapsed = elapsed_row(starts_ref, times_ref, me)
     row = lax.broadcasted_iota(jnp.int32, (SLAB, SLAB), 0)
@@ -59,9 +59,9 @@
     to_end = jnp.broadcast_to(to_end, (SLAB, LANES))
     from_start = jnp.broadcast_to(from_start, (SLAB, LANES))
     total = jnp.sum(elapsed, axis=1, keepdims=True)
-    for copy in copies[3:] + loads:
+    for copy in copies[2:] + loads:
         copy.wait()
-    bias = table_ref[pl.ds(star_ref[0], 1), :]
+    bias = table_ref[...]
     for h in range(blocks):
         cols = slice(h * LANES, (h + 1) * LANES)
         proj = jnp.dot(series_ref[0, :, cols], w_ref[cols, :], preferred_element_type=F32) + bias[:, cols]
@@ -276,10 +276,13 @@
     hits = [star == (first + k).astype(F32) for k in range(4)]
     stars = [jnp.sum(jnp.where(hit, terms, 0.0), axis=0, keepdims=True) for hit in hits]
     total = total * norm
-    tail = jnp.concatenate(stars + [logs], axis=0) * norm
+    lane = lax.broadcasted_iota(jnp.int32, (1, LANES), 1)
+    spare = LANES - share
+    stars = [jnp.where(lane < share, row, pltpu.roll(logs, (share - k * spare) % LANES, 1)) for k, row in enumerate(stars)]
+    tail = jnp.concatenate(stars, axis=0) * norm
     for d in range(out_ref.shape[0] // SHARE):
         out_ref[d * SHARE : d * SHARE + 24, :] = total
-        out_ref[d * SHARE + 24 : d * SHARE + 29, :] = tail
+        out_ref[d * SHARE + 24 : d * SHARE + 28, :] = tail
 
 
 def final_kernel(got_ref, weight_ref, star_ref, log_ref):
@@ -295,7 +298,13 @@
             weight_ref[q * 24 : q * 24 + 24, :] = total[0:24, :]
             star_ref[q * 4 : q * 4 + 4, :] = total[24:28, 0:share]
             if q == 0:
-                log_ref[...] = total[28:29, 0:share]
+                logs = total[24:25, :]
+                lane = lax.broadcasted_iota(jnp.int32, (1, LANES), 1)
+                spare = LANES - share
+                for k in range(4):
+                    row = pltpu.roll(total[24 + k : 25 + k, :], (k * spare - share) % LANES, 1)
+                    logs = jnp.where(lane // spare == k, row, logs)
+                log_ref[...] = logs[:, 0:share]
 
 
 def body(series, cotangent, step_times, seg_starts, star_of_row, block_weight, star_table, log_rate):
@@ -317,15 +326,16 @@
     ends = pl.pallas_call(
         functools.partial(ends_kernel, blocks, chips),
         out_shape=shape((chips * CARRY, LANES), F32),
-        in_specs=[hbm] * 8,
+        in_specs=[smem] + [hbm] * 7,
         out_specs=vmem,
         scratch_shapes=[pltpu.VMEM((2, 32, LANES), F32)]
-        + [pltpu.SMEM(v.shape, v.dtype) for v in common[:2]]
-        + [pltpu.VMEM(v.shape, v.dtype) for v in common[2:]]
-        + [pltpu.SemaphoreType.DMA((5,)), pltpu.SemaphoreType.DMA((3,))],
+        + [pltpu.SMEM(seg_starts.shape, jnp.int32)]
+        + [pltpu.VMEM(v.shape, v.dtype) for v in (step_times, series, cotangent, block_weight)]
+        + [pltpu.VMEM((1, width), F32), pltpu.VMEM(log_blocks.shape, F32)]
+        + [pltpu.SemaphoreType.DMA((4,)), pltpu.SemaphoreType.DMA((3,))],
         compiler_params=big,
         name="slab_ends",
-    )(*common)
+    )(star_of_row, seg_starts, *common[2:])
     ends = ends.reshape(chips, 1, CARRY * LANES)
     got = lax.all_gather(lax.all_to_all(ends, ("zh", "yh", "yl"), 0, 0), "core").reshape(slabs * CARRY, LANES)
     base, xt, sums, reach = pl.pallas_call(

time: 83.2 us -> 82.9 us (level)
  no operation moved by 1% of the time
where the time goes in v10:
time: 82.9 us; the launch traced here: 82.5 us
  blocking collectives  32.4 us (39%)
  starting transfers between devices  20.1 us (24%)
  waiting for transfers between devices  18.5 us (22%)
  Pallas kernels  9.47 us (11%)
  between operations  1.43 us (2%)
    all_to_all x1, blocking collectives, body(): lax.all_to_all(pair, ('x', 'zl', 'yl'), 0, 0)  20.3 us
    all_to_all x1, starting transfers between devices, body(): lax.all_to_all(ends, ('zh', 'yh', 'yl'), 0, 0)  16.3 us
    all_to_all x1, waiting for transfers between devices, body(): lax.all_to_all(piece.reshape(chips, 1, SHARE * LANES), ('zh', 'yh', 'yl')...  9.84 us
    all_to_all x1, waiting for transfers between devices, body(): lax.all_to_all(ends, ('zh', 'yh', 'yl'), 0, 0)  8.64 us
    all_gather x1, blocking collectives, body(): both = lax.all_gather(spread, 'core').reshape(slabs * SHARE, LANES)  5.8 us
    all_gather x1, blocking collectives, body(): lax.all_gather(lax.all_to_all(ends, ('zh', 'yh', 'yl'), 0, 0), 'core')  3.91 us
    all_to_all x1, starting transfers between devices, body(): lax.all_to_all(piece.reshape(chips, 1, SHARE * LANES), ('zh', 'yh', 'yl')...  3.73 us
    pallas_call x1, Pallas kernels, body(): pl.pallas_call(functools.partial(ends_kernel, blocks, chips), out_shape=s...  2.69 us
  transfers between devices with their start and end apart: 2, of which 2 were waited for; matrix products, arithmetic and copies ran while one was open for 0% of the time, Pallas kernels for 5%

profile of v10, /device:TPU:1, one launch (start us, length us, event | category | flops | bytes accessed | tf_op | source)
XLA Modules:
  0.0 82.5 jit_solution(16307987047056135279)
XLA Ops:
  1.3 0.0 copy-start.1
  1.3 0.0 copy-start.2
  1.3 0.0 copy-start.3
  1.3 2.7 %slab_ends.1 = f32[400,128]{1,0:T(8,128)} custom-call(s32[1]{0:T(128)S(6)} %copy.18.star_ref, s32[1,4]{1,0:T(1,128)} %starts_ref.1, f32[1,128]{1,0:T(1,128)} %times_ref.1, bf16[1,128,1536]{2,1,0:T(8,128)(2,1)} %series_ref.1, bf16[1,128,1536]{2,1,0:T(8,128)(2,1)} %cot_ref.3, bf16[1536,128]{1,0:T(8,128)(2,1)} %w_ref.3, f32[16,1536]{1,0:T(8,128)} %table_ref.1, ...), custom_call_target="tpu_custom_call" | custom-call | tf_op jit(solution)/shard_map/slab_ends/pallas_call | solution.py:326
  4.0 0.0 copy-start
  4.0 0.0 copy-start.4
  4.0 16.3 %all-to-all-start = ((f32[16,1,3200]{2,1,0:T(1,128)}), f32[16,1,3200]{2,1,0:T(1,128)S(1)}, u32[]{:S(2)}, u32[]{:S(2)}) async-start(f32[16,1,3200]{2,1,0:T(1,128)} %bitcast.18), calls=%async_computation | async-start | bytes 409600 | tf_op jit(solution)/shard_map/all_to_all | solution.py:340
  20.4 0.0 copy-done.4
  20.4 0.0 copy-start.5
  20.4 0.0 copy-start.6
  20.4 0.0 copy-done.1
  20.5 0.0 copy-done.2
  20.5 0.0 copy-done.3
  20.5 0.0 copy-done
  20.5 0.6 copy-done.5
  21.1 0.0 copy-done.6
  21.1 2.6 %local_scans.1 = (f32[1536,128]{1,0:T(8,128)S(1)}, bf16[1536,128]{1,0:T(8,128)(2,1)S(1)}, f32[12,16,128]{2,1,0:T(8,128)S(1)}, f32[2,128,128]{2,1,0:T(8,128)S(1)}) custom-call(s32[1,4]{1,0:T(1,128)S(1)} %copy-done.5, s32[1]{0:T(128)S(6)} %copy.18.star_ref, f32[1,128]{1,0:T(1,128)S(1)} %copy-done.6, bf16[1,128,1536]{2,1,0:T(8,128)(2,1)S(1)} %copy-done.2, ...), custom_call_target="tpu_custom_call" | custom-call | flops 20000000 | bytes 4000000 | tf_op jit(solution)/shard_map/local_scans/pallas_call | solution.py:341
  23.7 8.6 %all-to-all-done = f32[16,1,3200]{2,1,0:T(1,128)S(1)} async-done(((f32[16,1,3200]{2,1,0:T(1,128)}), f32[16,1,3200]{2,1,0:T(1,128)S(1)}, u32[]{:S(2)}, u32[]{:S(2)}) %all-to-all-start) | async-done | bytes 204832 | tf_op jit(solution)/shard_map/all_to_all | solution.py:340
  32.4 3.9 %all-gather = f32[32,1,3200]{2,1,0:T(1,128)S(1)} all-gather(f32[16,1,3200]{2,1,0:T(1,128)S(1)} %all-to-all-done), channel_id=2, replica_groups=mesh['x'=4,'zl'=4,'yh'=4,'yl'=2,'zh'=2,'core'=2] {'core'}, dimensions={0}, use_global_device_ids=true | all-gather | bytes 614400 | tf_op jit(solution)/shard_map/all_gather | solution.py:340
  36.3 0.8 gradients.1
  37.1 2.4 %all-gather.1 = f32[1600,128]{1,0:T(8,128)S(1)} all-gather(f32[800,128]{1,0:T(8,128)S(1)} %get-tuple-element.20), channel_id=3, replica_groups=mesh['x'=4,'zl'=4,'yh'=4,'yl'=2,'zh'=2,'core'=2] {'core'}, dimensions={0}, use_global_device_ids=true | all-gather | bytes 1228800 | tf_op jit(solution)/shard_map/all_gather | solution.py:365
  39.5 0.1 pair_sum.1
  39.6 20.3 %all_to_all.15 = f32[32,1,3328]{2,1,0:T(1,128)S(1)} all-to-all(f32[32,1,3328]{2,1,0:T(1,128)S(1)} %bitcast.13), channel_id=1, replica_groups=mesh['x'=4,'zl'=4,'yh'=4,'yl'=2,'zh'=2,'core'=2] {'x','zl','yl'}, dimensions={0} | all-to-all | bytes 851968 | tf_op jit(solution)/shard_map/all_to_all | solution.py:385
  59.9 0.8 sum_pieces.1
  60.7 3.7 %all-to-all-start.2 = ((f32[16,1,3584]{2,1,0:T(1,128)}), f32[16,1,3584]{2,1,0:T(1,128)S(1)}, u32[]{:S(2)}, u32[]{:S(2)}) async-start(f32[16,1,3584]{2,1,0:T(1,128)} %bitcast.6), calls=%async_computation.2 | async-start | bytes 458752 | tf_op jit(solution)/shard_map/all_to_all | solution.py:394
  64.4 1.8 %series_gradient.1 = bf16[1,128,1536]{2,1,0:T(8,128)(2,1)} custom-call(bf16[1536,128]{1,0:T(8,128)(2,1)S(1)} %get-tuple-element.18.low_ref, bf16[1,128,1536]{2,1,0:T(8,128)(2,1)S(1)} %copy-done, bf16[1536,128]{1,0:T(8,128)(2,1)S(1)} %copy-done.1), custom_call_target="tpu_custom_call" | custom-call | flops 100000000 | bytes 1600000 | tf_op jit(solution)/shard_map/series_gradient/pallas_call | solution.py:375
  66.2 9.8 %all-to-all-done.2 = f32[16,1,3584]{2,1,0:T(1,128)S(1)} async-done(((f32[16,1,3584]{2,1,0:T(1,128)}), f32[16,1,3584]{2,1,0:T(1,128)S(1)}, u32[]{:S(2)}, u32[]{:S(2)}) %all-to-all-start.2) | async-done | bytes 229408 | tf_op jit(solution)/shard_map/all_to_all | solution.py:394
  76.0 5.8 %all-gather.2 = f32[32,1,3584]{2,1,0:T(1,128)S(1)} all-gather(f32[16,1,3584]{2,1,0:T(1,128)S(1)} %all-to-all-done.2), channel_id=4, replica_groups=mesh['x'=4,'zl'=4,'yh'=4,'yl'=2,'zh'=2,'core'=2] {'core'}, dimensions={0}, use_global_device_ids=true | all-gather | bytes 688128 | tf_op jit(solution)/shard_map/all_gather | solution.py:395
  81.8 0.7 outputs.1
  (1 shorter events, 0.0 us)
Async XLA Ops:
  1.3 19.2 %copy-start.1 = (bf16[1536,128]{1,0:T(8,128)(2,1)S(1)}, bf16[1536,128]{1,0:T(8,128)(2,1)}, u32[]{:S(2)}) copy-start(bf16[1536,128]{1,0:T(8,128)(2,1)} %w_ref.3) | copy-start | bytes 1179652
  1.3 19.2 %copy-start.2 = (bf16[1,128,1536]{2,1,0:T(8,128)(2,1)S(1)}, bf16[1,128,1536]{2,1,0:T(8,128)(2,1)}, u32[]{:S(2)}) copy-start(bf16[1,128,1536]{2,1,0:T(8,128)(2,1)} %series_ref.1) | copy-start | bytes 1179652
  1.3 19.2 %copy-start.3 = (f32[16,1536]{1,0:T(8,128)S(1)}, f32[16,1536]{1,0:T(8,128)}, u32[]{:S(2)}) copy-start(f32[16,1536]{1,0:T(8,128)} %table_ref.1) | copy-start | bytes 294916
  4.0 16.5 %copy-start = (bf16[1,128,1536]{2,1,0:T(8,128)(2,1)S(1)}, bf16[1,128,1536]{2,1,0:T(8,128)(2,1)}, u32[]{:S(2)}) copy-start(bf16[1,128,1536]{2,1,0:T(8,128)(2,1)} %cot_ref.3) | copy-start | bytes 1179652
  4.0 16.4 %copy-start.4 = (f32[1536]{0:T(1024)S(1)}, f32[1536]{0:T(1024)}, u32[]{:S(2)}) copy-start(f32[1536]{0:T(1024)} %param.15) | copy-start | bytes 18436
  4.0 28.3 %all-to-all-start = ((f32[16,1,3200]{2,1,0:T(1,128)}), f32[16,1,3200]{2,1,0:T(1,128)S(1)}, u32[]{:S(2)}, u32[]{:S(2)}) async-start(f32[16,1,3200]{2,1,0:T(1,128)} %bitcast.18), calls=%async_computation | async-start | bytes 409600 | tf_op jit(solution)/shard_map/all_to_all | solution.py:340
  20.4 0.7 copy-start.5
  20.4 0.7 copy-start.6
  60.7 15.3 %all-to-all-start.2 = ((f32[16,1,3584]{2,1,0:T(1,128)}), f32[16,1,3584]{2,1,0:T(1,128)S(1)}, u32[]{:S(2)}, u32[]{:S(2)}) async-start(f32[16,1,3584]{2,1,0:T(1,128)} %bitcast.6), calls=%async_computation.2 | async-start | bytes 458752 | tf_op jit(solution)/shard_map/all_to_all | solution.py:394

commit v11 on v10

--- a/solution.py
+++ b/solution.py
@@ -383,6 +383,7 @@
     )(low, cotangent, block_weight)
     pair = pair.reshape(rows_dp * 2, 1, PIECE * LANES)
     pieces = lax.all_to_all(pair, ("x", "zl", "yl"), 0, 0).reshape(rows_dp * 2 * PIECE, LANES)
+    pieces, grad_series = lax.optimization_barrier((pieces, grad_series))
     piece = pl.pallas_call(
         functools.partial(piece_kernel, norm, width // rows_dp),
         out_shape=shape((chips * SHARE, LANES), F32),

time: 82.9 us -> 83 us (level)
  blocking collectives: 32.4 us -> 27.2 us
  starting transfers between devices: 20.1 us -> 24.9 us
    all_to_all x1, blocking collectives: 20.3 us -> 15.1 us  [body(): lax.all_to_all(piece.reshape(chips, 1, SHARE * LANES), ('zh', 'yh', 'yl')...]
    all_to_all x1, starting transfers between devices: 3.73 us -> 8.55 us  [body(): lax.all_to_all(pair, ('x', 'zl', 'yl'), 0, 0)]
where the time goes in v11:
time: 83 us; the launch traced here: 82.5 us
  blocking collectives  27.2 us (33%)
  starting transfers between devices  24.9 us (30%)
  waiting for transfers between devices  18.8 us (23%)
  Pallas kernels  9.51 us (11%)
  between operations  1.42 us (2%)
    all_to_all x1, starting transfers between devices, body(): lax.all_to_all(ends, ('zh', 'yh', 'yl'), 0, 0)  16.3 us
    all_to_all x1, blocking collectives, body(): lax.all_to_all(piece.reshape(chips, 1, SHARE * LANES), ('zh', 'yh', 'yl')...  15.1 us
    all_to_all x1, waiting for transfers between devices, body(): lax.all_to_all(pair, ('x', 'zl', 'yl'), 0, 0)  10.2 us
    all_to_all x1, waiting for transfers between devices, body(): lax.all_to_all(ends, ('zh', 'yh', 'yl'), 0, 0)  8.64 us
    all_to_all x1, starting transfers between devices, body(): lax.all_to_all(pair, ('x', 'zl', 'yl'), 0, 0)  8.55 us
    all_gather x1, blocking collectives, body(): both = lax.all_gather(spread, 'core').reshape(slabs * SHARE, LANES)  5.86 us
    all_gather x1, blocking collectives, body(): lax.all_gather(lax.all_to_all(ends, ('zh', 'yh', 'yl'), 0, 0), 'core')  3.91 us
    pallas_call x1, Pallas kernels, body(): pl.pallas_call(functools.partial(ends_kernel, blocks, chips), out_shape=s...  2.69 us
  transfers between devices with their start and end apart: 2, of which 2 were waited for; matrix products, arithmetic and copies ran while one was open for 0% of the time, Pallas kernels for 5%

profile of v11, /device:TPU:1, one launch (start us, length us, event | category | flops | bytes accessed | tf_op | source)
XLA Modules:
  0.0 82.5 jit_solution(18411515137647558307)
XLA Ops:
  1.3 0.0 copy-start.1
  1.3 0.0 copy-start.2
  1.3 0.0 copy-start.3
  1.3 2.7 %slab_ends.1 = f32[400,128]{1,0:T(8,128)} custom-call(s32[1]{0:T(128)S(6)} %copy.18.star_ref, s32[1,4]{1,0:T(1,128)} %starts_ref.1, f32[1,128]{1,0:T(1,128)} %times_ref.1, bf16[1,128,1536]{2,1,0:T(8,128)(2,1)} %series_ref.1, bf16[1,128,1536]{2,1,0:T(8,128)(2,1)} %cot_ref.3, bf16[1536,128]{1,0:T(8,128)(2,1)} %w_ref.3, f32[16,1536]{1,0:T(8,128)} %table_ref.1, ...), custom_call_target="tpu_custom_call" | custom-call | tf_op jit(solution)/shard_map/slab_ends/pallas_call | solution.py:326
  4.0 0.0 copy-start
  4.0 0.0 copy-start.4
  4.0 16.3 %all-to-all-start = ((f32[16,1,3200]{2,1,0:T(1,128)}), f32[16,1,3200]{2,1,0:T(1,128)S(1)}, u32[]{:S(2)}, u32[]{:S(2)}) async-start(f32[16,1,3200]{2,1,0:T(1,128)} %bitcast.18), calls=%async_computation | async-start | bytes 409600 | tf_op jit(solution)/shard_map/all_to_all | solution.py:340
  20.4 0.0 copy-done.4
  20.4 0.0 copy-start.5
  20.4 0.0 copy-start.6
  20.4 0.0 copy-done.1
  20.5 0.0 copy-done.2
  20.5 0.0 copy-done.3
  20.5 0.0 copy-done
  20.5 0.6 copy-done.5
  21.1 0.0 copy-done.6
  21.1 2.6 %local_scans.1 = (f32[1536,128]{1,0:T(8,128)S(1)}, bf16[1536,128]{1,0:T(8,128)(2,1)S(1)}, f32[12,16,128]{2,1,0:T(8,128)S(1)}, f32[2,128,128]{2,1,0:T(8,128)S(1)}) custom-call(s32[1,4]{1,0:T(1,128)S(1)} %copy-done.5, s32[1]{0:T(128)S(6)} %copy.18.star_ref, f32[1,128]{1,0:T(1,128)S(1)} %copy-done.6, bf16[1,128,1536]{2,1,0:T(8,128)(2,1)S(1)} %copy-done.2, ...), custom_call_target="tpu_custom_call" | custom-call | flops 20000000 | bytes 4000000 | tf_op jit(solution)/shard_map/local_scans/pallas_call | solution.py:341
  23.7 8.6 %all-to-all-done = f32[16,1,3200]{2,1,0:T(1,128)S(1)} async-done(((f32[16,1,3200]{2,1,0:T(1,128)}), f32[16,1,3200]{2,1,0:T(1,128)S(1)}, u32[]{:S(2)}, u32[]{:S(2)}) %all-to-all-start) | async-done | bytes 204832 | tf_op jit(solution)/shard_map/all_to_all | solution.py:340
  32.4 3.9 %all-gather = f32[32,1,3200]{2,1,0:T(1,128)S(1)} all-gather(f32[16,1,3200]{2,1,0:T(1,128)S(1)} %all-to-all-done), channel_id=2, replica_groups=mesh['x'=4,'zl'=4,'yh'=4,'yl'=2,'zh'=2,'core'=2] {'core'}, dimensions={0}, use_global_device_ids=true | all-gather | bytes 614400 | tf_op jit(solution)/shard_map/all_gather | solution.py:340
  36.3 0.8 gradients.1
  37.1 2.4 %all-gather.1 = f32[1600,128]{1,0:T(8,128)S(1)} all-gather(f32[800,128]{1,0:T(8,128)S(1)} %get-tuple-element.21), channel_id=3, replica_groups=mesh['x'=4,'zl'=4,'yh'=4,'yl'=2,'zh'=2,'core'=2] {'core'}, dimensions={0}, use_global_device_ids=true | all-gather | bytes 1228800 | tf_op jit(solution)/shard_map/all_gather | solution.py:365
  39.5 0.9 %pair_sum.1 = f32[832,128]{1,0:T(8,128)} custom-call(s32[1]{0:T(128)S(6)} %copy.18.star_ref, f32[800,128]{1,0:T(8,128)S(1)} %get-tuple-element.20.keep_ref, f32[2,800,128]{2,1,0:T(8,128)S(1)} %bitcast.10), custom_call_target="tpu_custom_call" | custom-call | tf_op jit(solution)/shard_map/pair_sum/pallas_call | solution.py:366
  40.3 8.5 %all-to-all-start.1 = ((f32[32,1,3328]{2,1,0:T(1,128)}), f32[32,1,3328]{2,1,0:T(1,128)S(1)}, u32[]{:S(2)}, u32[]{:S(2)}) async-start(f32[32,1,3328]{2,1,0:T(1,128)} %bitcast.4), calls=%async_computation.1 | async-start | bytes 851968 | tf_op jit(solution)/shard_map/all_to_all | solution.py:385
  48.9 1.8 %series_gradient.1 = bf16[1,128,1536]{2,1,0:T(8,128)(2,1)} custom-call(bf16[1536,128]{1,0:T(8,128)(2,1)S(1)} %get-tuple-element.22.low_ref, bf16[1,128,1536]{2,1,0:T(8,128)(2,1)S(1)} %copy-done, bf16[1536,128]{1,0:T(8,128)(2,1)S(1)} %copy-done.1), custom_call_target="tpu_custom_call" | custom-call | flops 100000000 | bytes 1600000 | tf_op jit(solution)/shard_map/series_gradient/pallas_call | solution.py:375
  50.7 10.2 %all-to-all-done.1 = f32[32,1,3328]{2,1,0:T(1,128)S(1)} async-done(((f32[32,1,3328]{2,1,0:T(1,128)}), f32[32,1,3328]{2,1,0:T(1,128)S(1)}, u32[]{:S(2)}, u32[]{:S(2)}) %all-to-all-start.1) | async-done | bytes 426016 | tf_op jit(solution)/shard_map/all_to_all | solution.py:385
  60.8 0.1 sum_pieces.1
  60.9 15.1 %all_to_all.15 = f32[16,1,3584]{2,1,0:T(1,128)S(1)} all-to-all(f32[16,1,3584]{2,1,0:T(1,128)S(1)} %bitcast.14), channel_id=1, replica_groups=mesh['x'=4,'zl'=4,'yh'=4,'yl'=2,'zh'=2,'core'=2] {'zh','yh','yl'}, dimensions={0} | all-to-all | bytes 458752 | tf_op jit(solution)/shard_map/all_to_all | solution.py:395
  76.0 5.9 %all-gather.2 = f32[32,1,3584]{2,1,0:T(1,128)S(1)} all-gather(f32[16,1,3584]{2,1,0:T(1,128)S(1)} %all_to_all.15), channel_id=4, replica_groups=mesh['x'=4,'zl'=4,'yh'=4,'yl'=2,'zh'=2,'core'=2] {'core'}, dimensions={0}, use_global_device_ids=true | all-gather | bytes 688128 | tf_op jit(solution)/shard_map/all_gather | solution.py:396
  81.8 0.7 outputs.1
  (1 shorter events, 0.0 us)
Async XLA Ops:
  1.3 19.2 %copy-start.1 = (bf16[1536,128]{1,0:T(8,128)(2,1)S(1)}, bf16[1536,128]{1,0:T(8,128)(2,1)}, u32[]{:S(2)}) copy-start(bf16[1536,128]{1,0:T(8,128)(2,1)} %w_ref.3) | copy-start | bytes 1179652
  1.3 19.2 %copy-start.2 = (bf16[1,128,1536]{2,1,0:T(8,128)(2,1)S(1)}, bf16[1,128,1536]{2,1,0:T(8,128)(2,1)}, u32[]{:S(2)}) copy-start(bf16[1,128,1536]{2,1,0:T(8,128)(2,1)} %series_ref.1) | copy-start | bytes 1179652
  1.3 19.2 %copy-start.3 = (f32[16,1536]{1,0:T(8,128)S(1)}, f32[16,1536]{1,0:T(8,128)}, u32[]{:S(2)}) copy-start(f32[16,1536]{1,0:T(8,128)} %table_ref.1) | copy-start | bytes 294916
  4.0 16.5 %copy-start = (bf16[1,128,1536]{2,1,0:T(8,128)(2,1)S(1)}, bf16[1,128,1536]{2,1,0:T(8,128)(2,1)}, u32[]{:S(2)}) copy-start(bf16[1,128,1536]{2,1,0:T(8,128)(2,1)} %cot_ref.3) | copy-start | bytes 1179652
  4.0 16.4 %copy-start.4 = (f32[1536]{0:T(1024)S(1)}, f32[1536]{0:T(1024)}, u32[]{:S(2)}) copy-start(f32[1536]{0:T(1024)} %param.15) | copy-start | bytes 18436
  4.0 28.3 %all-to-all-start = ((f32[16,1,3200]{2,1,0:T(1,128)}), f32[16,1,3200]{2,1,0:T(1,128)S(1)}, u32[]{:S(2)}, u32[]{:S(2)}) async-start(f32[16,1,3200]{2,1,0:T(1,128)} %bitcast.18), calls=%async_computation | async-start | bytes 409600 | tf_op jit(solution)/shard_map/all_to_all | solution.py:340
  20.4 0.7 copy-start.5
  20.4 0.7 copy-start.6
  40.3 20.5 %all-to-all-start.1 = ((f32[32,1,3328]{2,1,0:T(1,128)}), f32[32,1,3328]{2,1,0:T(1,128)S(1)}, u32[]{:S(2)}, u32[]{:S(2)}) async-start(f32[32,1,3328]{2,1,0:T(1,128)} %bitcast.4), calls=%async_computation.1 | async-start | bytes 851968 | tf_op jit(solution)/shard_map/all_to_all | solution.py:385

commit v12 on v11

--- a/solution.py
+++ b/solution.py
@@ -291,7 +291,7 @@
     for core in range(2):
         for yl in range(2):
             q = core * 2 + yl
-            parts = [(core * chips + chip) * SHARE for chip in range(chips) if chip % 2 == yl]
+            parts = [(core * chips + chip) * SHARE for chip in range(chips) if chip // 4 % 2 == yl]
             total = got_ref[parts[0] : parts[0] + SHARE, :]
             for at in parts[1:]:
                 total = total + got_ref[at : at + SHARE, :]
@@ -392,7 +392,7 @@
         compiler_params=params,
         name="sum_pieces",
     )(pieces)
-    spread = lax.all_to_all(piece.reshape(chips, 1, SHARE * LANES), ("zh", "yh", "yl"), 0, 0)
+    spread = lax.all_to_all(piece.reshape(chips, 1, SHARE * LANES), ("zh", "yl", "yh"), 0, 0)
     both = lax.all_gather(spread, "core").reshape(slabs * SHARE, LANES)
     share = width // rows_dp
     grad_weight, grad_star, grad_log = pl.pallas_call(

time: 83 us -> 83.3 us (level)
  no operation moved by 1% of the time
where the time goes in v12:
time: 83.3 us; the launch traced here: 82.8 us
  blocking collectives  27.6 us (33%)
  starting transfers between devices  24.9 us (30%)
  waiting for transfers between devices  18.8 us (23%)
  Pallas kernels  9.51 us (11%)
  between operations  1.42 us (2%)
    all_to_all x1, starting transfers between devices, body(): lax.all_to_all(ends, ('zh', 'yh', 'yl'), 0, 0)  16.3 us
    all_to_all x1, blocking collectives, body(): lax.all_to_all(piece.reshape(chips, 1, SHARE * LANES), ('zh', 'yl', 'yh')...  15.4 us
    all_to_all x1, waiting for transfers between devices, body(): lax.all_to_all(pair, ('x', 'zl', 'yl'), 0, 0)  10.2 us
    all_to_all x1, waiting for transfers between devices, body(): lax.all_to_all(ends, ('zh', 'yh', 'yl'), 0, 0)  8.64 us
    all_to_all x1, starting transfers between devices, body(): lax.all_to_all(pair, ('x', 'zl', 'yl'), 0, 0)  8.55 us
    all_gather x1, blocking collectives, body(): both = lax.all_gather(spread, 'core').reshape(slabs * SHARE, LANES)  5.93 us
    all_gather x1, blocking collectives, body(): lax.all_gather(lax.all_to_all(ends, ('zh', 'yh', 'yl'), 0, 0), 'core')  3.91 us
    pallas_call x1, Pallas kernels, body(): pl.pallas_call(functools.partial(ends_kernel, blocks, chips), out_shape=s...  2.69 us
  transfers between devices with their start and end apart: 2, of which 2 were waited for; matrix products, arithmetic and copies ran while one was open for 0% of the time, Pallas kernels for 5%

profile of v12, /device:TPU:1, one launch (start us, length us, event | category | flops | bytes accessed | tf_op | source)
XLA Modules:
  0.0 82.8 jit_solution(14912813690119348601)
XLA Ops:
  1.3 0.0 copy-start.1
  1.3 0.0 copy-start.2
  1.3 0.0 copy-start.3
  1.3 2.7 %slab_ends.1 = f32[400,128]{1,0:T(8,128)} custom-call(s32[1]{0:T(128)S(6)} %copy.18.star_ref, s32[1,4]{1,0:T(1,128)} %starts_ref.1, f32[1,128]{1,0:T(1,128)} %times_ref.1, bf16[1,128,1536]{2,1,0:T(8,128)(2,1)} %series_ref.1, bf16[1,128,1536]{2,1,0:T(8,128)(2,1)} %cot_ref.3, bf16[1536,128]{1,0:T(8,128)(2,1)} %w_ref.3, f32[16,1536]{1,0:T(8,128)} %table_ref.1, ...), custom_call_target="tpu_custom_call" | custom-call | tf_op jit(solution)/shard_map/slab_ends/pallas_call | solution.py:326
  4.0 0.0 copy-start
  4.0 0.0 copy-start.4
  4.0 16.3 %all-to-all-start = ((f32[16,1,3200]{2,1,0:T(1,128)}), f32[16,1,3200]{2,1,0:T(1,128)S(1)}, u32[]{:S(2)}, u32[]{:S(2)}) async-start(f32[16,1,3200]{2,1,0:T(1,128)} %bitcast.18), calls=%async_computation | async-start | bytes 409600 | tf_op jit(solution)/shard_map/all_to_all | solution.py:340
  20.4 0.0 copy-done.4
  20.4 0.0 copy-start.5
  20.4 0.0 copy-start.6
  20.4 0.0 copy-done.1
  20.5 0.0 copy-done.2
  20.5 0.0 copy-done.3
  20.5 0.0 copy-done
  20.5 0.6 copy-done.5
  21.1 0.0 copy-done.6
  21.1 2.6 %local_scans.1 = (f32[1536,128]{1,0:T(8,128)S(1)}, bf16[1536,128]{1,0:T(8,128)(2,1)S(1)}, f32[12,16,128]{2,1,0:T(8,128)S(1)}, f32[2,128,128]{2,1,0:T(8,128)S(1)}) custom-call(s32[1,4]{1,0:T(1,128)S(1)} %copy-done.5, s32[1]{0:T(128)S(6)} %copy.18.star_ref, f32[1,128]{1,0:T(1,128)S(1)} %copy-done.6, bf16[1,128,1536]{2,1,0:T(8,128)(2,1)S(1)} %copy-done.2, ...), custom_call_target="tpu_custom_call" | custom-call | flops 20000000 | bytes 4000000 | tf_op jit(solution)/shard_map/local_scans/pallas_call | solution.py:341
  23.7 8.6 %all-to-all-done = f32[16,1,3200]{2,1,0:T(1,128)S(1)} async-done(((f32[16,1,3200]{2,1,0:T(1,128)}), f32[16,1,3200]{2,1,0:T(1,128)S(1)}, u32[]{:S(2)}, u32[]{:S(2)}) %all-to-all-start) | async-done | bytes 204832 | tf_op jit(solution)/shard_map/all_to_all | solution.py:340
  32.4 3.9 %all-gather = f32[32,1,3200]{2,1,0:T(1,128)S(1)} all-gather(f32[16,1,3200]{2,1,0:T(1,128)S(1)} %all-to-all-done), channel_id=2, replica_groups=mesh['x'=4,'zl'=4,'yh'=4,'yl'=2,'zh'=2,'core'=2] {'core'}, dimensions={0}, use_global_device_ids=true | all-gather | bytes 614400 | tf_op jit(solution)/shard_map/all_gather | solution.py:340
  36.3 0.8 gradients.1
  37.1 2.4 %all-gather.1 = f32[1600,128]{1,0:T(8,128)S(1)} all-gather(f32[800,128]{1,0:T(8,128)S(1)} %get-tuple-element.21), channel_id=3, replica_groups=mesh['x'=4,'zl'=4,'yh'=4,'yl'=2,'zh'=2,'core'=2] {'core'}, dimensions={0}, use_global_device_ids=true | all-gather | bytes 1228800 | tf_op jit(solution)/shard_map/all_gather | solution.py:365
  39.5 0.9 %pair_sum.1 = f32[832,128]{1,0:T(8,128)} custom-call(s32[1]{0:T(128)S(6)} %copy.18.star_ref, f32[800,128]{1,0:T(8,128)S(1)} %get-tuple-element.20.keep_ref, f32[2,800,128]{2,1,0:T(8,128)S(1)} %bitcast.10), custom_call_target="tpu_custom_call" | custom-call | tf_op jit(solution)/shard_map/pair_sum/pallas_call | solution.py:366
  40.3 8.5 %all-to-all-start.1 = ((f32[32,1,3328]{2,1,0:T(1,128)}), f32[32,1,3328]{2,1,0:T(1,128)S(1)}, u32[]{:S(2)}, u32[]{:S(2)}) async-start(f32[32,1,3328]{2,1,0:T(1,128)} %bitcast.4), calls=%async_computation.1 | async-start | bytes 851968 | tf_op jit(solution)/shard_map/all_to_all | solution.py:385
  48.9 1.8 %series_gradient.1 = bf16[1,128,1536]{2,1,0:T(8,128)(2,1)} custom-call(bf16[1536,128]{1,0:T(8,128)(2,1)S(1)} %get-tuple-element.22.low_ref, bf16[1,128,1536]{2,1,0:T(8,128)(2,1)S(1)} %copy-done, bf16[1536,128]{1,0:T(8,128)(2,1)S(1)} %copy-done.1), custom_call_target="tpu_custom_call" | custom-call | flops 100000000 | bytes 1600000 | tf_op jit(solution)/shard_map/series_gradient/pallas_call | solution.py:375
  50.7 10.2 %all-to-all-done.1 = f32[32,1,3328]{2,1,0:T(1,128)S(1)} async-done(((f32[32,1,3328]{2,1,0:T(1,128)}), f32[32,1,3328]{2,1,0:T(1,128)S(1)}, u32[]{:S(2)}, u32[]{:S(2)}) %all-to-all-start.1) | async-done | bytes 426016 | tf_op jit(solution)/shard_map/all_to_all | solution.py:385
  60.8 0.1 sum_pieces.1
  60.9 15.4 %all_to_all.15 = f32[16,1,3584]{2,1,0:T(1,128)S(1)} all-to-all(f32[16,1,3584]{2,1,0:T(1,128)S(1)} %bitcast.14), channel_id=1, replica_groups=mesh['x'=4,'zl'=4,'yh'=4,'yl'=2,'zh'=2,'core'=2] {'zh','yl','yh'}, dimensions={0} | all-to-all | bytes 458752 | tf_op jit(solution)/shard_map/all_to_all | solution.py:395
  76.3 5.9 %all-gather.2 = f32[32,1,3584]{2,1,0:T(1,128)S(1)} all-gather(f32[16,1,3584]{2,1,0:T(1,128)S(1)} %all_to_all.15), channel_id=4, replica_groups=mesh['x'=4,'zl'=4,'yh'=4,'yl'=2,'zh'=2,'core'=2] {'core'}, dimensions={0}, use_global_device_ids=true | all-gather | bytes 688128 | tf_op jit(solution)/shard_map/all_gather | solution.py:396
  82.2 0.7 outputs.1
  (1 shorter events, 0.0 us)
Async XLA Ops:
  1.3 19.2 %copy-start.1 = (bf16[1536,128]{1,0:T(8,128)(2,1)S(1)}, bf16[1536,128]{1,0:T(8,128)(2,1)}, u32[]{:S(2)}) copy-start(bf16[1536,128]{1,0:T(8,128)(2,1)} %w_ref.3) | copy-start | bytes 1179652
  1.3 19.2 %copy-start.2 = (bf16[1,128,1536]{2,1,0:T(8,128)(2,1)S(1)}, bf16[1,128,1536]{2,1,0:T(8,128)(2,1)}, u32[]{:S(2)}) copy-start(bf16[1,128,1536]{2,1,0:T(8,128)(2,1)} %series_ref.1) | copy-start | bytes 1179652
  1.3 19.2 %copy-start.3 = (f32[16,1536]{1,0:T(8,128)S(1)}, f32[16,1536]{1,0:T(8,128)}, u32[]{:S(2)}) copy-start(f32[16,1536]{1,0:T(8,128)} %table_ref.1) | copy-start | bytes 294916
  4.0 16.5 %copy-start = (bf16[1,128,1536]{2,1,0:T(8,128)(2,1)S(1)}, bf16[1,128,1536]{2,1,0:T(8,128)(2,1)}, u32[]{:S(2)}) copy-start(bf16[1,128,1536]{2,1,0:T(8,128)(2,1)} %cot_ref.3) | copy-start | bytes 1179652
  4.0 16.4 %copy-start.4 = (f32[1536]{0:T(1024)S(1)}, f32[1536]{0:T(1024)}, u32[]{:S(2)}) copy-start(f32[1536]{0:T(1024)} %param.15) | copy-start | bytes 18436
  4.0 28.3 %all-to-all-start = ((f32[16,1,3200]{2,1,0:T(1,128)}), f32[16,1,3200]{2,1,0:T(1,128)S(1)}, u32[]{:S(2)}, u32[]{:S(2)}) async-start(f32[16,1,3200]{2,1,0:T(1,128)} %bitcast.18), calls=%async_computation | async-start | bytes 409600 | tf_op jit(solution)/shard_map/all_to_all | solution.py:340
  20.4 0.7 copy-start.5
  20.4 0.7 copy-start.6
  40.3 20.5 %all-to-all-start.1 = ((f32[32,1,3328]{2,1,0:T(1,128)}), f32[32,1,3328]{2,1,0:T(1,128)S(1)}, u32[]{:S(2)}, u32[]{:S(2)}) async-start(f32[32,1,3328]{2,1,0:T(1,128)} %bitcast.4), calls=%async_computation.1 | async-start | bytes 851968 | tf_op jit(solution)/shard_map/all_to_all | solution.py:385
